TPU v7x, 32 devices: a whole 2x2x4 slice. The times are simulated.
32 devices in a mesh: dp: 16 (over z, y, x), mp: 2 (over core).
Axes of the slice: x: 2, y: 2, z: 4, core: 2. Of those that a mesh axis runs over, the one named last changes fastest.
Arguments:
- sentence_layer_entry: bfloat16 [8192, 768], P('dp'), may hold values from -6 to 6
- sentence_word_ids: int32 [8192], P('dp'), may hold values from 0 to 31999, as said below
- picture_tile_activations: bfloat16 [512, 145, 768], P(('dp', 'mp')), may hold values from -6 to 6
- picture_detail_flag: int32 [512], P(('dp', 'mp')), may hold values 0 or 1
- matched_picture_ids: int32 [512], P('dp'), may hold values from 0 to 511, each once
- mixer_layernorm_gamma: float32 [768], replicated, may hold values from 0.5 to 1.5
- mixer_layernorm_offset: float32 [768], replicated, may hold values from -1.5 to 1.5
- mixer_triple_matrix: bfloat16 [3, 768, 768], P(None, None, 'mp'), may hold values from -0.21875 to 0.21875
- mixer_pair_offsets: float32 [2, 768], P(None, 'mp'), may hold values from -1.5 to 1.5
- mixer_result_matrix: bfloat16 [768, 768], P('mp'), may hold values from -0.4375 to 0.4375
- mixer_result_offset: float32 [768], replicated, may hold values from -1.5 to 1.5
- perceptron_layernorm_gamma: float32 [768], replicated, may hold values from 0.5 to 1.5
- perceptron_layernorm_offset: float32 [768], replicated, may hold values from -1.5 to 1.5
- widening_matrix: bfloat16 [768, 3072], P(None, 'mp'), may hold values from -0.21875 to 0.21875
- widening_offset: float32 [3072], P('mp'), may hold values from -1.5 to 1.5
- narrowing_matrix: bfloat16 [3072, 768], P('mp'), may hold values from -0.109375 to 0.109375
- narrowing_offset: float32 [768], replicated, may hold values from -1.5 to 1.5
- sharpening_log: float32 [1], replicated, may hold values from 3.7 to 4.2
- locked_layernorm_gammas: float32 [2, 768], replicated, may hold values from 0.5 to 1.5
- locked_mixer_triple_matrix: bfloat16 [3, 768, 768], replicated, may hold values from -0.21875 to 0.21875
- locked_mixer_result_matrix: bfloat16 [768, 768], replicated, may hold values from -0.875 to 0.875
- locked_widening_matrix: bfloat16 [768, 3072], replicated, may hold values from -0.21875 to 0.21875
- locked_narrowing_matrix: bfloat16 [3072, 768], replicated, may hold values from -0.109375 to 0.109375
Outputs:
- training_error: float32 [1], replicated
- grad_input: float32 [8192, 768], P('dp')
- grad_qkv: float32 [3, 768, 768], P(None, None, 'mp')
- grad_b_qv: float32 [2, 768], P(None, 'mp')
- grad_w_out: float32 [768, 768], P('mp')
- grad_b_out: float32 [768], replicated
- grad_w_up: float32 [768, 3072], P(None, 'mp')
- grad_b_up: float32 [3072], P('mp')
- grad_w_down: float32 [3072, 768], P('mp')
- grad_b_down: float32 [768], replicated
- grad_ln1_gain: float32 [768], replicated
- grad_ln1_bias: float32 [768], replicated
- grad_ln2_gain: float32 [768], replicated
- grad_ln2_bias: float32 [768], replicated
- grad_temperature: float32 [1], replicated
Inputs may be any that keep to these rules, and one draw needn't show every extreme that they name: `sentence_word_ids`: in each caption of 16 positions the nonzero ids form a prefix of 2 or more positions and 0 fills the rest; in every draw some caption has no 0 and some caption has exactly 2 nonzero ids.
All inputs are finite; a program needn't handle non-finite values. No bound on the sum of `picture_detail_flag` on one device may be relied on, other than what follows from the above.
Results may differ from a plain program's by a relative error of at most 0.0095.
The roundings to bfloat16 on the way count: a program that leaves them out, or rounds other values in their place, can miss the bound.
Values may be sent and summed in bfloat16 or wider, within the bound.
No kernel may reach another device: no remote copies, remote signals or barrier semaphores. Data moves between devices by JAX's collectives and lax.ppermute only.
A program may use at most 128 MiB of HBM per device.

v0:
```python
import functools

import jax
import jax.numpy as jnp
from jax import lax
from jax.experimental import pallas as pl
from jax.experimental.pallas import tpu as pltpu
from jax.sharding import PartitionSpec as P

HEAD = 64
IMG_TOK = 145
LOW_TOK = 50
CAP_LEN = 16


EPS_TEXT = 1e-05
EPS_UNIT = 1e-06
MASKED_SCORE = -1e30
BF16 = jnp.bfloat16
F32 = jnp.float32


def mp_other(values):
    return lax.ppermute(values, "mp", [(0, 1), (1, 0)])


def dp_swap(values, mask):
    size = lax.axis_size("dp")
    return lax.ppermute(values, "dp", [(index, index ^ mask) for index in range(size)])


def group_steps(size):
    steps, stride = [], 1
    while stride < size:
        steps.append([stride, 2 * stride, 3 * stride])
        stride *= 4
    return steps


def gather_masks(steps):
    masks = [0]
    for step in steps:
        masks = [mask ^ base for mask in [0] + step for base in masks]
    return masks


def dp_parts(values, step):
    return [values] + [dp_swap(values, mask) for mask in step]


def dp_gather(values, steps, waits):
    for step, wait in zip(steps, waits):
        parts = dp_parts(values, step)
        shape = (len(parts) * values.shape[0], values.shape[1])
        (values,) = call(stack_kernel, parts, ((shape, values.dtype),), after=(wait,))
    return values


def dp_sum(values):
    mask = 1
    while mask < lax.axis_size("dp"):
        values = values + dp_swap(values, mask)
        mask *= 2
    return values


HIGH_ROWS = 160
LOW_ROWS = 64
TILE = 256
PAIR = 2 * HEAD
NT = (((1,), (1,)), ((), ()))
VMEM_LIMIT = 56 * 1024 * 1024
BUSY = 10**12


def dot(left, right):
    return jnp.dot(left, right, preferred_element_type=F32)


def wide_dot(left, right):
    high = left.astype(BF16)
    rest = (left - high.astype(F32)).astype(BF16)
    return dot(high, right) + dot(rest, right)


def standard(values, epsilon):
    centered = values - jnp.mean(values, axis=-1, keepdims=True)
    variance = jnp.mean(centered * centered, axis=-1, keepdims=True)
    return centered * lax.rsqrt(variance + epsilon)


def gelu(values):
    return (0.5 * values) * (1.0 + lax.erf(values * (0.5**0.5)))


def image_kernel(
    flag_ref,
    token_ref,
    gain_ref,
    triple_hbm,
    result_hbm,
    widen_hbm,
    narrow_hbm,
    out_ref,
    packed,
    queries,
    keys,
    values,
    triple,
    result,
    widen,
    narrow,
    resid_sum,
    hidden_sum,
    starts,
    sems,
):
    images, _, width = token_ref.shape
    hidden = widen.shape[1]
    pairs = (
        (triple_hbm, triple),
        (result_hbm, result),
        (widen_hbm, widen),
        (narrow_hbm, narrow),
    )
    copies = [
        pltpu.make_async_copy(source, target, sems.at[place])
        for place, (source, target) in enumerate(pairs)
    ]
    for copy in copies:
        copy.start()
    resid_sum[...] = jnp.zeros_like(resid_sum)
    hidden_sum[...] = jnp.zeros_like(hidden_sum)

    tail = IMG_TOK // 16 * 16

    def pack(image, start):
        start = pl.multiple_of(start, 16)
        starts[image] = start
        high = flag_ref[image] == 1

        @pl.when(high)
        def _():
            packed[pl.ds(start, tail), :] = token_ref[image, 0:tail, :]
            last = token_ref[image, tail:IMG_TOK, :].astype(F32)
            row = lax.broadcasted_iota(jnp.int32, (HIGH_ROWS - tail, width), 0)
            packed[pl.ds(start + tail, HIGH_ROWS - tail), :] = jnp.where(
                row == 0, last, 0.0
            ).astype(BF16)

        @pl.when(jnp.logical_not(high))
        def _():
            packed[pl.ds(start, LOW_ROWS), :] = token_ref[image, 0:LOW_ROWS, :]

        return start + jnp.where(high, HIGH_ROWS, LOW_ROWS)

    total = lax.fori_loop(0, images, pack, jnp.int32(0))
    packed[pl.ds(pl.multiple_of(total, 16), TILE), :] = jnp.zeros((TILE, width), BF16)
    tiles = lax.div(total + (TILE - 1), jnp.int32(TILE))

    copies[0].wait()

    def project(tile, carry):
        rows = pl.ds(pl.multiple_of(tile * TILE, TILE), TILE)
        normed = (standard(packed[rows, :].astype(F32), EPS_UNIT) * gain_ref[0:1, :]).astype(BF16)
        queries[rows, :] = (dot(normed, triple[0]) * HEAD ** (-0.5)).astype(BF16)
        keys[rows, :] = dot(normed, triple[1]).astype(BF16)
        values[rows, :] = dot(normed, triple[2]).astype(BF16)
        return carry

    lax.fori_loop(0, tiles, project, 0)

    def attend(start, count, live):
        rows = pl.ds(start, count)
        left = lax.broadcasted_iota(jnp.int32, (count, PAIR), 1) < HEAD
        key_live = lax.broadcasted_iota(jnp.int32, (2 * count, count), 1) < live
        for pair in range(width // PAIR):
            lanes = slice(pair * PAIR, (pair + 1) * PAIR)
            q, k, v = queries[rows, lanes], keys[rows, lanes], values[rows, lanes]
            zero, one = jnp.zeros_like(q), jnp.ones_like(v)
            both = jnp.concatenate([jnp.where(left, q, zero), jnp.where(left, zero, q)], axis=0)
            scores = lax.dot_general(both, k, NT, preferred_element_type=F32)
            scores = jnp.where(key_live, scores, MASKED_SCORE)
            powers = jnp.exp(scores - jnp.max(scores, axis=-1, keepdims=True)).astype(BF16)
            first = dot(powers[:count], jnp.where(left, v, one))
            second = dot(powers[count:], jnp.where(left, one, v))
            sums = pltpu.roll(jnp.where(left, second, first), HEAD, 1)
            queries[rows, lanes] = (jnp.where(left, first, second) / sums).astype(BF16)

    def mix(image, carry):
        start = pl.multiple_of(starts[image], 16)
        high = flag_ref[image] == 1

        @pl.when(high)
        def _():
            attend(start, HIGH_ROWS, IMG_TOK)

        @pl.when(jnp.logical_not(high))
        def _():
            attend(start, LOW_ROWS, LOW_TOK)

        return carry

    lax.fori_loop(0, images, mix, 0)

    slot = lax.broadcasted_iota(jnp.int32, (images, 1), 0)
    begin = jnp.zeros((images, 1), jnp.int32)
    live = jnp.zeros((images, 1), jnp.int32)
    for image in range(images):
        begin = jnp.where(slot == image, starts[image], begin)
        live = jnp.where(
            slot == image, jnp.where(flag_ref[image] == 1, IMG_TOK, LOW_TOK), live
        )
    copies[1].wait()
    copies[2].wait()

    def perceptron(tile, carry):
        base = pl.multiple_of(tile * TILE, TILE)
        rows = pl.ds(base, TILE)
        place = base + lax.broadcasted_iota(jnp.int32, (images, TILE), 1)
        pool = jnp.where((place >= begin) & (place < begin + live), 1.0, 0.0).astype(BF16)
        residual = packed[rows, :].astype(F32) + dot(queries[rows, :], result[...])
        upper = residual.astype(BF16)
        lower = (residual - upper.astype(F32)).astype(BF16)
        resid_sum[...] += dot(pool, upper) + dot(pool, lower)
        normed = (standard(residual, EPS_UNIT) * gain_ref[1:2, :]).astype(BF16)
        for chunk in range(hidden // width):
            lanes = slice(chunk * width, (chunk + 1) * width)
            units = gelu(dot(normed, widen[:, lanes])).astype(BF16)
            hidden_sum[:, lanes] += dot(pool, units)
        return carry

    lax.fori_loop(0, tiles, perceptron, 0)
    copies[3].wait()
    pooled = (resid_sum[...] + wide_dot(hidden_sum[...], narrow[...])) / live.astype(F32)
    out_ref[...] = (
        pooled * lax.rsqrt(jnp.sum(pooled * pooled, axis=-1, keepdims=True) + EPS_UNIT)
    ).astype(BF16)


def image_tower(flags, tokens, gains, triple, result, widen, narrow):
    images, _, width = tokens.shape
    rows = images * HIGH_ROWS + TILE
    outside = pl.BlockSpec(memory_space=pl.ANY)
    inside = pl.BlockSpec(memory_space=pltpu.VMEM)
    return pl.pallas_call(
        image_kernel,
        out_shape=jax.ShapeDtypeStruct((images, width), BF16),
        in_specs=[pl.BlockSpec(memory_space=pltpu.SMEM), inside, inside]
        + [outside] * 4,
        out_specs=inside,
        scratch_shapes=[pltpu.VMEM((rows, width), BF16)] * 4
        + [pltpu.VMEM(weight.shape, BF16) for weight in (triple, result, widen, narrow)]
        + [
            pltpu.VMEM((images, width), F32),
            pltpu.VMEM((images, widen.shape[1]), F32),
            pltpu.SMEM((images,), jnp.int32),
            pltpu.SemaphoreType.DMA((4,)),
        ],
        compiler_params=pltpu.CompilerParams(vmem_limit_bytes=VMEM_LIMIT),
        cost_estimate=pl.CostEstimate(
            flops=30_000_000_000, bytes_accessed=20_000_000, transcendentals=10_000_000
        ),
    )(flags, tokens, gains, triple, result, widen, narrow)


TN = (((0,), (0,)), ((), ()))
BLOCK = 128
ROOT_HALF = 0.5**0.5
DENSITY = 0.3989422804014327


def dot_t(left, right):
    return lax.dot_general(left, right, NT, preferred_element_type=F32)


def t_dot(left, right):
    return lax.dot_general(left, right, TN, preferred_element_type=F32)


def fetch(sources, targets, sems):
    copies = [
        pltpu.make_async_copy(source, target, sems.at[place])
        for place, (source, target) in enumerate(zip(sources, targets))
    ]
    for copy in copies:
        copy.start()
    return copies


def stack_kernel(*refs):
    rows = refs[0].shape[0]
    for place, ref in enumerate(refs[:-1]):
        refs[-1][place * rows : (place + 1) * rows, :] = ref[...]


def caption_pool(ids_ref, captions):
    ids_row = ids_ref[...].reshape(1, -1)
    tokens = ids_row.shape[1]
    shape = (captions, tokens)
    caption = lax.broadcasted_iota(jnp.int32, shape, 0)
    token = lax.broadcasted_iota(jnp.int32, shape, 1)
    inside = (token // (tokens // captions)) == caption
    return jnp.where(inside & (ids_row != 0), 1.0, 0.0)


def valid_column(pool):
    pool = pool.astype(BF16)
    return t_dot(pool, jnp.ones((pool.shape[0], 128), BF16))[:, 0:1]


def number_column(ref):
    shape = (ref.shape[0], 1)
    place = lax.broadcasted_iota(jnp.int32, shape, 0)
    column = jnp.zeros(shape, jnp.int32)
    for index in range(shape[0]):
        column = jnp.where(place == index, ref[index], column)
    return column


def as_row(ref):
    return ref[...].reshape(1, -1)


def pair_masks(rows, pair_width):
    return lax.broadcasted_iota(jnp.int32, (rows, pair_width), 1) < HEAD


def two_heads(values, left):
    zero = jnp.zeros_like(values)
    return jnp.concatenate(
        [jnp.where(left, values, zero), jnp.where(left, zero, values)], axis=0
    )


def text_mix_kernel(
    entry_ref,
    ids_ref,
    gain_ref,
    shift_ref,
    triple_ref,
    pair_ref,
    result_ref,
    normed_ref,
    qkv_ref,
    soft_ref,
    mixed_ref,
    part_ref,
):
    tokens = entry_ref.shape[0]
    width = result_ref.shape[0]
    normed = (
        standard(entry_ref[...].astype(F32), EPS_TEXT) * as_row(gain_ref) + as_row(shift_ref)
    ).astype(BF16)
    normed_ref[...] = normed
    qkv_ref[0] = (dot(normed, triple_ref[0]) + pair_ref[0:1, :]).astype(BF16)
    qkv_ref[1] = dot(normed, triple_ref[1]).astype(BF16)
    qkv_ref[2] = (dot(normed, triple_ref[2]) + pair_ref[1:2, :]).astype(BF16)
    ids = as_row(ids_ref)
    left = pair_masks(BLOCK, PAIR)
    shape = (2 * BLOCK, BLOCK)
    query_caption = lax.broadcasted_iota(jnp.int32, shape, 0) % BLOCK // CAP_LEN
    same = query_caption == lax.broadcasted_iota(jnp.int32, shape, 1) // CAP_LEN
    for block in range(tokens // BLOCK):
        rows = slice(block * BLOCK, (block + 1) * BLOCK)
        seen = same & (ids[:, rows] != 0)
        for pair in range(width // PAIR):
            lanes = slice(pair * PAIR, (pair + 1) * PAIR)
            scores = dot_t(two_heads(qkv_ref[0, rows, lanes], left), qkv_ref[1, rows, lanes])
            scores = jnp.where(seen, scores * HEAD ** (-0.5), MASKED_SCORE)
            powers = jnp.exp(scores - jnp.max(scores, axis=-1, keepdims=True))
            soft = powers / jnp.sum(powers, axis=-1, keepdims=True)
            soft_ref[block, pair] = soft
            low = soft.astype(BF16)
            value = qkv_ref[2, rows, lanes]
            mixed_ref[rows, lanes] = jnp.where(
                left, dot(low[:BLOCK], value), dot(low[BLOCK:], value)
            ).astype(BF16)
    part_ref[...] = dot(mixed_ref[...], result_ref[...])


def text_widen_kernel(
    entry_ref,
    own_ref,
    other_ref,
    result_offset_ref,
    gain_ref,
    shift_ref,
    widen_offset_ref,
    ids_ref,
    widen_hbm,
    narrow_hbm,
    residual_ref,
    normed_ref,
    slope_ref,
    sums_ref,
    resid_sum_ref,
    branch_ref,
    widen,
    narrow,
    hidden_sum,
    sems,
):
    captions = sums_ref.shape[0]
    width = entry_ref.shape[1]
    copies = fetch((widen_hbm, narrow_hbm), (widen, narrow), sems)
    residual = entry_ref[...].astype(F32) + (
        (own_ref[...] + other_ref[...]) + as_row(result_offset_ref)
    )
    residual_ref[...] = residual
    normed = (standard(residual, EPS_TEXT) * as_row(gain_ref) + as_row(shift_ref)).astype(BF16)
    normed_ref[...] = normed
    pool = caption_pool(ids_ref, captions).astype(BF16)
    widen_offset = as_row(widen_offset_ref)
    upper = residual.astype(BF16)
    resid_sum_ref[...] = dot(pool, upper) + dot(
        pool, (residual - upper.astype(F32)).astype(BF16)
    )
    valid = valid_column(pool)
    copies[0].wait()
    for chunk in range(widen.shape[1] // width):
        lanes = slice(chunk * width, (chunk + 1) * width)
        before = dot(normed, widen[:, lanes]) + widen_offset[:, lanes]
        share = 0.5 * (1.0 + lax.erf(before * ROOT_HALF))
        hidden_sum[:, lanes] = dot(pool, (before * share).astype(BF16))
        slope = share + before * (jnp.exp(-0.5 * before * before) * DENSITY)
        slope_ref[:, lanes] = slope * valid
    sums_ref[...] = hidden_sum[...].astype(BF16)
    copies[1].wait()
    branch_ref[...] = wide_dot(hidden_sum[...], narrow[...])


def logits_kernel(
    masks,
    index_ref,
    matched_ref,
    sharpen_ref,
    near_ref,
    far_ref,
    resid_sum_ref,
    own_ref,
    other_ref,
    narrow_offset_ref,
    ids_ref,
    images_ref,
    unit_ref,
    factor_ref,
    logits_ref,
    powers_ref,
    row_sum_ref,
    col_sum_ref,
    loss_ref,
):
    captions, pairs = logits_ref.shape
    rows = images_ref.shape[0] // (2 * len(masks))
    core = index_ref[1]
    for place, mask in enumerate(masks):
        start = (index_ref[0] ^ mask) * (2 * rows)
        images_ref[pl.ds(pl.multiple_of(start + core * rows, rows), rows), :] = near_ref[
            place * rows : (place + 1) * rows, :
        ]
        images_ref[pl.ds(pl.multiple_of(start + (1 - core) * rows, rows), rows), :] = far_ref[
            place * rows : (place + 1) * rows, :
        ]
    count = jnp.sum(caption_pool(ids_ref, captions), axis=1, keepdims=True)
    pooled = (resid_sum_ref[...] + (own_ref[...] + other_ref[...])) / count + as_row(
        narrow_offset_ref
    )
    inverse = lax.rsqrt(jnp.sum(pooled * pooled, axis=-1, keepdims=True) + EPS_UNIT)
    unit = pooled * inverse
    unit_ref[...] = unit
    factor_ref[...] = jnp.broadcast_to(inverse / count, factor_ref.shape)
    logits = jnp.exp(jnp.full((1, 1), sharpen_ref[0], F32)) * dot_t(unit.astype(BF16), images_ref[...])
    logits_ref[...] = logits
    powers = jnp.exp(logits)
    powers_ref[...] = powers
    row_sum = jnp.sum(powers, axis=1, keepdims=True)
    row_sum_ref[...] = jnp.broadcast_to(row_sum, row_sum_ref.shape)
    col_sum_ref[...] = jnp.broadcast_to(
        jnp.sum(powers, axis=0, keepdims=True)[None], col_sum_ref.shape
    )
    positive = number_column(matched_ref) == lax.broadcasted_iota(jnp.int32, (captions, pairs), 1)
    wanted = jnp.sum(jnp.where(positive, logits, 0.0), axis=1, keepdims=True)
    loss_ref[...] = jnp.broadcast_to(
        jnp.sum(jnp.log(row_sum) - 2.0 * wanted, axis=0, keepdims=True), loss_ref.shape
    )


def loss_grad_kernel(
    matched_ref,
    sharpen_ref,
    col_parts_ref,
    logits_ref,
    powers_ref,
    row_sum_ref,
    unit_ref,
    factor_ref,
    images_ref,
    ids_ref,
    loss_ref,
    narrow_hbm,
    slope_hbm,
    widen_hbm,
    grad_ref,
    low_ref,
    before_ref,
    part_ref,
    stat_ref,
    narrow,
    slope,
    widen,
    sems,
):
    captions, pairs = logits_ref.shape
    tokens, hidden = slope.shape
    width = grad_ref.shape[1]
    copies = fetch((narrow_hbm, slope_hbm, widen_hbm), (narrow, slope, widen), sems)
    logits, powers = logits_ref[...], powers_ref[...]
    col_sum = jnp.sum(col_parts_ref[...], axis=0)
    positive = number_column(matched_ref) == lax.broadcasted_iota(jnp.int32, (captions, pairs), 1)
    derivative = (
        powers / row_sum_ref[:, 0:1] + powers / col_sum - jnp.where(positive, 2.0, 0.0)
    ) / (2.0 * pairs)
    temperature = jnp.sum(
        jnp.sum(derivative * logits, axis=1, keepdims=True), axis=0, keepdims=True
    )
    col_loss = jnp.sum(jnp.log(col_sum), axis=1, keepdims=True)
    text = dot((derivative * jnp.exp(jnp.full((1, 1), sharpen_ref[0], F32))).astype(BF16), images_ref[...])
    unit = unit_ref[...]
    grad = (text - unit * jnp.sum(unit * text, axis=-1, keepdims=True)) * factor_ref[:, 0:1]
    grad_ref[...] = grad
    low = grad.astype(BF16)
    low_ref[...] = low
    copies[0].wait()
    copies[1].wait()
    copies[2].wait()
    ones = jnp.ones((8, tokens), BF16)
    part = jnp.zeros(part_ref.shape, F32)
    for chunk in range(hidden // width):
        lanes = slice(chunk * width, (chunk + 1) * width)
        back = dot_t(low, narrow[lanes, :])
        before = (
            (back[:, None, :] * slope[:, lanes].reshape(captions, CAP_LEN, width))
            .reshape(tokens, width)
            .astype(BF16)
        )
        before_ref[:, lanes] = before
        stat_ref[chunk : chunk + 1, :] = dot(ones, before)[0:1]
        part = part + dot_t(before, widen[:, lanes])
    part_ref[...] = part
    count = jnp.sum(caption_pool(ids_ref, captions), axis=1, keepdims=True)
    stat_ref[2:3, :] = jnp.sum(low.astype(F32) * count, axis=0, keepdims=True)
    lane = lax.broadcasted_iota(jnp.int32, (1, width), 1)
    stat_ref[3:4, :] = jnp.where(
        lane == 0,
        temperature,
        jnp.where(lane == 1, loss_ref[0:1, 0:1], jnp.where(lane == 2, col_loss, 0.0)),
    )
    stat_ref[4:8, :] = jnp.zeros((4, width), F32)


def deal(index_ref, first, second, outs):
    half = first.shape[0] // 2
    for place, (values, bit) in enumerate(((first, 1), (second, 2))):
        mine = index_ref[0] // bit % 2
        for ref, which in ((outs[2 * place], 1 - mine), (outs[2 * place + 1], mine)):
            ref[...] = values[pl.ds(pl.multiple_of(which * half, half), half), :]


def widen_grad_kernel(index_ref, normed_ref, before_ref, *refs):
    outs, (first, second) = refs[:4], refs[4:]
    width = first.shape[1]
    normed = normed_ref[...]
    first[...] = t_dot(normed, before_ref[:, :width]).astype(BF16)
    second[...] = t_dot(normed, before_ref[:, width:]).astype(BF16)
    deal(index_ref, first, second, outs)


def mixer_back_kernel(
    own_ref,
    other_ref,
    residual_ref,
    grad_ref,
    ids_ref,
    gain_ref,
    result_ref,
    qkv_hbm,
    soft_hbm,
    triple_hbm,
    grad_residual_ref,
    low_ref,
    flat_ref,
    part_ref,
    stat_ref,
    qkv,
    soft_all,
    triple,
    sems,
):
    tokens, width = residual_ref.shape
    captions = grad_ref.shape[0]
    local_width = result_ref.shape[0]
    copies = fetch((qkv_hbm, soft_hbm, triple_hbm), (qkv, soft_all, triple), sems)
    residual = residual_ref[...]
    centered = residual - jnp.mean(residual, axis=-1, keepdims=True)
    rate = lax.rsqrt(jnp.mean(centered * centered, axis=-1, keepdims=True) + EPS_TEXT)
    unit = centered * rate
    grad = own_ref[...] + other_ref[...]
    stat_ref[1:2, :] = jnp.sum(grad * unit, axis=0, keepdims=True)
    stat_ref[2:3, :] = jnp.sum(grad, axis=0, keepdims=True)
    scaled = grad * as_row(gain_ref)
    inner = rate * (
        scaled
        - jnp.mean(scaled, axis=-1, keepdims=True)
        - unit * jnp.mean(scaled * unit, axis=-1, keepdims=True)
    )
    spread = jnp.broadcast_to(
        grad_ref[...][:, None, :], (captions, tokens // captions, width)
    ).reshape(tokens, width)
    grad_residual = spread * valid_column(caption_pool(ids_ref, captions)) + inner
    grad_residual_ref[...] = grad_residual
    low = grad_residual.astype(BF16)
    low_ref[...] = low
    ones = jnp.ones((8, tokens), BF16)
    stat_ref[0:1, :] = dot(ones, low)[0:1]
    grad_mixed = dot_t(low, result_ref[...]).astype(BF16)
    for copy in copies:
        copy.wait()
    left = pair_masks(BLOCK, PAIR)
    for block in range(tokens // BLOCK):
        rows = slice(block * BLOCK, (block + 1) * BLOCK)
        for pair in range(local_width // PAIR):
            lanes = slice(pair * PAIR, (pair + 1) * PAIR)
            soft = soft_all[block, pair]
            mixed = two_heads(grad_mixed[rows, lanes], left)
            query, key = qkv[0, rows, lanes], qkv[1, rows, lanes]
            grad_soft = dot_t(mixed, qkv[2, rows, lanes])
            flat_ref[2, rows, lanes] = t_dot(soft.astype(BF16), mixed).astype(BF16)
            scores = (
                soft * (grad_soft - jnp.sum(grad_soft * soft, axis=-1, keepdims=True))
            ).astype(BF16)
            back = jnp.where(left, dot(scores[:BLOCK], key), dot(scores[BLOCK:], key))
            flat_ref[0, rows, lanes] = (back * HEAD ** (-0.5)).astype(BF16)
            flat_ref[1, rows, lanes] = (
                t_dot(scores, two_heads(query, left)) * HEAD ** (-0.5)
            ).astype(BF16)
    part_ref[...] = (
        dot_t(flat_ref[0], triple[0])
        + dot_t(flat_ref[1], triple[1])
        + dot_t(flat_ref[2], triple[2])
    )
    stat_ref[3:4, :local_width] = dot(ones, flat_ref[0])[0:1]
    stat_ref[3:4, local_width:] = dot(ones, flat_ref[2])[0:1]
    stat_ref[4:8, :] = jnp.zeros((4, width), F32)


def mixer_grad_kernel(index_ref, normed_ref, flat_ref, mixed_ref, low_ref, *refs):
    outs, (first, second) = refs[:4], refs[4:]
    half = flat_ref.shape[2]
    rows = first.shape[0] // 2
    normed = normed_ref[...]
    for part, (target, place) in enumerate(((first, 0), (first, rows), (second, 0))):
        grad = t_dot(normed, flat_ref[part]).astype(BF16)
        target[place : place + rows, :half] = grad[:rows]
        target[place : place + rows, half:] = grad[rows:]
    second[rows:, :] = t_dot(mixed_ref[...], low_ref[...]).astype(BF16)
    deal(index_ref, first, second, outs)


def narrow_grad_kernel(half, index_ref, sums_ref, near_ref, far_ref, out_ref, grads):
    width = grads.shape[1]
    core = index_ref[0]
    for place in range(near_ref.shape[0] // half):
        for ref, which in ((near_ref, core), (far_ref, 1 - core)):
            start = pl.multiple_of((2 * place + which) * half, half)
            grads[pl.ds(start, half), :] = ref[place * half : (place + 1) * half, :]
    for chunk in range(sums_ref.shape[1] // width):
        lanes = slice(chunk * width, (chunk + 1) * width)
        out_ref[lanes, :] = t_dot(sums_ref[:, lanes], grads[...])


def entry_grad_kernel(
    own_ref,
    other_ref,
    entry_ref,
    gain_ref,
    grad_residual_ref,
    loss_stat_ref,
    mixer_stat_ref,
    out_ref,
    pack_ref,
):
    entry = entry_ref[...].astype(F32)
    centered = entry - jnp.mean(entry, axis=-1, keepdims=True)
    rate = lax.rsqrt(jnp.mean(centered * centered, axis=-1, keepdims=True) + EPS_TEXT)
    unit = centered * rate
    grad = own_ref[...] + other_ref[...]
    pack_ref[0:8, :] = loss_stat_ref[...]
    pack_ref[8:16, :] = mixer_stat_ref[...]
    pack_ref[4:5, :] = jnp.sum(grad * unit, axis=0, keepdims=True)
    pack_ref[5:6, :] = jnp.sum(grad, axis=0, keepdims=True)
    scaled = grad * as_row(gain_ref)
    out_ref[...] = grad_residual_ref[...] + rate * (
        scaled
        - jnp.mean(scaled, axis=-1, keepdims=True)
        - unit * jnp.mean(scaled * unit, axis=-1, keepdims=True)
    )


def call(kernel, inside, shapes, outside=(), scratch=(), index=(), small=(), after=()):
    vmem = pl.BlockSpec(memory_space=pltpu.VMEM)
    extra = [pltpu.VMEM(array.shape, array.dtype) for array in outside]
    extra += list(scratch)
    if outside:
        extra += [pltpu.SemaphoreType.DMA((len(outside),))]
    index = [jnp.stack(index).astype(jnp.int32)] if index else []
    small = index + list(small)
    before = len(small) + len(inside) + len(outside)

    def body(*refs):
        kernel(*refs[:before], *refs[before + len(after) :])

    return pl.pallas_call(
        body,
        out_shape=[jax.ShapeDtypeStruct(shape, kind) for shape, kind in shapes],
        in_specs=[pl.BlockSpec(memory_space=pltpu.SMEM)] * len(small)
        + [vmem] * len(inside)
        + [pl.BlockSpec(memory_space=pl.ANY)] * (len(outside) + len(after)),
        out_specs=[vmem] * len(shapes),
        scratch_shapes=extra,
        compiler_params=pltpu.CompilerParams(vmem_limit_bytes=VMEM_LIMIT),
        cost_estimate=pl.CostEstimate(flops=BUSY, bytes_accessed=BUSY, transcendentals=0),
    )(*small, *inside, *outside, *after)


GROUP = 16
Z_STRIDE, Z_SIZE = 4, 4


def fold_kernel(index_ref, *refs):
    ins, outs = refs[:4], refs[4:]
    half = ins[0].shape[0] // 2
    for place, bit in ((0, 2), (1, 1)):
        total = ins[2 * place][...].astype(F32) + ins[2 * place + 1][...].astype(F32)
        upper = index_ref[0] // bit % 2 == 1
        low, high = total[:half], total[half:]
        outs[2 * place][...] = jnp.where(upper, low, high).astype(BF16)
        outs[2 * place + 1][...] = jnp.where(upper, high, low)


def cut_kernel(index_ref, *refs):
    ins, outs, total = refs[:4], refs[4:-1], refs[-1]
    rows = total.shape[0] // (2 * Z_SIZE)
    for place in range(2):
        total[pl.ds(place * rows * Z_SIZE, rows * Z_SIZE), :] = ins[2 * place][...] + ins[
            2 * place + 1
        ][...].astype(F32)
        for step in range(Z_SIZE):
            block = (index_ref[0] // Z_STRIDE % Z_SIZE) ^ step
            start = pl.multiple_of((place * Z_SIZE + block) * rows, rows)
            outs[step][place * rows : (place + 1) * rows, :] = total[
                pl.ds(start, rows), :
            ].astype(outs[step].dtype)


def add_kernel(own_ref, *refs):
    out_ref = refs[-1]
    rows = own_ref.shape[0]
    total = own_ref[...]
    for ref in refs[: Z_SIZE - 1]:
        total = total + ref[...].astype(F32)
    out_ref[:rows, :] = total.astype(out_ref.dtype)
    if out_ref.shape[0] > rows:
        out_ref[rows:, :] = refs[Z_SIZE - 1][...]


def join_kernel(extra, *refs):
    ins, out = refs[:Z_SIZE], refs[Z_SIZE]
    rows = (ins[0].shape[0] - extra) // 2
    start = 0
    for first, count in ((0, rows), (2 * rows, extra), (rows, rows)):
        for ref in ins:
            if count:
                out[start : start + count, :] = ref[first : first + count, :]
            start += count


def scatter_steps(dealt, place, extra=None):
    first_sent, first_kept, second_sent, second_kept = dealt
    rows, width = first_sent.shape
    after = yield
    arrived = (dp_swap(first_sent, 1), dp_swap(second_sent, 2))
    half = (rows // 2, width)
    first_sent, first_kept, second_sent, second_kept = call(
        fold_kernel,
        (first_kept, arrived[0], second_kept, arrived[1]),
        ((half, BF16), (half, F32), (half, BF16), (half, F32)),
        index=(place,),
        after=after,
    )
    after = yield first_kept
    arrived = (dp_swap(first_sent, 2), dp_swap(second_sent, 1))
    block = (rows // Z_SIZE, width)
    own, *sent = call(
        cut_kernel,
        (first_kept, arrived[0], second_kept, arrived[1]),
        ((block, F32),) + ((block, BF16),) * (Z_SIZE - 1),
        scratch=(pltpu.VMEM((rows, width), F32),),
        index=(place,),
        after=after,
    )
    after = yield own
    arrived = [dp_swap(values, step * Z_STRIDE) for step, values in enumerate(sent, 1)]
    size = lax.axis_size("dp")
    more = 0 if extra is None else extra.shape[0]
    if size > GROUP:
        (mine,) = call(add_kernel, (own, *arrived), ((own.shape, F32),), after=after)
        groups = [list(range(index, size, GROUP)) for index in range(GROUP)]
        mine = lax.psum(mine, "dp", axis_index_groups=groups).astype(BF16)
        if more:
            mine = jnp.concatenate([mine, extra], axis=0)
    else:
        (mine,) = call(
            add_kernel,
            (own, *arrived) + ((extra,) if more else ()),
            (((block[0] + more, width), BF16),),
            after=after,
        )
    after = yield mine
    pieces = [mine] + [dp_swap(mine, step * Z_STRIDE) for step in range(1, Z_SIZE)]
    (joined,) = call(
        functools.partial(join_kernel, more),
        pieces,
        (((Z_SIZE * (block[0] + more), width), BF16),),
        after=after,
    )
    cut = Z_SIZE * (block[0] // 2 + more)
    along_x, along_y = dp_swap(joined, 1), dp_swap(joined, 2)
    after = yield joined
    yield joined, along_x, along_y, dp_swap(along_y[:cut], 1), dp_swap(along_x[cut:], 2)


def block_home(index, block, outer, inner):
    high = (block // 8) ^ (index // outer % 2)
    middle = (block // 4 % 2) ^ (index // inner % 2)
    return high * 8 + middle * 4 + ((block % 4) ^ (index // Z_STRIDE % Z_SIZE))


def relative_blocks(refs, tensor):
    joined, along_x, along_y, first_far, second_far = refs
    size = second_far.shape[0]
    start = joined.shape[0] - size if tensor else 0
    if tensor:
        pieces = ((joined, start), (along_x, start), (along_y, start), (second_far, 0))
    else:
        pieces = ((joined, 0), (along_y, 0), (along_x, 0), (first_far, 0))
    rows = size // Z_SIZE
    for piece, (ref, start) in enumerate(pieces):
        for step in range(Z_SIZE):
            first = start + step * rows
            yield piece * Z_SIZE + step, rows, ref[first : first + rows, :]


def unpack_widen_kernel(index_ref, *refs):
    refs, (out_ref, extra_ref) = refs[:-2], refs[-2:]
    width = out_ref.shape[1] // 2
    for tensor, bits in ((0, (1, 2)), (1, (2, 1))):
        for block, rows, values in relative_blocks(refs, tensor):
            start = pl.multiple_of(block_home(index_ref[0], block, *bits) * rows, rows)
            out_ref[pl.ds(start, rows), tensor * width : (tensor + 1) * width] = values.astype(F32)
    first, count = refs[4].shape[0], extra_ref.shape[0] // 4
    for place, ref in enumerate(refs[:4]):
        extra_ref[place * count : (place + 1) * count, :] = ref[first : first + count, :]


def unpack_mixer_kernel(index_ref, *refs):
    refs, (triple_ref, result_ref) = refs[:-2], refs[-2:]
    half, split = triple_ref.shape[2], triple_ref.shape[1] // 2
    for block, rows, values in relative_blocks(refs, 0):
        home = block_home(index_ref[0], block, 1, 2)
        part, row = home // 8, pl.multiple_of(home % 8 * rows, rows)
        triple_ref[part, pl.ds(row, rows), :] = values[:, :half].astype(F32)
        triple_ref[part, pl.ds(split + row, rows), :] = values[:, half:].astype(F32)
    for block, rows, values in relative_blocks(refs, 1):
        home = block_home(index_ref[0], block, 2, 1)
        row = pl.multiple_of(home % 8 * rows, rows)

        @pl.when(home < 8)
        def _():
            triple_ref[2, pl.ds(row, rows), :] = values[:, :half].astype(F32)
            triple_ref[2, pl.ds(split + row, rows), :] = values[:, half:].astype(F32)

        @pl.when(home >= 8)
        def _():
            result_ref[pl.ds(row, rows), :] = values.astype(F32)


def local(
    sentence_layer_entry,
    sentence_word_ids,
    picture_tile_activations,
    picture_detail_flag,
    matched_picture_ids,
    mixer_layernorm_gamma,
    mixer_layernorm_offset,
    mixer_triple_matrix,
    mixer_pair_offsets,
    mixer_result_matrix,
    mixer_result_offset,
    perceptron_layernorm_gamma,
    perceptron_layernorm_offset,
    widening_matrix,
    widening_offset,
    narrowing_matrix,
    narrowing_offset,
    sharpening_log,
    locked_layernorm_gammas,
    locked_mixer_triple_matrix,
    locked_mixer_result_matrix,
    locked_widening_matrix,
    locked_narrowing_matrix,
):
    captions = matched_picture_ids.shape[0]
    tokens, model_width = sentence_layer_entry.shape
    local_width = mixer_result_matrix.shape[0]
    hidden = narrowing_matrix.shape[0]
    devices = lax.axis_size("dp")
    all_pairs = captions * devices
    place, core = lax.axis_index("dp"), lax.axis_index("mp")
    blocks = tokens // BLOCK
    full = (tokens, model_width)
    short = (captions, model_width)
    square = (model_width, model_width)
    half_square = (model_width // 2, model_width)
    dealt = ((half_square, BF16),) * 4

    steps = group_steps(devices)

    image_emb = image_tower(
        picture_detail_flag,
        picture_tile_activations,
        locked_layernorm_gammas,
        locked_mixer_triple_matrix,
        locked_mixer_result_matrix,
        locked_widening_matrix,
        locked_narrowing_matrix,
    )
    normed, qkv, soft, mixed, part = call(
        text_mix_kernel,
        (
            sentence_layer_entry,
            sentence_word_ids,
            mixer_layernorm_gamma,
            mixer_layernorm_offset,
            mixer_triple_matrix,
            mixer_pair_offsets,
            mixer_result_matrix,
        ),
        (
            (full, BF16),
            ((3, tokens, local_width), BF16),
            ((blocks, local_width // PAIR, 2 * BLOCK, BLOCK), F32),
            ((tokens, local_width), BF16),
            (full, F32),
        ),
        after=(image_emb,),
    )
    other = mp_other(part)
    near_images = dp_gather(image_emb, steps[:0:-1], [part] * (len(steps) - 1))
    residual, normed2, slope, hidden_sums, resid_sum, branch = call(
        text_widen_kernel,
        (
            sentence_layer_entry,
            part,
            other,
            mixer_result_offset,
            perceptron_layernorm_gamma,
            perceptron_layernorm_offset,
            widening_offset,
            sentence_word_ids,
        ),
        (
            (full, F32),
            (full, BF16),
            ((tokens, hidden), F32),
            ((captions, hidden), BF16),
            (short, F32),
            (short, F32),
        ),
        outside=(widening_matrix, narrowing_matrix),
        scratch=(pltpu.VMEM((captions, hidden), F32),),
        after=(near_images,),
    )

    near_images = dp_gather(near_images, steps[:1], (branch,))
    sums_parts = dp_parts(hidden_sums, steps[-1])
    images, unit, factor, logits, powers, row_sum, col_sum, row_loss = call(
        functools.partial(logits_kernel, gather_masks(steps[::-1])),
        (
            near_images,
            mp_other(near_images),
            resid_sum,
            branch,
            mp_other(branch),
            narrowing_offset,
            sentence_word_ids,
        ),
        (
            ((all_pairs, model_width), BF16),
            (short, F32),
            ((captions, 128), F32),
            ((captions, all_pairs), F32),
            ((captions, all_pairs), F32),
            ((captions, 128), F32),
            ((devices, 1, all_pairs), F32),
            ((8, 128), F32),
        ),
        index=(place, core),
        small=(matched_picture_ids, sharpening_log),
    )
    col_parts = lax.all_to_all(col_sum, "dp", 0, 0, tiled=True)
    for step in steps[-2::-1]:
        shape = (len(sums_parts) * sums_parts[0].shape[0], hidden)
        (joined_sums,) = call(stack_kernel, sums_parts, ((shape, BF16),), after=(unit,))
        sums_parts = dp_parts(joined_sums, step)
    grad_caption, grad_caption_low, grad_pre, part, loss_stat = call(
        loss_grad_kernel,
        (
            col_parts,
            logits,
            powers,
            row_sum,
            unit,
            factor,
            images,
            sentence_word_ids,
            row_loss,
        ),
        (
            (short, F32),
            (short, BF16),
            ((tokens, hidden), BF16),
            (full, F32),
            ((8, model_width), F32),
        ),
        outside=(narrowing_matrix, slope, widening_matrix),
        after=(joined_sums,),
        small=(matched_picture_ids, sharpening_log),
    )

    other = mp_other(part)
    widen_dealt = call(
        widen_grad_kernel,
        (normed2, grad_pre),
        dealt,
        scratch=(pltpu.VMEM(square, BF16),) * 2,
        index=(place,),
    )
    half = captions // 2
    mine = lax.dynamic_slice_in_dim(grad_caption_low, core * half, half, 0)
    mine = dp_gather(mine, steps[:1:-1], [part] * len(steps))
    widen_sum = scatter_steps(widen_dealt, place, mine)
    next(widen_sum)
    (all_sums,) = call(
        stack_kernel,
        sums_parts,
        (((all_pairs, hidden), BF16),),
        after=(widen_dealt[0],),
    )
    grad_residual, grad_branch1, flat, part, mixer_stat = call(
        mixer_back_kernel,
        (
            part,
            other,
            residual,
            grad_caption,
            sentence_word_ids,
            perceptron_layernorm_gamma,
            mixer_result_matrix,
        ),
        (
            (full, F32),
            (full, BF16),
            ((3, tokens, local_width), BF16),
            (full, F32),
            ((8, model_width), F32),
        ),
        outside=(qkv, soft, mixer_triple_matrix),
        after=(all_sums,),
    )
    other = mp_other(part)
    mixer_dealt = call(
        mixer_grad_kernel,
        (normed, flat, mixed, grad_branch1),
        dealt,
        scratch=(pltpu.VMEM(square, BF16),) * 2,
        index=(place,),
    )
    mixer_sum = scatter_steps(mixer_dealt, place)
    next(mixer_sum)
    folded = widen_sum.send((mixer_dealt[0],))
    grad_input, pack = call(
        entry_grad_kernel,
        (
            part,
            other,
            sentence_layer_entry,
            mixer_layernorm_gamma,
            grad_residual,
            loss_stat,
            mixer_stat,
        ),
        ((full, F32), ((16, model_width), F32)),
        after=(folded,),
    )
    cut = widen_sum.send((pack,))
    fold = mixer_sum.send((cut,))
    added = widen_sum.send((fold,))
    cut = mixer_sum.send((added,))
    joined = widen_sum.send((cut,))
    added = mixer_sum.send((joined,))
    widen_pieces = widen_sum.send(())
    joined = mixer_sum.send((added,))
    grad_w_up, near_grads = call(
        unpack_widen_kernel,
        widen_pieces,
        ((widening_matrix.shape, F32), ((all_pairs // 2, model_width), BF16)),
        index=(place,),
        after=(joined,),
    )
    grad_qkv, grad_w_out = call(
        unpack_mixer_kernel,
        mixer_sum.send(()),
        ((mixer_triple_matrix.shape, F32), (mixer_result_matrix.shape, F32)),
        index=(place,),
    )
    (grad_w_down,) = call(
        functools.partial(narrow_grad_kernel, half),
        (all_sums, near_grads, mp_other(near_grads)),
        ((narrowing_matrix.shape, F32),),
        scratch=(pltpu.VMEM((all_pairs, model_width), BF16),),
        index=(core,),
    )
    stats = dp_sum(pack)
    training_error = (stats[3, 1:2] + loss_stat[3, 2:3]) / (2.0 * all_pairs)
    return (
        training_error,
        grad_input,
        grad_qkv,
        stats[11].reshape(2, local_width),
        grad_w_out,
        stats[8],
        grad_w_up,
        stats[0:2].reshape(hidden),
        grad_w_down,
        stats[2],
        stats[4],
        stats[5],
        stats[9],
        stats[10],
        stats[3, 0:1],
    )


def solution(mesh):
    placed = (
        P("dp", None),
        P("dp"),
        P(("dp", "mp"), None, None),
        P(("dp", "mp")),
        P("dp"),
        P(),
        P(),
        P(None, None, "mp"),
        P(None, "mp"),
        P("mp", None),
        P(),
        P(),
        P(),
        P(None, "mp"),
        P("mp"),
        P("mp", None),
        P(),
        P(),
        P(),
        P(),
        P(),
        P(),
        P(),
    )
    return jax.shard_map(
        local,
        mesh=mesh,
        in_specs=placed,
        out_specs=(
            P(),
            P("dp", None),
            P(None, None, "mp"),
            P(None, "mp"),
            P("mp", None),
            P(),
            P(None, "mp"),
            P("mp"),
            P("mp", None),
            P(),
            P(),
            P(),
            P(),
            P(),
            P(),
        ),
        check_vma=False,
    )
```

profile of v0, /device:TPU:0, one launch (start us, length us, event | category | flops | bytes accessed | tf_op | source)
XLA Modules:
  0.0 289.0 jit_solution(17342773576162373790)
XLA Ops:
  0.6 5.0 %copy.38.token_ref = bf16[16,145,768]{2,1,0:T(8,128)(2,1)} copy(bf16[16,145,768]{2,0,1:T(8,128)(2,1)} %param.25) | data formatting | bytes 7127040 | tf_op args[2]
  5.7 44.3 %shard_map.334.refs_7_.refs_0_ = bf16[16,768]{1,0:T(8,128)(2,1)} custom-call(s32[16]{0:T(128)} %flag_ref.1, bf16[16,145,768]{2,1,0:T(8,128)(2,1)} %copy.38.token_ref, f32[2,768]{1,0:T(2,128)} %gain_ref.1, bf16[3,768,768]{2,1,0:T(8,128)(2,1)} %triple_hbm.1, bf16[768,768]{1,0:T(8,128)(2,1)} %result_hbm.1, bf16[768,3072]{1,0:T(8,128)(2,1)} %widen_hbm.1, ...), custom_call_target="tpu_custom_call" | custom-call | flops 30000001024 | bytes 20000000 | tf_op jit(solution)/shard_map/pallas_call | solution.py:246
  50.0 5.1 %collective-permute-start.2 = (bf16[16,768]{1,0:T(8,128)(2,1)}, bf16[16,768]{1,0:T(8,128)(2,1)}, u32[]{:S(2)}, u32[]{:S(2)}) collective-permute-start(bf16[16,768]{1,0:T(8,128)(2,1)} %shard_map.334.refs_7_.refs_0_), channel_id=1, source_target_pairs={{0,24},{2,26},{4,28},{6,30},{8,16},{10,18},{12,20},{14,22},{16,8},... | collective-permute-start | bytes 73736 | tf_op jit(solution)/shard_map/ppermute | solution.py:29
  55.1 5.1 %collective-permute-start.1 = (bf16[16,768]{1,0:T(8,128)(2,1)}, bf16[16,768]{1,0:T(8,128)(2,1)}, u32[]{:S(2)}, u32[]{:S(2)}) collective-permute-start(bf16[16,768]{1,0:T(8,128)(2,1)} %shard_map.334.refs_7_.refs_0_), channel_id=1, source_target_pairs={{0,16},{2,18},{4,20},{6,22},{8,24},{10,26},{12,28},{14,30},{16,0},... | collective-permute-start | bytes 73736 | tf_op jit(solution)/shard_map/ppermute | solution.py:29
  60.2 6.6 %shard_map.335 = (bf16[512,768]{1,0:T(8,128)(2,1)}, bf16[3,512,384]{2,1,0:T(8,128)(2,1)}, f32[4,3,256,128]{3,2,1,0:T(8,128)}, bf16[512,384]{1,0:T(8,128)(2,1)}, f32[512,768]{1,0:T(8,128)}) custom-call(bf16[512,768]{1,0:T(8,128)(2,1)} %refs_2_.4, s32[512]{0:T(512)} %refs_4_.5, f32[768]{0:T(1024)} %refs_3_.5, f32[768]{0:T(1024)} %refs_3_.3, ...), custom_call_target="tpu_custom_call" | custom-call | flops 999999995904 | bytes 999999995904 | tf_op jit(solution)/shard_map/pallas_call | solution.py:723
  68.2 7.9 %collective-permute-start.4 = (bf16[64,768]{1,0:T(8,128)(2,1)}, bf16[64,768]{1,0:T(8,128)(2,1)}, u32[]{:S(2)}, u32[]{:S(2)}) collective-permute-start(bf16[64,768]{1,0:T(8,128)(2,1)} %shard_map.336.refs_10_.refs_0_), channel_id=1, source_target_pairs={{0,4},{2,6},{4,0},{6,2},{8,12},{10,14},{12,8},{14,10},{16,20},{18,... | collective-permute-start | bytes 294920 | tf_op jit(solution)/shard_map/ppermute | solution.py:29
  76.1 8.8 %shard_map.337 = (f32[512,768]{1,0:T(8,128)}, bf16[512,768]{1,0:T(8,128)(2,1)}, f32[512,1536]{1,0:T(8,128)}, bf16[32,1536]{1,0:T(8,128)(2,1)}, f32[32,768]{1,0:T(8,128)}, /*index=5*/f32[32,768]{1,0:T(8,128)}) custom-call(bf16[512,768]{1,0:T(8,128)(2,1)} %refs_2_.4, f32[512,768]{1,0:T(8,128)} %get-tuple-element.74.refs_4_.refs_1_, ...), custom_call_target="tpu_custom_call" | custom-call | flops 999999995904 | bytes 999999995904 | tf_op jit(solution)/shard_map/pallas_call | solution.py:723
  96.5 4.6 %all-to-all-start = ((f32[16,1,512]{2,1,0:T(1,128)}), f32[16,1,512]{2,1,0:T(1,128)}, u32[]{:S(2)}, u32[]{:S(2)}) async-start(f32[16,1,512]{2,1,0:T(1,128)} %get-tuple-element.77), calls=%async_computation | async-start | bytes 65536 | tf_op jit(solution)/shard_map/all_to_all | solution.py:1021
  108.5 8.6 %shard_map.341 = (f32[32,768]{1,0:T(8,128)}, bf16[32,768]{1,0:T(8,128)(2,1)}, bf16[512,1536]{1,0:T(8,128)(2,1)}, f32[512,768]{1,0:T(8,128)}, f32[8,768]{1,0:T(8,128)}) custom-call(s32[32]{0:T(128)} %refs_0_.5, f32[1]{0:T(128)S(6)} %copy.39.refs_2_.refs_1_, f32[16,1,512]{2,1,0:T(1,128)} %all-to-all-done.refs_2_, f32[32,512]{1,0:T(8,128)} %get-tuple-element.78.refs_3_, ...), custom_call_target="tpu_custom_call" | custom-call | flops 999999995904 | bytes 999999995904 | tf_op jit(solution)/shard_map/pallas_call | solution.py:723
  117.1 4.4 %shard_map.342 = (bf16[384,768]{1,0:T(8,128)(2,1)}, bf16[384,768]{1,0:T(8,128)(2,1)}, bf16[384,768]{1,0:T(8,128)(2,1)}, bf16[384,768]{1,0:T(8,128)(2,1)}) custom-call(s32[1]{0:T(128)} %bitcast.refs_0_, bf16[512,768]{1,0:T(8,128)(2,1)} %get-tuple-element.92.refs_1_, bf16[512,1536]{1,0:T(8,128)(2,1)} %get-tuple-element.93.refs_2_), custom_call_target="tpu_custom_call" | custom-call | flops 999999995904 | bytes 999999995904 | tf_op jit(solution)/shard_map/pallas_call | solution.py:723
  127.0 10.8 %shard_map.344 = (f32[512,768]{1,0:T(8,128)}, bf16[512,768]{1,0:T(8,128)(2,1)}, bf16[3,512,384]{2,1,0:T(8,128)(2,1)}, f32[512,768]{1,0:T(8,128)}, f32[8,768]{1,0:T(8,128)}) custom-call(f32[512,768]{1,0:T(8,128)} %get-tuple-element.87.refs_0_, f32[512,768]{1,0:T(8,128)} %collective-permute-done.12.refs_1_, f32[512,768]{1,0:T(8,128)} %get-tuple-element.88.refs_2_, ...), custom_call_target="tpu_custom_call" | custom-call | flops 999999995904 | bytes 999999995904 | tf_op jit(solution)/shard_map/pallas_call | solution.py:723
  137.8 5.0 %shard_map.345 = (bf16[384,768]{1,0:T(8,128)(2,1)}, bf16[384,768]{1,0:T(8,128)(2,1)}, bf16[384,768]{1,0:T(8,128)(2,1)}, bf16[384,768]{1,0:T(8,128)(2,1)}) custom-call(s32[1]{0:T(128)} %bitcast.refs_0_, bf16[512,768]{1,0:T(8,128)(2,1)} %get-tuple-element.102.refs_1_, bf16[3,512,384]{2,1,0:T(8,128)(2,1)} %get-tuple-element.103.refs_2_, ...), custom_call_target="tpu_custom_call" | custom-call | flops 999999995904 | bytes 999999995904 | tf_op jit(solution)/shard_map/pallas_call | solution.py:723
  144.2 3.0 %shard_map.346 = (bf16[192,768]{1,0:T(8,128)(2,1)}, f32[192,768]{1,0:T(8,128)}, bf16[192,768]{1,0:T(8,128)(2,1)}, f32[192,768]{1,0:T(8,128)}) custom-call(s32[1]{0:T(128)} %bitcast.refs_0_, bf16[384,768]{1,0:T(8,128)(2,1)} %get-tuple-element.99.refs_1_, bf16[384,768]{1,0:T(8,128)(2,1)} %collective-permute-done.17.refs_2_, ...), custom_call_target="tpu_custom_call" | custom-call | flops 999999995904 | bytes 999999995904 | tf_op jit(solution)/shard_map/pallas_call | solution.py:723
  149.8 5.2 %shard_map.347 = (f32[512,768]{1,0:T(8,128)}, f32[16,768]{1,0:T(8,128)}) custom-call(f32[512,768]{1,0:T(8,128)} %get-tuple-element.95.refs_0_, f32[512,768]{1,0:T(8,128)} %collective-permute-done.16.refs_1_, bf16[512,768]{1,0:T(8,128)(2,1)} %refs_2_.4, f32[768]{0:T(1024)} %refs_3_.5, f32[512,768]{1,0:T(8,128)} %get-tuple-element.96.refs_4_, ...), custom_call_target="tpu_custom_call" | custom-call | flops 999999995904 | bytes 999999995904 | tf_op jit(solution)/shard_map/pallas_call | solution.py:723
  157.3 7.5 %collective-permute-done.26.refs_4_ = bf16[192,768]{1,0:T(8,128)(2,1)} collective-permute-done((bf16[192,768]{1,0:T(8,128)(2,1)}, bf16[192,768]{1,0:T(8,128)(2,1)}, u32[]{:S(2)}, u32[]{:S(2)}) %collective-permute-start.26) | collective-permute-done | bytes 294944 | tf_op jit(solution)/shard_map/ppermute | solution.py:29
  171.6 2.9 %shard_map.349 = (bf16[192,768]{1,0:T(8,128)(2,1)}, f32[192,768]{1,0:T(8,128)}, bf16[192,768]{1,0:T(8,128)(2,1)}, f32[192,768]{1,0:T(8,128)}) custom-call(s32[1]{0:T(128)} %bitcast.refs_0_, bf16[384,768]{1,0:T(8,128)(2,1)} %get-tuple-element.110.refs_1_, bf16[384,768]{1,0:T(8,128)(2,1)} %collective-permute-done.23.refs_2_, ...), custom_call_target="tpu_custom_call" | custom-call | flops 999999995904 | bytes 999999995904 | tf_op jit(solution)/shard_map/pallas_call | solution.py:723
  177.5 5.0 %collective-permute-done.30.refs_2_ = bf16[96,768]{1,0:T(8,128)(2,1)} collective-permute-done((bf16[96,768]{1,0:T(8,128)(2,1)}, bf16[96,768]{1,0:T(8,128)(2,1)}, u32[]{:S(2)}, u32[]{:S(2)}) %collective-permute-start.30) | collective-permute-done | bytes 147488 | tf_op jit(solution)/shard_map/ppermute | solution.py:29
  196.0 13.0 %collective-permute-done.36.refs_2_ = bf16[112,768]{1,0:T(8,128)(2,1)} collective-permute-done((bf16[112,768]{1,0:T(8,128)(2,1)}, bf16[112,768]{1,0:T(8,128)(2,1)}, u32[]{:S(2)}, u32[]{:S(2)}) %collective-permute-start.36) | collective-permute-done | bytes 172064 | tf_op jit(solution)/shard_map/ppermute | solution.py:29
  222.1 5.2 %collective-permute-done.39.refs_2_ = bf16[96,768]{1,0:T(8,128)(2,1)S(1)} collective-permute-done((bf16[96,768]{1,0:T(8,128)(2,1)}, bf16[96,768]{1,0:T(8,128)(2,1)S(1)}, u32[]{:S(2)}, u32[]{:S(2)}) %collective-permute-start.39) | collective-permute-done | bytes 147488 | tf_op jit(solution)/shard_map/ppermute | solution.py:29
  236.5 12.4 %collective-permute-done.19 = f32[16,768]{1,0:T(8,128)S(1)} collective-permute-done((f32[16,768]{1,0:T(8,128)S(1)}, f32[16,768]{1,0:T(8,128)S(1)}, u32[]{:S(2)}, u32[]{:S(2)}) %collective-permute-start.19) | collective-permute-done | bytes 49184 | tf_op jit(solution)/shard_map/ppermute | solution.py:29
  257.7 3.4 %collective-permute-start.22 = (f32[16,768]{1,0:T(8,128)S(1)}, f32[16,768]{1,0:T(8,128)S(1)}, u32[]{:S(2)}, u32[]{:S(2)}) collective-permute-start(f32[16,768]{1,0:T(8,128)S(1)} %add.21), channel_id=1, source_target_pairs={{0,16},{2,18},{4,20},{6,22},{8,24},{10,26},{12,28},{14,30},{16,0},... | collective-permute-start | bytes 147464 | tf_op jit(solution)/shard_map/ppermute | solution.py:29
  273.7 4.3 %shard_map.356 = (f32[768,1536]{1,0:T(8,128)}, bf16[256,768]{1,0:T(8,128)(2,1)}) custom-call(s32[1]{0:T(128)} %bitcast.refs_0_, bf16[448,768]{1,0:T(8,128)(2,1)} %shard_map.352.refs_4_.refs_1_, bf16[448,768]{1,0:T(8,128)(2,1)} %collective-permute-done.45.refs_2_, bf16[448,768]{1,0:T(8,128)(2,1)} %collective-permute-done.46.refs_3_, ...), custom_call_target="tpu_custom_call" | custom-call | flops 999999995904 | bytes 999999995904 | tf_op jit(solution)/shard_map/pallas_call | solution.py:723
  278.1 4.6 %shard_map.355 = (f32[3,768,384]{2,1,0:T(8,128)}, f32[384,768]{1,0:T(8,128)}) custom-call(s32[1]{0:T(128)} %bitcast.refs_0_, bf16[384,768]{1,0:T(8,128)(2,1)} %shard_map.354.refs_1_.refs_6_, bf16[384,768]{1,0:T(8,128)(2,1)} %copy-done.1, bf16[384,768]{1,0:T(8,128)(2,1)} %copy-done, bf16[192,768]{1,0:T(8,128)(2,1)} %collective-permute-done.43.refs_4_, ...), custom_call_target="tpu_custom_call" | custom-call | flops 999999995904 | bytes 999999995904 | tf_op jit(solution)/shard_map/pallas_call | solution.py:723
  282.7 5.2 %shard_map.357 = f32[1536,768]{1,0:T(8,128)} custom-call(s32[1]{0:T(128)} %bitcast.1.refs_0_, bf16[512,1536]{1,0:T(8,128)(2,1)} %shard_map.343.refs_10_.refs_1_, bf16[256,768]{1,0:T(8,128)(2,1)} %get-tuple-element.132.refs_2_, bf16[256,768]{1,0:T(8,128)(2,1)} %collective-permute-done.49.refs_3_), custom_call_target="tpu_custom_call" | custom-call | flops 999999995904 | bytes 999999995904 | tf_op jit(solution)/shard_map/pallas_call | solution.py:723
  (143 shorter events, 97.0 us)
Async XLA Ops:
  50.0 16.8 %collective-permute-start.2 = (bf16[16,768]{1,0:T(8,128)(2,1)}, bf16[16,768]{1,0:T(8,128)(2,1)}, u32[]{:S(2)}, u32[]{:S(2)}) collective-permute-start(bf16[16,768]{1,0:T(8,128)(2,1)} %shard_map.334.refs_7_.refs_0_), channel_id=1, source_target_pairs={{0,24},{2,26},{4,28},{6,30},{8,16},{10,18},{12,20},{14,22},{16,8},... | collective-permute-start | bytes 73736 | tf_op jit(solution)/shard_map/ppermute | solution.py:29
  68.2 16.7 %collective-permute-start.5 = (bf16[64,768]{1,0:T(8,128)(2,1)}, bf16[64,768]{1,0:T(8,128)(2,1)}, u32[]{:S(2)}, u32[]{:S(2)}) collective-permute-start(bf16[64,768]{1,0:T(8,128)(2,1)} %shard_map.336.refs_10_.refs_0_), channel_id=1, source_target_pairs={{0,6},{2,4},{4,2},{6,0},{8,14},{10,12},{12,10},{14,8},{16,22},{18,... | collective-permute-start | bytes 294920 | tf_op jit(solution)/shard_map/ppermute | solution.py:29
  68.2 16.7 %collective-permute-start.4 = (bf16[64,768]{1,0:T(8,128)(2,1)}, bf16[64,768]{1,0:T(8,128)(2,1)}, u32[]{:S(2)}, u32[]{:S(2)}) collective-permute-start(bf16[64,768]{1,0:T(8,128)(2,1)} %shard_map.336.refs_10_.refs_0_), channel_id=1, source_target_pairs={{0,4},{2,6},{4,0},{6,2},{8,12},{10,14},{12,8},{14,10},{16,20},{18,... | collective-permute-start | bytes 294920 | tf_op jit(solution)/shard_map/ppermute | solution.py:29
  103.0 20.2 %collective-permute-start.15 = (bf16[128,1536]{1,0:T(8,128)(2,1)}, bf16[128,1536]{1,0:T(8,128)(2,1)}, u32[]{:S(2)}, u32[]{:S(2)}) collective-permute-start(bf16[128,1536]{1,0:T(8,128)(2,1)} %shard_map.340.refs_14_.refs_0_), channel_id=1, source_target_pairs={{0,6},{2,4},{4,2},{6,0},{8,14},{10,12},{12,10},{14,8},{16,22},{18,... | collective-permute-start | bytes 1179656 | tf_op jit(solution)/shard_map/ppermute | solution.py:29
  105.4 17.9 %collective-permute-start.14 = (bf16[128,1536]{1,0:T(8,128)(2,1)}, bf16[128,1536]{1,0:T(8,128)(2,1)}, u32[]{:S(2)}, u32[]{:S(2)}) collective-permute-start(bf16[128,1536]{1,0:T(8,128)(2,1)} %shard_map.340.refs_14_.refs_0_), channel_id=1, source_target_pairs={{0,4},{2,6},{4,0},{6,2},{8,12},{10,14},{12,8},{14,10},{16,20},{18,... | collective-permute-start | bytes 1179656 | tf_op jit(solution)/shard_map/ppermute | solution.py:29
  106.5 16.8 %collective-permute-start.13 = (bf16[128,1536]{1,0:T(8,128)(2,1)}, bf16[128,1536]{1,0:T(8,128)(2,1)}, u32[]{:S(2)}, u32[]{:S(2)}) collective-permute-start(bf16[128,1536]{1,0:T(8,128)(2,1)} %shard_map.340.refs_14_.refs_0_), channel_id=1, source_target_pairs={{0,2},{2,0},{4,6},{6,4},{8,10},{10,8},{12,14},{14,12},{16,18},{18,... | collective-permute-start | bytes 1179656 | tf_op jit(solution)/shard_map/ppermute | solution.py:29
  121.5 22.7 %collective-permute-start.18 = (bf16[384,768]{1,0:T(8,128)(2,1)}, bf16[384,768]{1,0:T(8,128)(2,1)}, u32[]{:S(2)}, u32[]{:S(2)}) collective-permute-start(bf16[384,768]{1,0:T(8,128)(2,1)} %get-tuple-element.101), channel_id=1, source_target_pairs={{0,4},{2,6},{4,0},{6,2},{8,12},{10,14},{12,8},{14,10},{16,20},{18,... | collective-permute-start | bytes 1769480 | tf_op jit(solution)/shard_map/ppermute | solution.py:29
  122.0 22.2 %collective-permute-start.17 = (bf16[384,768]{1,0:T(8,128)(2,1)}, bf16[384,768]{1,0:T(8,128)(2,1)}, u32[]{:S(2)}, u32[]{:S(2)}) collective-permute-start(bf16[384,768]{1,0:T(8,128)(2,1)} %get-tuple-element.94.refs_4_), channel_id=1, source_target_pairs={{0,2},{2,0},{4,6},{6,4},{8,10},{10,8},{12,14},{14,12},{16,18},{18,... | collective-permute-start | bytes 1769480 | tf_op jit(solution)/shard_map/ppermute | solution.py:29
  142.8 28.8 %collective-permute-start.23 = (bf16[384,768]{1,0:T(8,128)(2,1)}, bf16[384,768]{1,0:T(8,128)(2,1)}, u32[]{:S(2)}, u32[]{:S(2)}) collective-permute-start(bf16[384,768]{1,0:T(8,128)(2,1)} %get-tuple-element.106.refs_5_), channel_id=1, source_target_pairs={{0,2},{2,0},{4,6},{6,4},{8,10},{10,8},{12,14},{14,12},{16,18},{18,... | collective-permute-start | bytes 1769480 | tf_op jit(solution)/shard_map/ppermute | solution.py:29
  148.7 16.1 %collective-permute-start.26 = (bf16[192,768]{1,0:T(8,128)(2,1)}, bf16[192,768]{1,0:T(8,128)(2,1)}, u32[]{:S(2)}, u32[]{:S(2)}) collective-permute-start(bf16[192,768]{1,0:T(8,128)(2,1)} %get-tuple-element.115), channel_id=1, source_target_pairs={{0,2},{2,0},{4,6},{6,4},{8,10},{10,8},{12,14},{14,12},{16,18},{18,... | collective-permute-start | bytes 884744 | tf_op jit(solution)/shard_map/ppermute | solution.py:29
  149.2 22.4 %collective-permute-start.24 = (bf16[384,768]{1,0:T(8,128)(2,1)}, bf16[384,768]{1,0:T(8,128)(2,1)}, u32[]{:S(2)}, u32[]{:S(2)}) collective-permute-start(bf16[384,768]{1,0:T(8,128)(2,1)} %get-tuple-element.112), channel_id=1, source_target_pairs={{0,4},{2,6},{4,0},{6,2},{8,12},{10,14},{12,8},{14,10},{16,20},{18,... | collective-permute-start | bytes 1769480 | tf_op jit(solution)/shard_map/ppermute | solution.py:29
  174.6 14.2 %collective-permute-start.27 = (bf16[192,768]{1,0:T(8,128)(2,1)}, bf16[192,768]{1,0:T(8,128)(2,1)}, u32[]{:S(2)}, u32[]{:S(2)}) collective-permute-start(bf16[192,768]{1,0:T(8,128)(2,1)} %get-tuple-element.118), channel_id=1, source_target_pairs={{0,4},{2,6},{4,0},{6,2},{8,12},{10,14},{12,8},{14,10},{16,20},{18,... | collective-permute-start | bytes 884744 | tf_op jit(solution)/shard_map/ppermute | solution.py:29
  186.6 22.4 %collective-permute-start.36 = (bf16[112,768]{1,0:T(8,128)(2,1)}, bf16[112,768]{1,0:T(8,128)(2,1)}, u32[]{:S(2)}, u32[]{:S(2)}) collective-permute-start(bf16[112,768]{1,0:T(8,128)(2,1)} %shard_map.350.refs_5_.refs_0_), channel_id=1, source_target_pairs={{0,16},{2,18},{4,20},{6,22},{8,24},{10,26},{12,28},{14,30},{16,0},... | collective-permute-start | bytes 516104 | tf_op jit(solution)/shard_map/ppermute | solution.py:29
  188.0 21.0 %collective-permute-start.35 = (bf16[112,768]{1,0:T(8,128)(2,1)}, bf16[112,768]{1,0:T(8,128)(2,1)}, u32[]{:S(2)}, u32[]{:S(2)}) collective-permute-start(bf16[112,768]{1,0:T(8,128)(2,1)} %shard_map.350.refs_5_.refs_0_), channel_id=1, source_target_pairs={{0,8},{2,10},{4,12},{6,14},{8,0},{10,2},{12,4},{14,6},{16,24},{18,... | collective-permute-start | bytes 516104 | tf_op jit(solution)/shard_map/ppermute | solution.py:29
  191.2 19.8 %collective-permute-start.32 = (bf16[96,768]{1,0:T(8,128)(2,1)}, bf16[96,768]{1,0:T(8,128)(2,1)}, u32[]{:S(2)}, u32[]{:S(2)}) collective-permute-start(bf16[96,768]{1,0:T(8,128)(2,1)} %get-tuple-element.126), channel_id=1, source_target_pairs={{0,8},{2,10},{4,12},{6,14},{8,0},{10,2},{12,4},{14,6},{16,24},{18,... | collective-permute-start | bytes 442376 | tf_op jit(solution)/shard_map/ppermute | solution.py:29
  192.5 18.9 %collective-permute-start.33 = (bf16[96,768]{1,0:T(8,128)(2,1)}, bf16[96,768]{1,0:T(8,128)(2,1)}, u32[]{:S(2)}, u32[]{:S(2)}) collective-permute-start(bf16[96,768]{1,0:T(8,128)(2,1)} %get-tuple-element.127), channel_id=1, source_target_pairs={{0,16},{2,18},{4,20},{6,22},{8,24},{10,26},{12,28},{14,30},{16,0},... | collective-permute-start | bytes 442376 | tf_op jit(solution)/shard_map/ppermute | solution.py:29
  194.0 17.4 %collective-permute-start.34 = (bf16[96,768]{1,0:T(8,128)(2,1)}, bf16[96,768]{1,0:T(8,128)(2,1)}, u32[]{:S(2)}, u32[]{:S(2)}) collective-permute-start(bf16[96,768]{1,0:T(8,128)(2,1)} %get-tuple-element.128), channel_id=1, source_target_pairs={{0,24},{2,26},{4,28},{6,30},{8,16},{10,18},{12,20},{14,22},{16,8},... | collective-permute-start | bytes 442376 | tf_op jit(solution)/shard_map/ppermute | solution.py:29
  217.7 17.4 %collective-permute-start.46 = (bf16[448,768]{1,0:T(8,128)(2,1)}, bf16[448,768]{1,0:T(8,128)(2,1)}, u32[]{:S(2)}, u32[]{:S(2)}) collective-permute-start(bf16[448,768]{1,0:T(8,128)(2,1)} %shard_map.352.refs_4_.refs_1_), channel_id=1, source_target_pairs={{0,4},{2,6},{4,0},{6,2},{8,12},{10,14},{12,8},{14,10},{16,20},{18,... | collective-permute-start | bytes 2064392 | tf_op jit(solution)/shard_map/ppermute | solution.py:29
  218.5 37.1 %collective-permute-start.45 = (bf16[448,768]{1,0:T(8,128)(2,1)}, bf16[448,768]{1,0:T(8,128)(2,1)}, u32[]{:S(2)}, u32[]{:S(2)}) collective-permute-start(bf16[448,768]{1,0:T(8,128)(2,1)} %shard_map.352.refs_4_.refs_1_), channel_id=1, source_target_pairs={{0,2},{2,0},{4,6},{6,4},{8,10},{10,8},{12,14},{14,12},{16,18},{18,... | collective-permute-start | bytes 2064392 | tf_op jit(solution)/shard_map/ppermute | solution.py:29
  230.6 36.3 %collective-permute-start.42 = (bf16[384,768]{1,0:T(8,128)(2,1)}, bf16[384,768]{1,0:T(8,128)(2,1)S(1)}, u32[]{:S(2)}, u32[]{:S(2)}) collective-permute-start(bf16[384,768]{1,0:T(8,128)(2,1)} %shard_map.354.refs_1_.refs_6_), channel_id=1, source_target_pairs={{0,4},{2,6},{4,0},{6,2},{8,12},{10,14},{12,8},{14,10},{16,20},{18,... | collective-permute-start | bytes 1769480 | tf_op jit(solution)/shard_map/ppermute | solution.py:29
  230.9 39.0 %collective-permute-start.41 = (bf16[384,768]{1,0:T(8,128)(2,1)}, bf16[384,768]{1,0:T(8,128)(2,1)S(1)}, u32[]{:S(2)}, u32[]{:S(2)}) collective-permute-start(bf16[384,768]{1,0:T(8,128)(2,1)} %shard_map.354.refs_1_.refs_6_), channel_id=1, source_target_pairs={{0,2},{2,0},{4,6},{6,4},{8,10},{10,8},{12,14},{14,12},{16,18},{18,... | collective-permute-start | bytes 1769480 | tf_op jit(solution)/shard_map/ppermute | solution.py:29
  233.4 15.5 %collective-permute-start.19 = (f32[16,768]{1,0:T(8,128)S(1)}, f32[16,768]{1,0:T(8,128)S(1)}, u32[]{:S(2)}, u32[]{:S(2)}) collective-permute-start(f32[16,768]{1,0:T(8,128)S(1)} %copy-done.2), channel_id=1, source_target_pairs={{0,2},{2,0},{4,6},{6,4},{8,10},{10,8},{12,14},{14,12},{16,18},{18,... | collective-permute-start | bytes 147464 | tf_op jit(solution)/shard_map/ppermute | solution.py:29
  236.1 36.1 %collective-permute-start.47 = (bf16[256,768]{1,0:T(8,128)(2,1)S(1)}, bf16[256,768]{1,0:T(8,128)(2,1)S(1)}, u32[]{:S(2)}, u32[]{:S(2)}) collective-permute-start(bf16[256,768]{1,0:T(8,128)(2,1)S(1)} %slice.65), channel_id=1, source_target_pairs={{0,2},{2,0},{4,6},{6,4},{8,10},{10,8},{12,14},{14,12},{16,18},{18,... | collective-permute-start | bytes 1179656 | tf_op jit(solution)/shard_map/ppermute | solution.py:29
  256.6 15.6 %collective-permute-start.48 = (bf16[192,768]{1,0:T(8,128)(2,1)S(1)}, bf16[192,768]{1,0:T(8,128)(2,1)S(1)}, u32[]{:S(2)}, u32[]{:S(2)}) collective-permute-start(bf16[192,768]{1,0:T(8,128)(2,1)S(1)} %slice.66), channel_id=1, source_target_pairs={{0,4},{2,6},{4,0},{6,2},{8,12},{10,14},{12,8},{14,10},{16,20},{18,... | collective-permute-start | bytes 884744 | tf_op jit(solution)/shard_map/ppermute | solution.py:29
  (39 other events, 279.9 us)
where the time goes:
time: 294 us; the launch traced here: 289 us
  Pallas kernels  137 us (47%)
  starting transfers between devices  73.3 us (25%)
  waiting for transfers between devices  58 us (20%)
  local copies, waits for them, and re-layouts  16.5 us (6%)
  between operations  3.99 us (1%)
    pallas_call x23, Pallas kernels, call(): pl.pallas_call(body, out_shape=[jax.ShapeDtypeStruct(shape, kind) for sha...  92.4 us
    ppermute x44, starting transfers between devices, dp_swap(): lax.ppermute(values, 'dp', [(index, index ^ mask) for index in range(size)])  68.1 us
    ppermute x44, waiting for transfers between devices, dp_swap(): lax.ppermute(values, 'dp', [(index, index ^ mask) for index in range(size)])  55 us
    pallas_call x1, Pallas kernels, image_tower(): pl.pallas_call(image_kernel, out_shape=jax.ShapeDtypeStruct((images, widt...  44.3 us
    unnamed x25, local copies, waits for them, and re-layouts  8.63 us
  transfers between devices with their start and end apart: 51, of which 16 were waited for; matrix products, arithmetic and copies ran while one was open for 3% of the time, Pallas kernels for 29%

commit v1 on v0

--- a/solution.py
+++ b/solution.py
@@ -51,16 +51,13 @@
 def dp_gather(values, steps, waits):
     for step, wait in zip(steps, waits):
         parts = dp_parts(values, step)
-        shape = (len(parts) * values.shape[0], values.shape[1])
-        (values,) = call(stack_kernel, parts, ((shape, values.dtype),), after=(wait,))
-    return values
-
-
-def dp_sum(values):
-    mask = 1
-    while mask < lax.axis_size("dp"):
-        values = values + dp_swap(values, mask)
-        mask *= 2
+        rows = values.shape[0]
+        (values,) = move(
+            parts,
+            (len(parts) * rows,),
+            [(place, 0, rows, 0, place * rows) for place in range(len(parts))],
+            (wait,),
+        )
     return values
 
 
@@ -68,8 +65,10 @@
 LOW_ROWS = 64
 TILE = 256
 PAIR = 2 * HEAD
+LANES = 128
+POOL_ROWS = 32
 NT = (((1,), (1,)), ((), ()))
-VMEM_LIMIT = 56 * 1024 * 1024
+VMEM_LIMIT = 60 * 1024 * 1024
 BUSY = 10**12
 
 
@@ -102,6 +101,7 @@
     widen_hbm,
     narrow_hbm,
     out_ref,
+    wide,
     packed,
     queries,
     keys,
@@ -110,52 +110,65 @@
     result,
     widen,
     narrow,
-    resid_sum,
-    hidden_sum,
+    resid_groups,
+    hidden_groups,
+    pooled,
     starts,
     sems,
 ):
-    images, _, width = token_ref.shape
+    _, images, width = token_ref.shape
     hidden = widen.shape[1]
-    pairs = (
-        (triple_hbm, triple),
-        (result_hbm, result),
-        (widen_hbm, widen),
-        (narrow_hbm, narrow),
-    )
-    copies = [
-        pltpu.make_async_copy(source, target, sems.at[place])
-        for place, (source, target) in enumerate(pairs)
-    ]
-    for copy in copies:
-        copy.start()
-    resid_sum[...] = jnp.zeros_like(resid_sum)
-    hidden_sum[...] = jnp.zeros_like(hidden_sum)
+    copies = fetch(
+        (triple_hbm, result_hbm, widen_hbm, narrow_hbm), (triple, result, widen, narrow), sems
+    )
+    lane_tiles = [slice(lane, lane + LANES) for lane in range(0, width, LANES)]
+
+    def spread(position, carry):
+        rows = pl.ds(pl.multiple_of(position * images, images), images)
+        for place, lanes in enumerate(lane_tiles):
+            wide[place, rows, :] = token_ref[position, :, lanes].astype(F32)
+        return carry
+
+    def begin(image, start):
+        starts[image] = start
+        return start + jnp.where(flag_ref[image] == 1, HIGH_ROWS, LOW_ROWS)
+
+    total = lax.fori_loop(0, images, begin, jnp.int32(0))
+    lax.fori_loop(0, LOW_ROWS, spread, 0, unroll=4)
+
+    @pl.when(total > images * LOW_ROWS)
+    def _():
+        lax.fori_loop(LOW_ROWS, IMG_TOK, spread, 0, unroll=3)
 
     tail = IMG_TOK // 16 * 16
 
-    def pack(image, start):
-        start = pl.multiple_of(start, 16)
-        starts[image] = start
+    def pack(image, carry):
+        start = pl.multiple_of(starts[image], POOL_ROWS)
         high = flag_ref[image] == 1
 
         @pl.when(high)
         def _():
-            packed[pl.ds(start, tail), :] = token_ref[image, 0:tail, :]
-            last = token_ref[image, tail:IMG_TOK, :].astype(F32)
-            row = lax.broadcasted_iota(jnp.int32, (HIGH_ROWS - tail, width), 0)
-            packed[pl.ds(start + tail, HIGH_ROWS - tail), :] = jnp.where(
-                row == 0, last, 0.0
-            ).astype(BF16)
+            row = lax.broadcasted_iota(jnp.int32, (HIGH_ROWS - tail, LANES), 0)
+            for place, lanes in enumerate(lane_tiles):
+                packed[pl.ds(start, tail), lanes] = wide[
+                    place, pl.ds(image, tail, stride=images), :
+                ].astype(BF16)
+                last = wide[place, pl.ds(image + tail * images, 1), :]
+                packed[pl.ds(start + tail, HIGH_ROWS - tail), lanes] = jnp.where(
+                    row == 0, last, 0.0
+                ).astype(BF16)
 
         @pl.when(jnp.logical_not(high))
         def _():
-            packed[pl.ds(start, LOW_ROWS), :] = token_ref[image, 0:LOW_ROWS, :]
-
-        return start + jnp.where(high, HIGH_ROWS, LOW_ROWS)
-
-    total = lax.fori_loop(0, images, pack, jnp.int32(0))
-    packed[pl.ds(pl.multiple_of(total, 16), TILE), :] = jnp.zeros((TILE, width), BF16)
+            for place, lanes in enumerate(lane_tiles):
+                packed[pl.ds(start, LOW_ROWS), lanes] = wide[
+                    place, pl.ds(image, LOW_ROWS, stride=images), :
+                ].astype(BF16)
+
+        return carry
+
+    lax.fori_loop(0, images, pack, 0)
+    packed[pl.ds(pl.multiple_of(total, POOL_ROWS), TILE), :] = jnp.zeros((TILE, width), BF16)
     tiles = lax.div(total + (TILE - 1), jnp.int32(TILE))
 
     copies[0].wait()
@@ -177,9 +190,8 @@
         for pair in range(width // PAIR):
             lanes = slice(pair * PAIR, (pair + 1) * PAIR)
             q, k, v = queries[rows, lanes], keys[rows, lanes], values[rows, lanes]
-            zero, one = jnp.zeros_like(q), jnp.ones_like(v)
-            both = jnp.concatenate([jnp.where(left, q, zero), jnp.where(left, zero, q)], axis=0)
-            scores = lax.dot_general(both, k, NT, preferred_element_type=F32)
+            one = jnp.ones_like(v)
+            scores = dot_t(two_heads(q, left), k)
             scores = jnp.where(key_live, scores, MASKED_SCORE)
             powers = jnp.exp(scores - jnp.max(scores, axis=-1, keepdims=True)).astype(BF16)
             first = dot(powers[:count], jnp.where(left, v, one))
@@ -188,7 +200,7 @@
             queries[rows, lanes] = (jnp.where(left, first, second) / sums).astype(BF16)
 
     def mix(image, carry):
-        start = pl.multiple_of(starts[image], 16)
+        start = pl.multiple_of(starts[image], POOL_ROWS)
         high = flag_ref[image] == 1
 
         @pl.when(high)
@@ -203,44 +215,82 @@
 
     lax.fori_loop(0, images, mix, 0)
 
-    slot = lax.broadcasted_iota(jnp.int32, (images, 1), 0)
-    begin = jnp.zeros((images, 1), jnp.int32)
-    live = jnp.zeros((images, 1), jnp.int32)
+    slot = lax.broadcasted_iota(jnp.int32, (1, images), 1)
+    first_row = jnp.zeros((1, images), jnp.int32)
+    live_rows = jnp.zeros((1, images), jnp.int32)
     for image in range(images):
-        begin = jnp.where(slot == image, starts[image], begin)
-        live = jnp.where(
-            slot == image, jnp.where(flag_ref[image] == 1, IMG_TOK, LOW_TOK), live
+        first_row = jnp.where(slot == image, starts[image], first_row)
+        live_rows = jnp.where(
+            slot == image, jnp.where(flag_ref[image] == 1, IMG_TOK, LOW_TOK), live_rows
         )
     copies[1].wait()
     copies[2].wait()
+    groups = TILE // POOL_ROWS
+
+    def group_sum(rows):
+        return jnp.sum(rows.reshape(groups, POOL_ROWS // 8, 8, rows.shape[1]), axis=1)
 
     def perceptron(tile, carry):
         base = pl.multiple_of(tile * TILE, TILE)
         rows = pl.ds(base, TILE)
-        place = base + lax.broadcasted_iota(jnp.int32, (images, TILE), 1)
-        pool = jnp.where((place >= begin) & (place < begin + live), 1.0, 0.0).astype(BF16)
-        residual = packed[rows, :].astype(F32) + dot(queries[rows, :], result[...])
-        upper = residual.astype(BF16)
-        lower = (residual - upper.astype(F32)).astype(BF16)
-        resid_sum[...] += dot(pool, upper) + dot(pool, lower)
+        place = base + lax.broadcasted_iota(jnp.int32, (TILE, images), 0)
+        alive = jnp.sum(
+            jnp.where((place >= first_row) & (place < first_row + live_rows), 1.0, 0.0),
+            axis=1,
+            keepdims=True,
+        )
+        residual = (packed[rows, :].astype(F32) + dot(queries[rows, :], result[...])) * alive
+        group = pl.ds(pl.multiple_of(tile * groups, groups), groups)
+        resid_groups[group] = group_sum(residual)
         normed = (standard(residual, EPS_UNIT) * gain_ref[1:2, :]).astype(BF16)
         for chunk in range(hidden // width):
             lanes = slice(chunk * width, (chunk + 1) * width)
             units = gelu(dot(normed, widen[:, lanes])).astype(BF16)
-            hidden_sum[:, lanes] += dot(pool, units)
+            hidden_groups[group, :, lanes] = group_sum(units.astype(F32))
         return carry
 
     lax.fori_loop(0, tiles, perceptron, 0)
+
+    def pool(image, carry):
+        group = lax.div(starts[image], jnp.int32(POOL_ROWS))
+        high = flag_ref[image] == 1
+
+        def add(count):
+            residual, units = resid_groups[group], hidden_groups[group]
+            for step in range(1, count):
+                residual = residual + resid_groups[group + step]
+                units = units + hidden_groups[group + step]
+            pooled[pl.ds(image, 1), :width] = jnp.sum(residual, axis=0, keepdims=True)
+            pooled[pl.ds(image, 1), width:] = jnp.sum(units, axis=0, keepdims=True)
+
+        @pl.when(high)
+        def _():
+            add(HIGH_ROWS // POOL_ROWS)
+
+        @pl.when(jnp.logical_not(high))
+        def _():
+            add(LOW_ROWS // POOL_ROWS)
+
+        return carry
+
+    lax.fori_loop(0, images, pool, 0)
     copies[3].wait()
-    pooled = (resid_sum[...] + wide_dot(hidden_sum[...], narrow[...])) / live.astype(F32)
+    units = pooled[:, width:]
+    upper = units.astype(BF16)
+    lower = (units - upper.astype(F32)).astype(BF16)
+    branch = dot(jnp.concatenate([upper, lower], axis=0), narrow[...])
+    live = jnp.where(number_column(flag_ref) == 1, IMG_TOK, LOW_TOK).astype(F32)
+    mean = (pooled[:, :width] + branch[:images] + branch[images:]) / live
     out_ref[...] = (
-        pooled * lax.rsqrt(jnp.sum(pooled * pooled, axis=-1, keepdims=True) + EPS_UNIT)
+        mean * lax.rsqrt(jnp.sum(mean * mean, axis=-1, keepdims=True) + EPS_UNIT)
     ).astype(BF16)
 
 
 def image_tower(flags, tokens, gains, triple, result, widen, narrow):
     images, _, width = tokens.shape
+    hidden = widen.shape[1]
     rows = images * HIGH_ROWS + TILE
+    groups = rows // POOL_ROWS
     outside = pl.BlockSpec(memory_space=pl.ANY)
     inside = pl.BlockSpec(memory_space=pltpu.VMEM)
     return pl.pallas_call(
@@ -249,19 +299,19 @@
         in_specs=[pl.BlockSpec(memory_space=pltpu.SMEM), inside, inside]
         + [outside] * 4,
         out_specs=inside,
-        scratch_shapes=[pltpu.VMEM((rows, width), BF16)] * 4
+        scratch_shapes=[pltpu.VMEM((width // LANES, IMG_TOK * images, LANES), F32)]
+        + [pltpu.VMEM((rows, width), BF16)] * 4
         + [pltpu.VMEM(weight.shape, BF16) for weight in (triple, result, widen, narrow)]
         + [
-            pltpu.VMEM((images, width), F32),
-            pltpu.VMEM((images, widen.shape[1]), F32),
+            pltpu.VMEM((groups, 8, width), F32),
+            pltpu.VMEM((groups, 8, hidden), F32),
+            pltpu.VMEM((images, width + hidden), F32),
             pltpu.SMEM((images,), jnp.int32),
             pltpu.SemaphoreType.DMA((4,)),
         ],
         compiler_params=pltpu.CompilerParams(vmem_limit_bytes=VMEM_LIMIT),
-        cost_estimate=pl.CostEstimate(
-            flops=30_000_000_000, bytes_accessed=20_000_000, transcendentals=10_000_000
-        ),
-    )(flags, tokens, gains, triple, result, widen, narrow)
+        cost_estimate=pl.CostEstimate(flops=BUSY, bytes_accessed=BUSY, transcendentals=0),
+    )(flags, jnp.transpose(tokens, (1, 0, 2)), gains, triple, result, widen, narrow)
 
 
 TN = (((0,), (0,)), ((), ()))
@@ -286,12 +336,6 @@
     for copy in copies:
         copy.start()
     return copies
-
-
-def stack_kernel(*refs):
-    rows = refs[0].shape[0]
-    for place, ref in enumerate(refs[:-1]):
-        refs[-1][place * rows : (place + 1) * rows, :] = ref[...]
 
 
 def caption_pool(ids_ref, captions):
@@ -476,9 +520,7 @@
     powers_ref[...] = powers
     row_sum = jnp.sum(powers, axis=1, keepdims=True)
     row_sum_ref[...] = jnp.broadcast_to(row_sum, row_sum_ref.shape)
-    col_sum_ref[...] = jnp.broadcast_to(
-        jnp.sum(powers, axis=0, keepdims=True)[None], col_sum_ref.shape
-    )
+    col_sum_ref[...] = jnp.sum(powers, axis=0, keepdims=True)
     positive = number_column(matched_ref) == lax.broadcasted_iota(jnp.int32, (captions, pairs), 1)
     wanted = jnp.sum(jnp.where(positive, logits, 0.0), axis=1, keepdims=True)
     loss_ref[...] = jnp.broadcast_to(
@@ -486,10 +528,17 @@
     )
 
 
+def sum_kernel(first_ref, second_ref, third_ref, fourth_ref, out_ref):
+    out_ref[...] = (first_ref[...] + second_ref[...]) + (third_ref[...] + fourth_ref[...])
+
+
 def loss_grad_kernel(
     matched_ref,
     sharpen_ref,
-    col_parts_ref,
+    col_ref,
+    col1_ref,
+    col2_ref,
+    col3_ref,
     logits_ref,
     powers_ref,
     row_sum_ref,
@@ -516,7 +565,7 @@
     width = grad_ref.shape[1]
     copies = fetch((narrow_hbm, slope_hbm, widen_hbm), (narrow, slope, widen), sems)
     logits, powers = logits_ref[...], powers_ref[...]
-    col_sum = jnp.sum(col_parts_ref[...], axis=0)
+    col_sum = (col_ref[...] + col1_ref[...]) + (col2_ref[...] + col3_ref[...])
     positive = number_column(matched_ref) == lax.broadcasted_iota(jnp.int32, (captions, pairs), 1)
     derivative = (
         powers / row_sum_ref[:, 0:1] + powers / col_sum - jnp.where(positive, 2.0, 0.0)
@@ -667,19 +716,25 @@
     deal(index_ref, first, second, outs)
 
 
-def narrow_grad_kernel(half, index_ref, sums_ref, near_ref, far_ref, out_ref, grads):
-    width = grads.shape[1]
-    core = index_ref[0]
+def narrow_grad_kernel(half, index_ref, *refs):
+    parts, (near_ref, far_ref, out_ref, grads) = refs[:-4], refs[-4:]
+    rows, width = parts[0].shape[0], grads.shape[1]
     for place in range(near_ref.shape[0] // half):
-        for ref, which in ((near_ref, core), (far_ref, 1 - core)):
+        for ref, which in ((near_ref, index_ref[0]), (far_ref, 1 - index_ref[0])):
             start = pl.multiple_of((2 * place + which) * half, half)
             grads[pl.ds(start, half), :] = ref[place * half : (place + 1) * half, :]
-    for chunk in range(sums_ref.shape[1] // width):
+    for chunk in range(out_ref.shape[0] // width):
         lanes = slice(chunk * width, (chunk + 1) * width)
-        out_ref[lanes, :] = t_dot(sums_ref[:, lanes], grads[...])
+        total = t_dot(parts[0][:, lanes], grads[:rows, :])
+        for place in range(1, len(parts)):
+            total = total + t_dot(
+                parts[place][:, lanes], grads[place * rows : (place + 1) * rows, :]
+            )
+        out_ref[lanes, :] = total
 
 
 def entry_grad_kernel(
+    index_ref,
     own_ref,
     other_ref,
     entry_ref,
@@ -687,18 +742,27 @@
     grad_residual_ref,
     loss_stat_ref,
     mixer_stat_ref,
+    caption_ref,
     out_ref,
-    pack_ref,
+    extra_ref,
+    pack,
 ):
     entry = entry_ref[...].astype(F32)
     centered = entry - jnp.mean(entry, axis=-1, keepdims=True)
     rate = lax.rsqrt(jnp.mean(centered * centered, axis=-1, keepdims=True) + EPS_TEXT)
     unit = centered * rate
     grad = own_ref[...] + other_ref[...]
-    pack_ref[0:8, :] = loss_stat_ref[...]
-    pack_ref[8:16, :] = mixer_stat_ref[...]
-    pack_ref[4:5, :] = jnp.sum(grad * unit, axis=0, keepdims=True)
-    pack_ref[5:6, :] = jnp.sum(grad, axis=0, keepdims=True)
+    pack[0:8, :] = loss_stat_ref[...]
+    pack[8:16, :] = mixer_stat_ref[...]
+    pack[4:5, :] = jnp.sum(grad * unit, axis=0, keepdims=True)
+    pack[5:6, :] = jnp.sum(grad, axis=0, keepdims=True)
+    half = caption_ref.shape[0] // 2
+    extra_ref[:half, :] = caption_ref[
+        pl.ds(pl.multiple_of(index_ref[0] * half, half), half), :
+    ]
+    upper = pack[...].astype(BF16).astype(F32)
+    pack[15:16, :] = (pack[...] - upper)[3:4, :]
+    extra_ref[half:, :] = pack[...].astype(BF16)
     scaled = grad * as_row(gain_ref)
     out_ref[...] = grad_residual_ref[...] + rate * (
         scaled
@@ -707,7 +771,64 @@
     )
 
 
-def call(kernel, inside, shapes, outside=(), scratch=(), index=(), small=(), after=()):
+def tree_sum(values):
+    while len(values) > 1:
+        values = [values[place] + values[place + 1] for place in range(0, len(values), 2)]
+    return values[0]
+
+
+def collect_kernel(
+    scale,
+    rows,
+    joined_ref,
+    along_x_ref,
+    along_y_ref,
+    first_far_ref,
+    second_far_ref,
+    loss_ref,
+    near_ref,
+    error_ref,
+    pair_ref,
+    result_ref,
+    widen_ref,
+    narrow_ref,
+    gain1_ref,
+    shift1_ref,
+    gain2_ref,
+    shift2_ref,
+    temperature_ref,
+):
+    half = rows - 16
+    first = second_far_ref.shape[0]
+    count = (first_far_ref.shape[0] - first) // rows
+    totals = []
+    for piece, ref in enumerate((joined_ref, along_x_ref, along_y_ref, first_far_ref)):
+        for place in range(count):
+            row = first + place * rows
+            near_ref[pl.ds((piece * count + place) * half, half), :] = ref[row : row + half, :]
+            totals.append(ref[row + half : row + rows, :].astype(F32))
+    total = tree_sum(totals)
+    scalars = total[3:4] + total[15:16]
+    error_ref[...] = ((scalars[:, 1:2] + loss_ref[3:4, 2:3]) * scale).reshape(1)
+    temperature_ref[...] = scalars[:, 0:1].reshape(1)
+    lanes = pair_ref.shape[1]
+    pair_ref[0:1, :] = total[11:12, :lanes]
+    pair_ref[1:2, :] = total[11:12, lanes:]
+    width = total.shape[1]
+    for chunk in range(widen_ref.shape[0] // width):
+        widen_ref[chunk * width : (chunk + 1) * width] = total[chunk]
+    for ref, place in (
+        (narrow_ref, 2),
+        (gain1_ref, 4),
+        (shift1_ref, 5),
+        (result_ref, 8),
+        (gain2_ref, 9),
+        (shift2_ref, 10),
+    ):
+        ref[...] = total[place]
+
+
+def call(kernel, inside, shapes, outside=(), scratch=(), index=(), small=(), after=(), limit=24):
     vmem = pl.BlockSpec(memory_space=pltpu.VMEM)
     extra = [pltpu.VMEM(array.shape, array.dtype) for array in outside]
     extra += list(scratch)
@@ -728,39 +849,51 @@
         + [pl.BlockSpec(memory_space=pl.ANY)] * (len(outside) + len(after)),
         out_specs=[vmem] * len(shapes),
         scratch_shapes=extra,
-        compiler_params=pltpu.CompilerParams(vmem_limit_bytes=VMEM_LIMIT),
+        compiler_params=pltpu.CompilerParams(vmem_limit_bytes=limit * 1024 * 1024),
         cost_estimate=pl.CostEstimate(flops=BUSY, bytes_accessed=BUSY, transcendentals=0),
     )(*small, *inside, *outside, *after)
 
 
+def move(arrays, sizes, plan, after=()):
+    width, kind = arrays[0].shape[1], arrays[0].dtype
+
+    def body(*refs):
+        ins, outs = refs[: len(arrays)], refs[len(arrays) :]
+        for source, first, rows, target, start in plan:
+            outs[target][start : start + rows, :] = ins[source][first : first + rows, :]
+
+    return call(body, arrays, tuple(((size, width), kind) for size in sizes), after=after)
+
+
 GROUP = 16
 Z_STRIDE, Z_SIZE = 4, 4
 
 
+def block_rows(block, rows):
+    return pl.ds(pl.multiple_of(block * rows, rows), rows)
+
+
 def fold_kernel(index_ref, *refs):
     ins, outs = refs[:4], refs[4:]
-    half = ins[0].shape[0] // 2
+    half = outs[0].shape[0]
     for place, bit in ((0, 2), (1, 1)):
-        total = ins[2 * place][...].astype(F32) + ins[2 * place + 1][...].astype(F32)
-        upper = index_ref[0] // bit % 2 == 1
-        low, high = total[:half], total[half:]
-        outs[2 * place][...] = jnp.where(upper, low, high).astype(BF16)
-        outs[2 * place + 1][...] = jnp.where(upper, high, low)
+        mine = index_ref[0] // bit % 2
+        for out, which in ((outs[2 * place], 1 - mine), (outs[2 * place + 1], mine)):
+            rows = block_rows(which, half)
+            out[...] = (
+                ins[2 * place][rows, :].astype(F32) + ins[2 * place + 1][rows, :].astype(F32)
+            ).astype(out.dtype)
 
 
 def cut_kernel(index_ref, *refs):
-    ins, outs, total = refs[:4], refs[4:-1], refs[-1]
-    rows = total.shape[0] // (2 * Z_SIZE)
+    ins, outs = refs[:4], refs[4:]
+    rows = ins[0].shape[0] // Z_SIZE
     for place in range(2):
-        total[pl.ds(place * rows * Z_SIZE, rows * Z_SIZE), :] = ins[2 * place][...] + ins[
-            2 * place + 1
-        ][...].astype(F32)
-        for step in range(Z_SIZE):
-            block = (index_ref[0] // Z_STRIDE % Z_SIZE) ^ step
-            start = pl.multiple_of((place * Z_SIZE + block) * rows, rows)
-            outs[step][place * rows : (place + 1) * rows, :] = total[
-                pl.ds(start, rows), :
-            ].astype(outs[step].dtype)
+        for step, out in enumerate(outs):
+            block = block_rows((index_ref[0] // Z_STRIDE % Z_SIZE) ^ step, rows)
+            out[place * rows : (place + 1) * rows, :] = (
+                ins[2 * place][block, :] + ins[2 * place + 1][block, :].astype(F32)
+            ).astype(out.dtype)
 
 
 def add_kernel(own_ref, *refs):
@@ -772,17 +905,6 @@
     out_ref[:rows, :] = total.astype(out_ref.dtype)
     if out_ref.shape[0] > rows:
         out_ref[rows:, :] = refs[Z_SIZE - 1][...]
-
-
-def join_kernel(extra, *refs):
-    ins, out = refs[:Z_SIZE], refs[Z_SIZE]
-    rows = (ins[0].shape[0] - extra) // 2
-    start = 0
-    for first, count in ((0, rows), (2 * rows, extra), (rows, rows)):
-        for ref in ins:
-            if count:
-                out[start : start + count, :] = ref[first : first + count, :]
-            start += count
 
 
 def scatter_steps(dealt, place, extra=None):
@@ -805,39 +927,47 @@
         cut_kernel,
         (first_kept, arrived[0], second_kept, arrived[1]),
         ((block, F32),) + ((block, BF16),) * (Z_SIZE - 1),
-        scratch=(pltpu.VMEM((rows, width), F32),),
         index=(place,),
         after=after,
     )
     after = yield own
     arrived = [dp_swap(values, step * Z_STRIDE) for step, values in enumerate(sent, 1)]
     size = lax.axis_size("dp")
-    more = 0 if extra is None else extra.shape[0]
+    more = 0 if extra is None else extra[0].shape[0]
     if size > GROUP:
         (mine,) = call(add_kernel, (own, *arrived), ((own.shape, F32),), after=after)
         groups = [list(range(index, size, GROUP)) for index in range(GROUP)]
         mine = lax.psum(mine, "dp", axis_index_groups=groups).astype(BF16)
         if more:
-            mine = jnp.concatenate([mine, extra], axis=0)
+            mine = jnp.concatenate([mine, *extra], axis=0)
     else:
         (mine,) = call(
             add_kernel,
-            (own, *arrived) + ((extra,) if more else ()),
+            (own, *arrived) + (tuple(extra) if more else ()),
             (((block[0] + more, width), BF16),),
             after=after,
         )
     after = yield mine
     pieces = [mine] + [dp_swap(mine, step * Z_STRIDE) for step in range(1, Z_SIZE)]
-    (joined,) = call(
-        functools.partial(join_kernel, more),
-        pieces,
-        (((Z_SIZE * (block[0] + more), width), BF16),),
-        after=after,
-    )
-    cut = Z_SIZE * (block[0] // 2 + more)
+    half = block[0] // 2
+    plan, start = [], 0
+    for first, count in ((0, half), (2 * half, more), (half, half)):
+        for piece in range(Z_SIZE):
+            if count:
+                plan.append((piece, first, count, 0, start))
+            start += count
+    (joined,) = move(pieces, (start,), plan, after)
     along_x, along_y = dp_swap(joined, 1), dp_swap(joined, 2)
     after = yield joined
-    yield joined, along_x, along_y, dp_swap(along_y[:cut], 1), dp_swap(along_x[cut:], 2)
+    share = Z_SIZE * half
+    first, second = move(
+        (along_y, along_x),
+        (start - share, share),
+        ((0, 0, start - share, 0, 0), (1, start - share, share, 1, 0)),
+        after,
+    )
+    after = yield first
+    yield joined, along_x, along_y, dp_swap(first, 1), dp_swap(second, 2)
 
 
 def block_home(index, block, outer, inner):
@@ -862,15 +992,12 @@
 
 
 def unpack_widen_kernel(index_ref, *refs):
-    refs, (out_ref, extra_ref) = refs[:-2], refs[-2:]
+    refs, out_ref = refs[:-1], refs[-1]
     width = out_ref.shape[1] // 2
     for tensor, bits in ((0, (1, 2)), (1, (2, 1))):
         for block, rows, values in relative_blocks(refs, tensor):
             start = pl.multiple_of(block_home(index_ref[0], block, *bits) * rows, rows)
             out_ref[pl.ds(start, rows), tensor * width : (tensor + 1) * width] = values.astype(F32)
-    first, count = refs[4].shape[0], extra_ref.shape[0] // 4
-    for place, ref in enumerate(refs[:4]):
-        extra_ref[place * count : (place + 1) * count, :] = ref[first : first + count, :]
 
 
 def unpack_mixer_kernel(index_ref, *refs):
@@ -1012,21 +1139,30 @@
             ((captions, all_pairs), F32),
             ((captions, all_pairs), F32),
             ((captions, 128), F32),
-            ((devices, 1, all_pairs), F32),
+            ((1, all_pairs), F32),
             ((8, 128), F32),
         ),
         index=(place, core),
         small=(matched_picture_ids, sharpening_log),
     )
-    col_parts = lax.all_to_all(col_sum, "dp", 0, 0, tiled=True)
+    after = (unit,)
     for step in steps[-2::-1]:
-        shape = (len(sums_parts) * sums_parts[0].shape[0], hidden)
-        (joined_sums,) = call(stack_kernel, sums_parts, ((shape, BF16),), after=(unit,))
-        sums_parts = dp_parts(joined_sums, step)
+        rows = sums_parts[0].shape[0]
+        (joined_sums,) = move(
+            sums_parts,
+            (4 * rows,),
+            [(place, 0, rows, 0, place * rows) for place in range(4)],
+            after,
+        )
+        sums_parts, after = dp_parts(joined_sums, step), (joined_sums,)
+    col_parts = dp_parts(col_sum, steps[0])
+    for step in steps[1:]:
+        (col_sum,) = call(sum_kernel, col_parts, ((col_sum.shape, F32),), after=after)
+        col_parts = dp_parts(col_sum, step)
     grad_caption, grad_caption_low, grad_pre, part, loss_stat = call(
         loss_grad_kernel,
         (
-            col_parts,
+            *col_parts,
             logits,
             powers,
             row_sum,
@@ -1044,7 +1180,6 @@
             ((8, model_width), F32),
         ),
         outside=(narrowing_matrix, slope, widening_matrix),
-        after=(joined_sums,),
         small=(matched_picture_ids, sharpening_log),
     )
 
@@ -1055,17 +1190,6 @@
         dealt,
         scratch=(pltpu.VMEM(square, BF16),) * 2,
         index=(place,),
-    )
-    half = captions // 2
-    mine = lax.dynamic_slice_in_dim(grad_caption_low, core * half, half, 0)
-    mine = dp_gather(mine, steps[:1:-1], [part] * len(steps))
-    widen_sum = scatter_steps(widen_dealt, place, mine)
-    next(widen_sum)
-    (all_sums,) = call(
-        stack_kernel,
-        sums_parts,
-        (((all_pairs, hidden), BF16),),
-        after=(widen_dealt[0],),
     )
     grad_residual, grad_branch1, flat, part, mixer_stat = call(
         mixer_back_kernel,
@@ -1086,20 +1210,26 @@
             ((8, model_width), F32),
         ),
         outside=(qkv, soft, mixer_triple_matrix),
-        after=(all_sums,),
+        after=(widen_dealt[0],),
     )
     other = mp_other(part)
+    extra = []
+    widen_sum = scatter_steps(widen_dealt, place, extra)
+    next(widen_sum)
+    last = widen_sum.send((part, *sums_parts))
     mixer_dealt = call(
         mixer_grad_kernel,
         (normed, flat, mixed, grad_branch1),
         dealt,
         scratch=(pltpu.VMEM(square, BF16),) * 2,
         index=(place,),
+        after=(last,),
     )
     mixer_sum = scatter_steps(mixer_dealt, place)
     next(mixer_sum)
-    folded = widen_sum.send((mixer_dealt[0],))
-    grad_input, pack = call(
+    last = widen_sum.send((mixer_dealt[0],))
+    extra_rows = captions // 2 + 16
+    grad_input, mine = call(
         entry_grad_kernel,
         (
             part,
@@ -1109,56 +1239,73 @@
             grad_residual,
             loss_stat,
             mixer_stat,
+            grad_caption_low,
         ),
-        ((full, F32), ((16, model_width), F32)),
-        after=(folded,),
-    )
-    cut = widen_sum.send((pack,))
-    fold = mixer_sum.send((cut,))
-    added = widen_sum.send((fold,))
-    cut = mixer_sum.send((added,))
-    joined = widen_sum.send((cut,))
-    added = mixer_sum.send((joined,))
+        ((full, F32), ((extra_rows, model_width), BF16)),
+        scratch=(pltpu.VMEM((16, model_width), F32),),
+        index=(core,),
+        after=(last,),
+    )
+    extra.append(dp_gather(mine, steps[:1:-1], [mine] * len(steps)))
+    last = mixer_sum.send((mine,))
+    last = widen_sum.send((last,))
+    last = mixer_sum.send((last,))
+    last = widen_sum.send((last,))
+    last = mixer_sum.send((last,))
+    last = widen_sum.send((last,))
+    last = mixer_sum.send((last,))
     widen_pieces = widen_sum.send(())
-    joined = mixer_sum.send((added,))
-    grad_w_up, near_grads = call(
+    near_grads, *results = call(
+        functools.partial(collect_kernel, 1.0 / (2.0 * all_pairs), extra_rows),
+        (*widen_pieces, loss_stat),
+        (
+            ((all_pairs // 2, model_width), BF16),
+            ((1,), F32),
+            ((2, local_width), F32),
+            ((model_width,), F32),
+            ((hidden,), F32),
+        )
+        + (((model_width,), F32),) * 5
+        + (((1,), F32),),
+        after=(last,),
+    )
+    error, grad_pair, grad_b_out, grad_b_up, grad_b_down = results[:5]
+    (grad_w_up,) = call(
         unpack_widen_kernel,
         widen_pieces,
-        ((widening_matrix.shape, F32), ((all_pairs // 2, model_width), BF16)),
+        ((widening_matrix.shape, F32),),
         index=(place,),
-        after=(joined,),
+        after=(near_grads,),
+    )
+    last = mixer_sum.send((grad_w_up,))
+    (grad_w_down,) = call(
+        functools.partial(narrow_grad_kernel, captions // 2),
+        (*sums_parts, near_grads, mp_other(near_grads)),
+        ((narrowing_matrix.shape, F32),),
+        scratch=(pltpu.VMEM((all_pairs, model_width), BF16),),
+        index=(core,),
+        after=(last,),
     )
     grad_qkv, grad_w_out = call(
         unpack_mixer_kernel,
         mixer_sum.send(()),
         ((mixer_triple_matrix.shape, F32), (mixer_result_matrix.shape, F32)),
         index=(place,),
-    )
-    (grad_w_down,) = call(
-        functools.partial(narrow_grad_kernel, half),
-        (all_sums, near_grads, mp_other(near_grads)),
-        ((narrowing_matrix.shape, F32),),
-        scratch=(pltpu.VMEM((all_pairs, model_width), BF16),),
-        index=(core,),
-    )
-    stats = dp_sum(pack)
-    training_error = (stats[3, 1:2] + loss_stat[3, 2:3]) / (2.0 * all_pairs)
+        after=(grad_w_down,),
+        limit=56,
+    )
     return (
-        training_error,
+        error,
         grad_input,
         grad_qkv,
-        stats[11].reshape(2, local_width),
+        grad_pair,
         grad_w_out,
-        stats[8],
+        grad_b_out,
         grad_w_up,
-        stats[0:2].reshape(hidden),
+        grad_b_up,
         grad_w_down,
-        stats[2],
-        stats[4],
-        stats[5],
-        stats[9],
-        stats[10],
-        stats[3, 0:1],
+        grad_b_down,
+        *results[5:],
     )
 
 

time: 294 us -> 252 us (0.86)
  the two profiles are of different devices: /device:TPU:0 before, /device:TPU:16 now
where the time goes in v1:
time: 252 us; the launch traced here: 255 us
  Pallas kernels  125 us (50%)
  starting transfers between devices  63 us (25%)
  waiting for transfers between devices  56.8 us (23%)
  local copies, waits for them, and re-layouts  7.63 us (3%)
    pallas_call x26, Pallas kernels, call(): pl.pallas_call(body, out_shape=[jax.ShapeDtypeStruct(shape, kind) for sha...  83.1 us
    ppermute x46, starting transfers between devices, dp_swap(): lax.ppermute(values, 'dp', [(index, index ^ mask) for index in range(size)])  62.2 us
    ppermute x46, waiting for transfers between devices, dp_swap(): lax.ppermute(values, 'dp', [(index, index ^ mask) for index in range(size)])  56.2 us
    pallas_call x1, Pallas kernels, image_tower(): pl.pallas_call(image_kernel, out_shape=jax.ShapeDtypeStruct((images, widt...  42.3 us
    unnamed x80, local copies, waits for them, and re-layouts  7.63 us
  transfers between devices with their start and end apart: 52, of which 19 were waited for; matrix products, arithmetic and copies ran while one was open for 0% of the time, Pallas kernels for 30%

profile of v1, /device:TPU:16, one launch (start us, length us, event | category | flops | bytes accessed | tf_op | source)
XLA Modules:
  0.0 254.8 jit_solution(14290310071375822182)
XLA Ops:
  0.7 42.3 %shard_map.334.refs_7_.refs_0_ = bf16[16,768]{1,0:T(8,128)(2,1)} custom-call(s32[16]{0:T(128)} %flag_ref.1, bf16[145,16,768]{2,1,0:T(8,128)(2,1)} %bitcast.3, f32[2,768]{1,0:T(2,128)} %gain_ref.1, bf16[3,768,768]{2,1,0:T(8,128)(2,1)} %triple_hbm.1, bf16[768,768]{1,0:T(8,128)(2,1)} %result_hbm.1, bf16[768,3072]{1,0:T(8,128)(2,1)} %widen_hbm.1, ...), custom_call_target="tpu_custom_call" | custom-call | flops 999999995904 | bytes 999999995904 | tf_op jit(solution)/shard_map/pallas_call | solution.py:296
  43.0 7.0 %collective-permute-start.1 = (bf16[16,768]{1,0:T(8,128)(2,1)}, bf16[16,768]{1,0:T(8,128)(2,1)}, u32[]{:S(2)}, u32[]{:S(2)}) collective-permute-start(bf16[16,768]{1,0:T(8,128)(2,1)} %shard_map.334.refs_7_.refs_0_), channel_id=1, source_target_pairs={{0,8},{2,10},{4,12},{6,14},{8,0},{10,2},{12,4},{14,6},{16,24},{18,... | collective-permute-start | bytes 73736 | tf_op jit(solution)/shard_map/ppermute | solution.py:29
  52.3 4.4 %shard_map.335 = (bf16[512,768]{1,0:T(8,128)(2,1)S(1)}, bf16[3,512,384]{2,1,0:T(8,128)(2,1)S(1)}, f32[4,3,256,128]{3,2,1,0:T(8,128)S(1)}, bf16[512,384]{1,0:T(8,128)(2,1)S(1)}, f32[512,768]{1,0:T(8,128)}) custom-call(bf16[512,768]{1,0:T(8,128)(2,1)S(1)} %copy-done.6, s32[512]{0:T(512)S(1)} %copy-done.20, f32[768]{0:T(1024)S(1)} %copy-done.17, ...), custom_call_target="tpu_custom_call" | custom-call | flops 999999995904 | bytes 999999995904 | tf_op jit(solution)/shard_map/pallas_call | solution.py:844
  62.3 7.2 %collective-permute-start.5 = (bf16[64,768]{1,0:T(8,128)(2,1)}, bf16[64,768]{1,0:T(8,128)(2,1)}, u32[]{:S(2)}, u32[]{:S(2)}) collective-permute-start(bf16[64,768]{1,0:T(8,128)(2,1)} %shard_map.336.refs_10_.refs_0_), channel_id=1, source_target_pairs={{0,4},{2,6},{4,0},{6,2},{8,12},{10,14},{12,8},{14,10},{16,20},{18,... | collective-permute-start | bytes 294920 | tf_op jit(solution)/shard_map/ppermute | solution.py:29
  70.9 6.6 %shard_map.337 = (f32[512,768]{1,0:T(8,128)S(1)}, bf16[512,768]{1,0:T(8,128)(2,1)S(1)}, f32[512,1536]{1,0:T(8,128)S(1)}, bf16[32,1536]{1,0:T(8,128)(2,1)}, f32[32,768]{1,0:T(8,128)S(1)}, /*index=5*/f32[32,768]{1,0:T(8,128)S(1)}) custom-call(bf16[512,768]{1,0:T(8,128)(2,1)S(1)} %copy-done.6, f32[512,768]{1,0:T(8,128)} %get-tuple-element.87.refs_4_.refs_1_, ...), custom_call_target="tpu_custom_call" | custom-call | flops 999999995904 | bytes 999999995904 | tf_op jit(solution)/shard_map/pallas_call | solution.py:844
  90.6 3.0 %collective-permute-done.14.refs_3_ = bf16[32,1536]{1,0:T(8,128)(2,1)} collective-permute-done((bf16[32,1536]{1,0:T(8,128)(2,1)}, bf16[32,1536]{1,0:T(8,128)(2,1)}, u32[]{:S(2)}, u32[]{:S(2)}) %collective-permute-start.14) | collective-permute-done | bytes 98336 | tf_op jit(solution)/shard_map/ppermute | solution.py:29
  103.4 5.4 %shard_map.342 = (f32[32,768]{1,0:T(8,128)S(1)}, bf16[32,768]{1,0:T(8,128)(2,1)S(1)}, bf16[512,1536]{1,0:T(8,128)(2,1)S(1)}, f32[512,768]{1,0:T(8,128)}, f32[8,768]{1,0:T(8,128)S(1)}) custom-call(s32[32]{0:T(128)S(1)} %copy-done.22, f32[1]{0:T(128)S(6)} %copy.38.refs_2_.refs_1_, f32[1,512]{1,0:T(1,128)S(1)} %shard_map.341.refs_2_, ...), custom_call_target="tpu_custom_call" | custom-call | flops 999999995904 | bytes 999999995904 | tf_op jit(solution)/shard_map/pallas_call | solution.py:844
  108.9 2.5 shard_map.343
  114.6 10.8 %shard_map.344 = (f32[512,768]{1,0:T(8,128)S(1)}, bf16[512,768]{1,0:T(8,128)(2,1)S(1)}, bf16[3,512,384]{2,1,0:T(8,128)(2,1)S(1)}, f32[512,768]{1,0:T(8,128)}, f32[8,768]{1,0:T(8,128)S(1)}) custom-call(f32[512,768]{1,0:T(8,128)} %get-tuple-element.106.refs_0_, f32[512,768]{1,0:T(8,128)} %collective-permute-done.20.refs_1_, f32[512,768]{1,0:T(8,128)S(1)} %copy-done.29, ...), custom_call_target="tpu_custom_call" | custom-call | flops 999999995904 | bytes 999999995904 | tf_op jit(solution)/shard_map/pallas_call | solution.py:844
  125.5 5.5 %collective-permute-done.18.refs_2_ = bf16[384,768]{1,0:T(8,128)(2,1)} collective-permute-done((bf16[384,768]{1,0:T(8,128)(2,1)}, bf16[384,768]{1,0:T(8,128)(2,1)}, u32[]{:S(2)}, u32[]{:S(2)}) %collective-permute-start.18) | collective-permute-done | bytes 589856 | tf_op jit(solution)/shard_map/ppermute | solution.py:29
  137.0 3.0 %shard_map.346 = (bf16[384,768]{1,0:T(8,128)(2,1)}, bf16[384,768]{1,0:T(8,128)(2,1)S(1)}, bf16[384,768]{1,0:T(8,128)(2,1)}, bf16[384,768]{1,0:T(8,128)(2,1)S(1)}) custom-call(s32[1]{0:T(128)} %bitcast.refs_0_, bf16[512,768]{1,0:T(8,128)(2,1)S(1)} %copy-done.33, bf16[3,512,384]{2,1,0:T(8,128)(2,1)S(1)} %get-tuple-element.117.refs_2_, ...), custom_call_target="tpu_custom_call" | custom-call | flops 999999995904 | bytes 999999995904 | tf_op jit(solution)/shard_map/pallas_call | solution.py:844
  141.7 3.2 %collective-permute-done.24.refs_2_ = bf16[192,768]{1,0:T(8,128)(2,1)} collective-permute-done((bf16[192,768]{1,0:T(8,128)(2,1)}, bf16[192,768]{1,0:T(8,128)(2,1)}, u32[]{:S(2)}, u32[]{:S(2)}) %collective-permute-start.24) | collective-permute-done | bytes 294944 | tf_op jit(solution)/shard_map/ppermute | solution.py:29
  150.9 4.3 %shard_map.348 = (f32[512,768]{1,0:T(8,128)}, bf16[32,768]{1,0:T(8,128)(2,1)S(1)}) custom-call(s32[1]{0:T(128)} %bitcast.2.refs_0_, f32[512,768]{1,0:T(8,128)} %get-tuple-element.111.refs_5_.refs_1_, f32[512,768]{1,0:T(8,128)} %collective-permute-done.29.refs_2_, bf16[512,768]{1,0:T(8,128)(2,1)S(1)} %copy-done.6, f32[768]{0:T(1024)S(1)} %copy-done.18, ...), custom_call_target="tpu_custom_call" | custom-call | flops 999999995904 | bytes 999999995904 | tf_op jit(solution)/shard_map/pallas_call | solution.py:844
  173.8 6.4 %collective-permute-done.33.refs_2_ = bf16[128,768]{1,0:T(8,128)(2,1)} collective-permute-done((bf16[128,768]{1,0:T(8,128)(2,1)}, bf16[128,768]{1,0:T(8,128)(2,1)}, u32[]{:S(2)}, u32[]{:S(2)}) %collective-permute-start.33) | collective-permute-done | bytes 196640 | tf_op jit(solution)/shard_map/ppermute | solution.py:29
  180.1 10.4 %collective-permute-done.34.refs_3_ = bf16[128,768]{1,0:T(8,128)(2,1)} collective-permute-done((bf16[128,768]{1,0:T(8,128)(2,1)}, bf16[128,768]{1,0:T(8,128)(2,1)}, u32[]{:S(2)}, u32[]{:S(2)}) %collective-permute-start.34) | collective-permute-done | bytes 196640 | tf_op jit(solution)/shard_map/ppermute | solution.py:29
  201.1 9.4 %collective-permute-done.37.refs_1_.refs_2_ = bf16[512,768]{1,0:T(8,128)(2,1)} collective-permute-done((bf16[512,768]{1,0:T(8,128)(2,1)}, bf16[512,768]{1,0:T(8,128)(2,1)}, u32[]{:S(2)}, u32[]{:S(2)}) %collective-permute-start.37) | collective-permute-done | bytes 786464 | tf_op jit(solution)/shard_map/ppermute | solution.py:29
  210.5 2.3 shard_map.354
  218.8 5.9 %collective-permute-done.43.refs_4_.refs_5_ = bf16[192,768]{1,0:T(8,128)(2,1)} collective-permute-done((bf16[192,768]{1,0:T(8,128)(2,1)}, bf16[192,768]{1,0:T(8,128)(2,1)}, u32[]{:S(2)}, u32[]{:S(2)}) %collective-permute-start.43) | collective-permute-done | bytes 294944 | tf_op jit(solution)/shard_map/ppermute | solution.py:29
  224.7 2.5 collective-permute-done.42.refs_3_.refs_4_
  227.2 2.7 %shard_map.356 = (bf16[256,768]{1,0:T(8,128)(2,1)}, f32[1]{0:T(128)}, f32[2,384]{1,0:T(2,128)}, f32[768]{0:T(1024)}, f32[1536]{0:T(1024)}, /*index=5*/f32[768]{0...) custom-call(bf16[512,768]{1,0:T(8,128)(2,1)} %shard_map.352.refs_4_.refs_0_.refs_1_, ...), custom_call_target="tpu_custom_call" | custom-call | flops 999999995904 | bytes 999999995904 | tf_op jit(solution)/shard_map/pallas_call | solution.py:844
  230.0 4.6 %shard_map.357.refs_2_ = f32[768,1536]{1,0:T(8,128)} custom-call(s32[1]{0:T(128)} %bitcast.refs_0_, bf16[512,768]{1,0:T(8,128)(2,1)} %shard_map.352.refs_4_.refs_0_.refs_1_, bf16[512,768]{1,0:T(8,128)(2,1)} %collective-permute-done.37.refs_1_.refs_2_, bf16[512,768]{1,0:T(8,128)(2,1)} %collective-permute-done.38.refs_0_.refs_2_.refs_3_, ...), custom_call_target="tpu_custom_call" | custom-call | flops 999999995904 | bytes 999999995904 | tf_op jit(solution)/shard_map/pallas_call | solution.py:844
  235.9 2.3 copy-done.23
  241.9 6.4 %shard_map.359.refs_6_ = f32[1536,768]{1,0:T(8,128)} custom-call(s32[1]{0:T(128)} %bitcast.2.refs_0_, bf16[128,1536]{1,0:T(8,128)(2,1)} %shard_map.340.refs_4_.refs_6_.refs_1_, bf16[128,1536]{1,0:T(8,128)(2,1)} %collective-permute-done.21.refs_7_.refs_2_, bf16[128,1536]{1,0:T(8,128)(2,1)} %collective-permute-done.22.refs_8_.refs_3_, ...), custom_call_target="tpu_custom_call" | custom-call | flops 999999995904 | bytes 999999995904 | tf_op jit(solution)/shard_map/pallas_call | solution.py:844
  250.2 4.6 %shard_map.360 = (f32[3,768,384]{2,1,0:T(8,128)}, f32[384,768]{1,0:T(8,128)}) custom-call(s32[1]{0:T(128)} %bitcast.refs_0_, bf16[384,768]{1,0:T(8,128)(2,1)} %shard_map.355.refs_6_.refs_1_, bf16[384,768]{1,0:T(8,128)(2,1)} %collective-permute-done.47.refs_1_.refs_2_, bf16[384,768]{1,0:T(8,128)(2,1)} %collective-permute-done.48.refs_0_.refs_3_, ...), custom_call_target="tpu_custom_call" | custom-call | flops 999999995904 | bytes 999999995904 | tf_op jit(solution)/shard_map/pallas_call | solution.py:844
  (188 shorter events, 90.4 us)
Async XLA Ops:
  43.0 16.8 %collective-permute-start.1 = (bf16[16,768]{1,0:T(8,128)(2,1)}, bf16[16,768]{1,0:T(8,128)(2,1)}, u32[]{:S(2)}, u32[]{:S(2)}) collective-permute-start(bf16[16,768]{1,0:T(8,128)(2,1)} %shard_map.334.refs_7_.refs_0_), channel_id=1, source_target_pairs={{0,8},{2,10},{4,12},{6,14},{8,0},{10,2},{12,4},{14,6},{16,24},{18,... | collective-permute-start | bytes 73736 | tf_op jit(solution)/shard_map/ppermute | solution.py:29
  61.4 16.2 %collective-permute-start.4 = (bf16[64,768]{1,0:T(8,128)(2,1)}, bf16[64,768]{1,0:T(8,128)(2,1)}, u32[]{:S(2)}, u32[]{:S(2)}) collective-permute-start(bf16[64,768]{1,0:T(8,128)(2,1)} %shard_map.336.refs_10_.refs_0_), channel_id=1, source_target_pairs={{0,2},{2,0},{4,6},{6,4},{8,10},{10,8},{12,14},{14,12},{16,18},{18,... | collective-permute-start | bytes 294920 | tf_op jit(solution)/shard_map/ppermute | solution.py:29
  62.3 15.3 %collective-permute-start.5 = (bf16[64,768]{1,0:T(8,128)(2,1)}, bf16[64,768]{1,0:T(8,128)(2,1)}, u32[]{:S(2)}, u32[]{:S(2)}) collective-permute-start(bf16[64,768]{1,0:T(8,128)(2,1)} %shard_map.336.refs_10_.refs_0_), channel_id=1, source_target_pairs={{0,4},{2,6},{4,0},{6,2},{8,12},{10,14},{12,8},{14,10},{16,20},{18,... | collective-permute-start | bytes 294920 | tf_op jit(solution)/shard_map/ppermute | solution.py:29
  99.8 25.6 %collective-permute-start.21 = (bf16[128,1536]{1,0:T(8,128)(2,1)}, bf16[128,1536]{1,0:T(8,128)(2,1)}, u32[]{:S(2)}, u32[]{:S(2)}) collective-permute-start(bf16[128,1536]{1,0:T(8,128)(2,1)} %shard_map.340.refs_4_.refs_6_.refs_1_), channel_id=1, source_target_pairs={{0,2},{2,0},{4,6},{6,4},{8,10},{10,8},{12,14},{14,12},{16,18},{18,... | collective-permute-start | bytes 1179656 | tf_op jit(solution)/shard_map/ppermute | solution.py:29
  100.4 25.1 %collective-permute-start.22 = (bf16[128,1536]{1,0:T(8,128)(2,1)}, bf16[128,1536]{1,0:T(8,128)(2,1)}, u32[]{:S(2)}, u32[]{:S(2)}) collective-permute-start(bf16[128,1536]{1,0:T(8,128)(2,1)} %shard_map.340.refs_4_.refs_6_.refs_1_), channel_id=1, source_target_pairs={{0,4},{2,6},{4,0},{6,2},{8,12},{10,14},{12,8},{14,10},{16,20},{18,... | collective-permute-start | bytes 1179656 | tf_op jit(solution)/shard_map/ppermute | solution.py:29
  101.9 23.7 %collective-permute-start.23 = (bf16[128,1536]{1,0:T(8,128)(2,1)}, bf16[128,1536]{1,0:T(8,128)(2,1)}, u32[]{:S(2)}, u32[]{:S(2)}) collective-permute-start(bf16[128,1536]{1,0:T(8,128)(2,1)} %shard_map.340.refs_4_.refs_6_.refs_1_), channel_id=1, source_target_pairs={{0,6},{2,4},{4,2},{6,0},{8,14},{10,12},{12,10},{14,8},{16,22},{18,... | collective-permute-start | bytes 1179656 | tf_op jit(solution)/shard_map/ppermute | solution.py:29
  111.4 19.6 %collective-permute-start.18 = (bf16[384,768]{1,0:T(8,128)(2,1)}, bf16[384,768]{1,0:T(8,128)(2,1)}, u32[]{:S(2)}, u32[]{:S(2)}) collective-permute-start(bf16[384,768]{1,0:T(8,128)(2,1)} %get-tuple-element.103.refs_10_), channel_id=1, source_target_pairs={{0,2},{2,0},{4,6},{6,4},{8,10},{10,8},{12,14},{14,12},{16,18},{18,... | collective-permute-start | bytes 1769480 | tf_op jit(solution)/shard_map/ppermute | solution.py:29
  112.6 19.9 %collective-permute-start.19 = (bf16[384,768]{1,0:T(8,128)(2,1)}, bf16[384,768]{1,0:T(8,128)(2,1)}, u32[]{:S(2)}, u32[]{:S(2)}) collective-permute-start(bf16[384,768]{1,0:T(8,128)(2,1)} %get-tuple-element.105), channel_id=1, source_target_pairs={{0,4},{2,6},{4,0},{6,2},{8,12},{10,14},{12,8},{14,10},{16,20},{18,... | collective-permute-start | bytes 1769480 | tf_op jit(solution)/shard_map/ppermute | solution.py:29
  125.4 23.7 %collective-permute-start.29 = (f32[512,768]{1,0:T(8,128)}, f32[512,768]{1,0:T(8,128)}, u32[]{:S(2)}, u32[]{:S(2)}) collective-permute-start(f32[512,768]{1,0:T(8,128)} %get-tuple-element.111.refs_5_.refs_1_), channel_id=1, source_target_pairs={{0,1},{1,0},{2,3},{3,2},{4,5},{5,4},{6,7},{7,6},{8,9},{9,8},{10,11... | collective-permute-start | bytes 4718600 | tf_op jit(solution)/shard_map/ppermute | solution.py:24
  140.0 16.6 %collective-permute-start.30 = (bf16[384,768]{1,0:T(8,128)(2,1)}, bf16[384,768]{1,0:T(8,128)(2,1)}, u32[]{:S(2)}, u32[]{:S(2)}) collective-permute-start(bf16[384,768]{1,0:T(8,128)(2,1)} %get-tuple-element.120.refs_5_), channel_id=1, source_target_pairs={{0,2},{2,0},{4,6},{6,4},{8,10},{10,8},{12,14},{14,12},{16,18},{18,... | collective-permute-start | bytes 1769480 | tf_op jit(solution)/shard_map/ppermute | solution.py:29
  140.2 16.4 %collective-permute-start.31 = (bf16[384,768]{1,0:T(8,128)(2,1)}, bf16[384,768]{1,0:T(8,128)(2,1)}, u32[]{:S(2)}, u32[]{:S(2)}) collective-permute-start(bf16[384,768]{1,0:T(8,128)(2,1)} %get-tuple-element.132), channel_id=1, source_target_pairs={{0,4},{2,6},{4,0},{6,2},{8,12},{10,14},{12,8},{14,10},{16,20},{18,... | collective-permute-start | bytes 1769480 | tf_op jit(solution)/shard_map/ppermute | solution.py:29
  164.1 16.0 %collective-permute-start.33 = (bf16[128,768]{1,0:T(8,128)(2,1)}, bf16[128,768]{1,0:T(8,128)(2,1)}, u32[]{:S(2)}, u32[]{:S(2)}) collective-permute-start(bf16[128,768]{1,0:T(8,128)(2,1)} %shard_map.350.refs_5_.refs_0_), channel_id=1, source_target_pairs={{0,16},{2,18},{4,20},{6,22},{8,24},{10,26},{12,28},{14,30},{16,0},... | collective-permute-start | bytes 589832 | tf_op jit(solution)/shard_map/ppermute | solution.py:29
  165.4 25.1 %collective-permute-start.34 = (bf16[128,768]{1,0:T(8,128)(2,1)}, bf16[128,768]{1,0:T(8,128)(2,1)}, u32[]{:S(2)}, u32[]{:S(2)}) collective-permute-start(bf16[128,768]{1,0:T(8,128)(2,1)} %shard_map.350.refs_5_.refs_0_), channel_id=1, source_target_pairs={{0,24},{2,26},{4,28},{6,30},{8,16},{10,18},{12,20},{14,22},{16,8},... | collective-permute-start | bytes 589832 | tf_op jit(solution)/shard_map/ppermute | solution.py:29
  170.3 24.3 %collective-permute-start.39 = (bf16[96,768]{1,0:T(8,128)(2,1)}, bf16[96,768]{1,0:T(8,128)(2,1)}, u32[]{:S(2)}, u32[]{:S(2)}) collective-permute-start(bf16[96,768]{1,0:T(8,128)(2,1)} %get-tuple-element.138), channel_id=1, source_target_pairs={{0,8},{2,10},{4,12},{6,14},{8,0},{10,2},{12,4},{14,6},{16,24},{18,... | collective-permute-start | bytes 442376 | tf_op jit(solution)/shard_map/ppermute | solution.py:29
  171.4 23.1 %collective-permute-start.40 = (bf16[96,768]{1,0:T(8,128)(2,1)}, bf16[96,768]{1,0:T(8,128)(2,1)}, u32[]{:S(2)}, u32[]{:S(2)}) collective-permute-start(bf16[96,768]{1,0:T(8,128)(2,1)} %get-tuple-element.139), channel_id=1, source_target_pairs={{0,16},{2,18},{4,20},{6,22},{8,24},{10,26},{12,28},{14,30},{16,0},... | collective-permute-start | bytes 442376 | tf_op jit(solution)/shard_map/ppermute | solution.py:29
  172.0 23.8 %collective-permute-start.41 = (bf16[96,768]{1,0:T(8,128)(2,1)}, bf16[96,768]{1,0:T(8,128)(2,1)}, u32[]{:S(2)}, u32[]{:S(2)}) collective-permute-start(bf16[96,768]{1,0:T(8,128)(2,1)} %get-tuple-element.140), channel_id=1, source_target_pairs={{0,24},{2,26},{4,28},{6,30},{8,16},{10,18},{12,20},{14,22},{16,8},... | collective-permute-start | bytes 442376 | tf_op jit(solution)/shard_map/ppermute | solution.py:29
  192.7 17.8 %collective-permute-start.37 = (bf16[512,768]{1,0:T(8,128)(2,1)}, bf16[512,768]{1,0:T(8,128)(2,1)}, u32[]{:S(2)}, u32[]{:S(2)}) collective-permute-start(bf16[512,768]{1,0:T(8,128)(2,1)} %shard_map.352.refs_4_.refs_0_.refs_1_), channel_id=1, source_target_pairs={{0,2},{2,0},{4,6},{6,4},{8,10},{10,8},{12,14},{14,12},{16,18},{18,... | collective-permute-start | bytes 2359304 | tf_op jit(solution)/shard_map/ppermute | solution.py:29
  193.7 16.7 %collective-permute-start.38 = (bf16[512,768]{1,0:T(8,128)(2,1)}, bf16[512,768]{1,0:T(8,128)(2,1)}, u32[]{:S(2)}, u32[]{:S(2)}) collective-permute-start(bf16[512,768]{1,0:T(8,128)(2,1)} %shard_map.352.refs_4_.refs_0_.refs_1_), channel_id=1, source_target_pairs={{0,4},{2,6},{4,0},{6,2},{8,12},{10,14},{12,8},{14,10},{16,20},{18,... | collective-permute-start | bytes 2359304 | tf_op jit(solution)/shard_map/ppermute | solution.py:29
  197.6 17.7 %collective-permute-start.44 = (bf16[96,768]{1,0:T(8,128)(2,1)}, bf16[96,768]{1,0:T(8,128)(2,1)}, u32[]{:S(2)}, u32[]{:S(2)}) collective-permute-start(bf16[96,768]{1,0:T(8,128)(2,1)} %shard_map.353.refs_2_.refs_0_), channel_id=1, source_target_pairs={{0,8},{2,10},{4,12},{6,14},{8,0},{10,2},{12,4},{14,6},{16,24},{18,... | collective-permute-start | bytes 442376 | tf_op jit(solution)/shard_map/ppermute | solution.py:29
  197.6 17.7 %collective-permute-start.45 = (bf16[96,768]{1,0:T(8,128)(2,1)}, bf16[96,768]{1,0:T(8,128)(2,1)}, u32[]{:S(2)}, u32[]{:S(2)}) collective-permute-start(bf16[96,768]{1,0:T(8,128)(2,1)} %shard_map.353.refs_2_.refs_0_), channel_id=1, source_target_pairs={{0,16},{2,18},{4,20},{6,22},{8,24},{10,26},{12,28},{14,30},{16,0},... | collective-permute-start | bytes 442376 | tf_op jit(solution)/shard_map/ppermute | solution.py:29
  199.0 16.3 %collective-permute-start.46 = (bf16[96,768]{1,0:T(8,128)(2,1)}, bf16[96,768]{1,0:T(8,128)(2,1)}, u32[]{:S(2)}, u32[]{:S(2)}) collective-permute-start(bf16[96,768]{1,0:T(8,128)(2,1)} %shard_map.353.refs_2_.refs_0_), channel_id=1, source_target_pairs={{0,24},{2,26},{4,28},{6,30},{8,16},{10,18},{12,20},{14,22},{16,8},... | collective-permute-start | bytes 442376 | tf_op jit(solution)/shard_map/ppermute | solution.py:29
  212.7 14.5 %collective-permute-start.42 = (bf16[320,768]{1,0:T(8,128)(2,1)}, bf16[320,768]{1,0:T(8,128)(2,1)}, u32[]{:S(2)}, u32[]{:S(2)}) collective-permute-start(bf16[320,768]{1,0:T(8,128)(2,1)} %get-tuple-element.141.refs_4_), channel_id=1, source_target_pairs={{0,2},{2,0},{4,6},{6,4},{8,10},{10,8},{12,14},{14,12},{16,18},{18,... | collective-permute-start | bytes 1474568 | tf_op jit(solution)/shard_map/ppermute | solution.py:29
  217.3 18.6 %collective-permute-start.47 = (bf16[384,768]{1,0:T(8,128)(2,1)}, bf16[384,768]{1,0:T(8,128)(2,1)}, u32[]{:S(2)}, u32[]{:S(2)}) collective-permute-start(bf16[384,768]{1,0:T(8,128)(2,1)} %shard_map.355.refs_6_.refs_1_), channel_id=1, source_target_pairs={{0,2},{2,0},{4,6},{6,4},{8,10},{10,8},{12,14},{14,12},{16,18},{18,... | collective-permute-start | bytes 1769480 | tf_op jit(solution)/shard_map/ppermute | solution.py:29
  217.7 18.2 %collective-permute-start.48 = (bf16[384,768]{1,0:T(8,128)(2,1)}, bf16[384,768]{1,0:T(8,128)(2,1)}, u32[]{:S(2)}, u32[]{:S(2)}) collective-permute-start(bf16[384,768]{1,0:T(8,128)(2,1)} %shard_map.355.refs_6_.refs_1_), channel_id=1, source_target_pairs={{0,4},{2,6},{4,0},{6,2},{8,12},{10,14},{12,8},{14,10},{16,20},{18,... | collective-permute-start | bytes 1769480 | tf_op jit(solution)/shard_map/ppermute | solution.py:29
  (68 other events, 797.5 us)

commit v2 on v1

--- a/solution.py
+++ b/solution.py
@@ -103,6 +103,7 @@
     out_ref,
     wide,
     packed,
+    mixed,
     queries,
     keys,
     values,
@@ -113,7 +114,10 @@
     resid_groups,
     hidden_groups,
     pooled,
+    ready,
     starts,
+    high_starts,
+    low_starts,
     sems,
 ):
     _, images, width = token_ref.shape
@@ -129,11 +133,22 @@
             wide[place, rows, :] = token_ref[position, :, lanes].astype(F32)
         return carry
 
-    def begin(image, start):
+    def begin(image, carry):
+        start, highs = carry
         starts[image] = start
-        return start + jnp.where(flag_ref[image] == 1, HIGH_ROWS, LOW_ROWS)
-
-    total = lax.fori_loop(0, images, begin, jnp.int32(0))
+        high = flag_ref[image] == 1
+
+        @pl.when(high)
+        def _():
+            high_starts[highs] = start
+
+        @pl.when(jnp.logical_not(high))
+        def _():
+            low_starts[image - highs] = start
+
+        return start + jnp.where(high, HIGH_ROWS, LOW_ROWS), highs + jnp.where(high, 1, 0)
+
+    total, highs = lax.fori_loop(0, images, begin, (jnp.int32(0), jnp.int32(0)))
     lax.fori_loop(0, LOW_ROWS, spread, 0, unroll=4)
 
     @pl.when(total > images * LOW_ROWS)
@@ -173,47 +188,63 @@
 
     copies[0].wait()
 
+    def prepare(tile):
+        rows = pl.ds(pl.multiple_of(tile * TILE, TILE), TILE)
+        ready[tile % 2] = (
+            standard(packed[rows, :].astype(F32), EPS_UNIT) * gain_ref[0:1, :]
+        ).astype(BF16)
+
     def project(tile, carry):
         rows = pl.ds(pl.multiple_of(tile * TILE, TILE), TILE)
-        normed = (standard(packed[rows, :].astype(F32), EPS_UNIT) * gain_ref[0:1, :]).astype(BF16)
+        normed = ready[tile % 2]
         queries[rows, :] = (dot(normed, triple[0]) * HEAD ** (-0.5)).astype(BF16)
+        prepare(tile + 1)
         keys[rows, :] = dot(normed, triple[1]).astype(BF16)
         values[rows, :] = dot(normed, triple[2]).astype(BF16)
         return carry
 
+    prepare(jnp.int32(0))
     lax.fori_loop(0, tiles, project, 0)
 
-    def attend(start, count, live):
-        rows = pl.ds(start, count)
+    def attend(begins, count, live):
         left = lax.broadcasted_iota(jnp.int32, (count, PAIR), 1) < HEAD
         key_live = lax.broadcasted_iota(jnp.int32, (2 * count, count), 1) < live
-        for pair in range(width // PAIR):
-            lanes = slice(pair * PAIR, (pair + 1) * PAIR)
-            q, k, v = queries[rows, lanes], keys[rows, lanes], values[rows, lanes]
-            one = jnp.ones_like(v)
-            scores = dot_t(two_heads(q, left), k)
+        places = [
+            (pl.ds(pl.multiple_of(start, POOL_ROWS), count), slice(lane, lane + PAIR))
+            for start in begins
+            for lane in range(0, width, PAIR)
+        ]
+        all_scores = [dot_t(two_heads(queries[place], left), keys[place]) for place in places]
+        all_powers = []
+        for scores in all_scores:
             scores = jnp.where(key_live, scores, MASKED_SCORE)
-            powers = jnp.exp(scores - jnp.max(scores, axis=-1, keepdims=True)).astype(BF16)
-            first = dot(powers[:count], jnp.where(left, v, one))
-            second = dot(powers[count:], jnp.where(left, one, v))
+            top = jnp.max(scores, axis=-1, keepdims=True)
+            all_powers.append(jnp.exp(scores - top).astype(BF16))
+        for place, powers in zip(places, all_powers):
+            value = values[place]
+            one = jnp.ones_like(value)
+            first = dot(powers[:count], jnp.where(left, value, one))
+            second = dot(powers[count:], jnp.where(left, one, value))
             sums = pltpu.roll(jnp.where(left, second, first), HEAD, 1)
-            queries[rows, lanes] = (jnp.where(left, first, second) / sums).astype(BF16)
-
-    def mix(image, carry):
-        start = pl.multiple_of(starts[image], POOL_ROWS)
-        high = flag_ref[image] == 1
-
-        @pl.when(high)
-        def _():
-            attend(start, HIGH_ROWS, IMG_TOK)
-
-        @pl.when(jnp.logical_not(high))
-        def _():
-            attend(start, LOW_ROWS, LOW_TOK)
-
-        return carry
-
-    lax.fori_loop(0, images, mix, 0)
+            mixed[place] = (jnp.where(left, first, second) / sums).astype(BF16)
+
+    def attend_all(begins, number, together, count, live):
+        groups = lax.div(number, jnp.int32(together))
+
+        def group(index, carry):
+            attend([begins[index * together + step] for step in range(together)], count, live)
+            return carry
+
+        def rest(index, carry):
+            attend([begins[index]], count, live)
+            return carry
+
+        lax.fori_loop(0, groups, group, 0)
+        if together > 1:
+            lax.fori_loop(groups * together, number, rest, 0)
+
+    attend_all(high_starts, highs, 1, HIGH_ROWS, IMG_TOK)
+    attend_all(low_starts, images - highs, 4, LOW_ROWS, LOW_TOK)
 
     slot = lax.broadcasted_iota(jnp.int32, (1, images), 1)
     first_row = jnp.zeros((1, images), jnp.int32)
@@ -230,7 +261,7 @@
     def group_sum(rows):
         return jnp.sum(rows.reshape(groups, POOL_ROWS // 8, 8, rows.shape[1]), axis=1)
 
-    def perceptron(tile, carry):
+    def resume(tile):
         base = pl.multiple_of(tile * TILE, TILE)
         rows = pl.ds(base, TILE)
         place = base + lax.broadcasted_iota(jnp.int32, (TILE, images), 0)
@@ -239,16 +270,23 @@
             axis=1,
             keepdims=True,
         )
-        residual = (packed[rows, :].astype(F32) + dot(queries[rows, :], result[...])) * alive
+        residual = (packed[rows, :].astype(F32) + dot(mixed[rows, :], result[...])) * alive
         group = pl.ds(pl.multiple_of(tile * groups, groups), groups)
         resid_groups[group] = group_sum(residual)
-        normed = (standard(residual, EPS_UNIT) * gain_ref[1:2, :]).astype(BF16)
+        ready[tile % 2] = (standard(residual, EPS_UNIT) * gain_ref[1:2, :]).astype(BF16)
+
+    def perceptron(tile, carry):
+        group = pl.ds(pl.multiple_of(tile * groups, groups), groups)
+        normed = ready[tile % 2]
         for chunk in range(hidden // width):
+            if chunk == 1:
+                resume(tile + 1)
             lanes = slice(chunk * width, (chunk + 1) * width)
             units = gelu(dot(normed, widen[:, lanes])).astype(BF16)
             hidden_groups[group, :, lanes] = group_sum(units.astype(F32))
         return carry
 
+    resume(jnp.int32(0))
     lax.fori_loop(0, tiles, perceptron, 0)
 
     def pool(image, carry):
@@ -300,12 +338,15 @@
         + [outside] * 4,
         out_specs=inside,
         scratch_shapes=[pltpu.VMEM((width // LANES, IMG_TOK * images, LANES), F32)]
-        + [pltpu.VMEM((rows, width), BF16)] * 4
+        + [pltpu.VMEM((rows, width), BF16)] * 5
         + [pltpu.VMEM(weight.shape, BF16) for weight in (triple, result, widen, narrow)]
         + [
             pltpu.VMEM((groups, 8, width), F32),
             pltpu.VMEM((groups, 8, hidden), F32),
             pltpu.VMEM((images, width + hidden), F32),
+            pltpu.VMEM((2, TILE, width), BF16),
+            pltpu.SMEM((images,), jnp.int32),
+            pltpu.SMEM((images,), jnp.int32),
             pltpu.SMEM((images,), jnp.int32),
             pltpu.SemaphoreType.DMA((4,)),
         ],
@@ -676,23 +717,30 @@
     for copy in copies:
         copy.wait()
     left = pair_masks(BLOCK, PAIR)
-    for block in range(tokens // BLOCK):
-        rows = slice(block * BLOCK, (block + 1) * BLOCK)
-        for pair in range(local_width // PAIR):
-            lanes = slice(pair * PAIR, (pair + 1) * PAIR)
-            soft = soft_all[block, pair]
-            mixed = two_heads(grad_mixed[rows, lanes], left)
-            query, key = qkv[0, rows, lanes], qkv[1, rows, lanes]
-            grad_soft = dot_t(mixed, qkv[2, rows, lanes])
-            flat_ref[2, rows, lanes] = t_dot(soft.astype(BF16), mixed).astype(BF16)
-            scores = (
-                soft * (grad_soft - jnp.sum(grad_soft * soft, axis=-1, keepdims=True))
-            ).astype(BF16)
-            back = jnp.where(left, dot(scores[:BLOCK], key), dot(scores[BLOCK:], key))
-            flat_ref[0, rows, lanes] = (back * HEAD ** (-0.5)).astype(BF16)
-            flat_ref[1, rows, lanes] = (
-                t_dot(scores, two_heads(query, left)) * HEAD ** (-0.5)
-            ).astype(BF16)
+    places = [
+        (block, pair, slice(block * BLOCK, (block + 1) * BLOCK), slice(pair * PAIR, (pair + 1) * PAIR))
+        for block in range(tokens // BLOCK)
+        for pair in range(local_width // PAIR)
+    ]
+    mixed = [two_heads(grad_mixed[rows, lanes], left) for _, _, rows, lanes in places]
+    softs = [soft_all[block, pair] for block, pair, _, _ in places]
+    grads = [
+        dot_t(value, qkv[2, rows, lanes]) for value, (_, _, rows, lanes) in zip(mixed, places)
+    ]
+    scores = [
+        (soft * (grad - jnp.sum(grad * soft, axis=-1, keepdims=True))).astype(BF16)
+        for soft, grad in zip(softs, grads)
+    ]
+    for value, soft, (_, _, rows, lanes) in zip(mixed, softs, places):
+        flat_ref[2, rows, lanes] = t_dot(soft.astype(BF16), value).astype(BF16)
+    for score, (_, _, rows, lanes) in zip(scores, places):
+        key = qkv[1, rows, lanes]
+        back = jnp.where(left, dot(score[:BLOCK], key), dot(score[BLOCK:], key))
+        flat_ref[0, rows, lanes] = (back * HEAD ** (-0.5)).astype(BF16)
+    for score, (_, _, rows, lanes) in zip(scores, places):
+        flat_ref[1, rows, lanes] = (
+            t_dot(score, two_heads(qkv[0, rows, lanes], left)) * HEAD ** (-0.5)
+        ).astype(BF16)
     part_ref[...] = (
         dot_t(flat_ref[0], triple[0])
         + dot_t(flat_ref[1], triple[1])
@@ -1091,6 +1139,7 @@
             (full, F32),
         ),
         after=(image_emb,),
+        limit=60,
     )
     other = mp_other(part)
     near_images = dp_gather(image_emb, steps[:0:-1], [part] * (len(steps) - 1))
@@ -1216,18 +1265,18 @@
     extra = []
     widen_sum = scatter_steps(widen_dealt, place, extra)
     next(widen_sum)
-    last = widen_sum.send((part, *sums_parts))
     mixer_dealt = call(
         mixer_grad_kernel,
         (normed, flat, mixed, grad_branch1),
         dealt,
         scratch=(pltpu.VMEM(square, BF16),) * 2,
         index=(place,),
-        after=(last,),
+        after=sums_parts,
     )
     mixer_sum = scatter_steps(mixer_dealt, place)
     next(mixer_sum)
     last = widen_sum.send((mixer_dealt[0],))
+    last = widen_sum.send((last,))
     extra_rows = captions // 2 + 16
     grad_input, mine = call(
         entry_grad_kernel,
@@ -1276,6 +1325,7 @@
         ((widening_matrix.shape, F32),),
         index=(place,),
         after=(near_grads,),
+        limit=56,
     )
     last = mixer_sum.send((grad_w_up,))
     (grad_w_down,) = call(

time: 252 us -> 245 us (0.972)
  local copies, waits for them, and re-layouts: 7.63 us -> 3.89 us
  Pallas kernels: 125 us -> 122 us
    unnamed x80 -> x60, local copies, waits for them, and re-layouts: 7.63 us -> 3.89 us
  transfers between devices with their start and end apart: 52 -> 52, of which waited for: 19 -> 18; matrix products, arithmetic and copies ran while one was open for 0% -> 0% of each run, Pallas kernels for 30% -> 29%
where the time goes in v2:
time: 245 us; the launch traced here: 250 us
  Pallas kernels  122 us (50%)
  starting transfers between devices  64.9 us (26%)
  waiting for transfers between devices  57.2 us (23%)
  local copies, waits for them, and re-layouts  3.89 us (2%)
    pallas_call x26, Pallas kernels, call(): pl.pallas_call(body, out_shape=[jax.ShapeDtypeStruct(shape, kind) for sha...  81 us
    ppermute x46, starting transfers between devices, dp_swap(): lax.ppermute(values, 'dp', [(index, index ^ mask) for index in range(size)])  64.1 us
    ppermute x46, waiting for transfers between devices, dp_swap(): lax.ppermute(values, 'dp', [(index, index ^ mask) for index in range(size)])  56.6 us
    pallas_call x1, Pallas kernels, image_tower(): pl.pallas_call(image_kernel, out_shape=jax.ShapeDtypeStruct((images, widt...  40.8 us
  transfers between devices with their start and end apart: 52, of which 18 were waited for; matrix products, arithmetic and copies ran while one was open for 0% of the time, Pallas kernels for 29%

profile of v2, /device:TPU:16, one launch (start us, length us, event | category | flops | bytes accessed | tf_op | source)
XLA Modules:
  0.0 249.7 jit_solution(9917334798311328428)
XLA Ops:
  0.6 40.8 %shard_map.334.refs_7_.refs_0_ = bf16[16,768]{1,0:T(8,128)(2,1)} custom-call(s32[16]{0:T(128)} %flag_ref.1, bf16[145,16,768]{2,1,0:T(8,128)(2,1)} %bitcast.3, f32[2,768]{1,0:T(2,128)} %gain_ref.1, bf16[3,768,768]{2,1,0:T(8,128)(2,1)} %triple_hbm.1, bf16[768,768]{1,0:T(8,128)(2,1)} %result_hbm.1, bf16[768,3072]{1,0:T(8,128)(2,1)} %widen_hbm.1, ...), custom_call_target="tpu_custom_call" | custom-call | flops 999999995904 | bytes 999999995904 | tf_op jit(solution)/shard_map/pallas_call | solution.py:334
  45.0 6.6 %shard_map.335 = (bf16[512,768]{1,0:T(8,128)(2,1)}, bf16[3,512,384]{2,1,0:T(8,128)(2,1)}, f32[4,3,256,128]{3,2,1,0:T(8,128)}, bf16[512,384]{1,0:T(8,128)(2,1)}, f32[512,768]{1,0:T(8,128)}) custom-call(bf16[512,768]{1,0:T(8,128)(2,1)} %refs_3_.5, s32[512]{0:T(512)} %refs_4_.6, f32[768]{0:T(1024)} %refs_4_.7, f32[768]{0:T(1024)} %refs_3_.3, ...), custom_call_target="tpu_custom_call" | custom-call | flops 999999995904 | bytes 999999995904 | tf_op jit(solution)/shard_map/pallas_call | solution.py:892
  55.5 10.4 %collective-permute-start.5 = (bf16[64,768]{1,0:T(8,128)(2,1)}, bf16[64,768]{1,0:T(8,128)(2,1)}, u32[]{:S(2)}, u32[]{:S(2)}) collective-permute-start(bf16[64,768]{1,0:T(8,128)(2,1)} %shard_map.336.refs_10_.refs_0_), channel_id=1, source_target_pairs={{0,4},{2,6},{4,0},{6,2},{8,12},{10,14},{12,8},{14,10},{16,20},{18,... | collective-permute-start | bytes 294920 | tf_op jit(solution)/shard_map/ppermute | solution.py:29
  67.5 6.2 %shard_map.337 = (f32[512,768]{1,0:T(8,128)S(1)}, bf16[512,768]{1,0:T(8,128)(2,1)S(1)}, f32[512,1536]{1,0:T(8,128)S(1)}, bf16[32,1536]{1,0:T(8,128)(2,1)}, f32[32,768]{1,0:T(8,128)S(1)}, /*index=5*/f32[32,768]{1,0:T(8,128)S(1)}) custom-call(bf16[512,768]{1,0:T(8,128)(2,1)S(1)} %copy-done.7, f32[512,768]{1,0:T(8,128)S(1)} %copy-done.6, ...), custom_call_target="tpu_custom_call" | custom-call | flops 999999995904 | bytes 999999995904 | tf_op jit(solution)/shard_map/pallas_call | solution.py:892
  76.8 2.6 %collective-permute-start.12 = (bf16[32,1536]{1,0:T(8,128)(2,1)}, bf16[32,1536]{1,0:T(8,128)(2,1)}, u32[]{:S(2)}, u32[]{:S(2)}) collective-permute-start(bf16[32,1536]{1,0:T(8,128)(2,1)} %get-tuple-element.92.refs_0_), channel_id=1, source_target_pairs={{0,8},{2,10},{4,12},{6,14},{8,0},{10,2},{12,4},{14,6},{16,24},{18,... | collective-permute-start | bytes 294920 | tf_op jit(solution)/shard_map/ppermute | solution.py:29
  87.1 3.2 %collective-permute-done.14.refs_3_ = bf16[32,1536]{1,0:T(8,128)(2,1)} collective-permute-done((bf16[32,1536]{1,0:T(8,128)(2,1)}, bf16[32,1536]{1,0:T(8,128)(2,1)}, u32[]{:S(2)}, u32[]{:S(2)}) %collective-permute-start.14) | collective-permute-done | bytes 98336 | tf_op jit(solution)/shard_map/ppermute | solution.py:29
  100.1 5.4 %shard_map.342 = (f32[32,768]{1,0:T(8,128)S(1)}, bf16[32,768]{1,0:T(8,128)(2,1)S(1)}, bf16[512,1536]{1,0:T(8,128)(2,1)S(1)}, f32[512,768]{1,0:T(8,128)}, f32[8,768]{1,0:T(8,128)S(1)}) custom-call(s32[32]{0:T(128)S(1)} %copy-done.20, f32[1]{0:T(128)S(6)} %copy.38.refs_2_.refs_1_, f32[1,512]{1,0:T(1,128)S(1)} %shard_map.341.refs_2_, ...), custom_call_target="tpu_custom_call" | custom-call | flops 999999995904 | bytes 999999995904 | tf_op jit(solution)/shard_map/pallas_call | solution.py:892
  105.6 2.5 %shard_map.343 = (bf16[384,768]{1,0:T(8,128)(2,1)}, bf16[384,768]{1,0:T(8,128)(2,1)S(1)}, bf16[384,768]{1,0:T(8,128)(2,1)}, bf16[384,768]{1,0:T(8,128)(2,1)S(1)}) custom-call(s32[1]{0:T(128)} %bitcast.refs_0_, bf16[512,768]{1,0:T(8,128)(2,1)S(1)} %get-tuple-element.88.refs_1_, bf16[512,1536]{1,0:T(8,128)(2,1)S(1)} %get-tuple-element.101.refs_2_), custom_call_target="tpu_custom_call" | custom-call | flops 999999995904 | bytes 999999995904 | tf_op jit(solution)/shard_map/pallas_call | solution.py:892
  111.3 8.7 %shard_map.344 = (f32[512,768]{1,0:T(8,128)S(1)}, bf16[512,768]{1,0:T(8,128)(2,1)S(1)}, bf16[3,512,384]{2,1,0:T(8,128)(2,1)S(1)}, f32[512,768]{1,0:T(8,128)}, f32[8,768]{1,0:T(8,128)S(1)}) custom-call(f32[512,768]{1,0:T(8,128)} %get-tuple-element.107.refs_0_, f32[512,768]{1,0:T(8,128)} %collective-permute-done.20.refs_1_, ...), custom_call_target="tpu_custom_call" | custom-call | flops 999999995904 | bytes 999999995904 | tf_op jit(solution)/shard_map/pallas_call | solution.py:892
  120.1 3.0 %shard_map.345 = (bf16[384,768]{1,0:T(8,128)(2,1)}, bf16[384,768]{1,0:T(8,128)(2,1)S(1)}, bf16[384,768]{1,0:T(8,128)(2,1)}, bf16[384,768]{1,0:T(8,128)(2,1)S(1)}) custom-call(s32[1]{0:T(128)} %bitcast.refs_0_, bf16[512,768]{1,0:T(8,128)(2,1)S(1)} %copy-done.26, bf16[3,512,384]{2,1,0:T(8,128)(2,1)S(1)} %get-tuple-element.112.refs_2_, ...), custom_call_target="tpu_custom_call" | custom-call | flops 999999995904 | bytes 999999995904 | tf_op jit(solution)/shard_map/pallas_call | solution.py:892
  123.1 4.2 %collective-permute-done.18.refs_2_ = bf16[384,768]{1,0:T(8,128)(2,1)} collective-permute-done((bf16[384,768]{1,0:T(8,128)(2,1)}, bf16[384,768]{1,0:T(8,128)(2,1)}, u32[]{:S(2)}, u32[]{:S(2)}) %collective-permute-start.18) | collective-permute-done | bytes 589856 | tf_op jit(solution)/shard_map/ppermute | solution.py:29
  134.4 5.8 %collective-permute-done.24.refs_2_ = bf16[192,768]{1,0:T(8,128)(2,1)S(1)} collective-permute-done((bf16[192,768]{1,0:T(8,128)(2,1)S(1)}, bf16[192,768]{1,0:T(8,128)(2,1)S(1)}, u32[]{:S(2)}, u32[]{:S(2)}) %collective-permute-start.24) | collective-permute-done | bytes 294944 | tf_op jit(solution)/shard_map/ppermute | solution.py:29
  145.2 4.3 %shard_map.348 = (f32[512,768]{1,0:T(8,128)}, bf16[32,768]{1,0:T(8,128)(2,1)S(1)}) custom-call(s32[1]{0:T(128)} %bitcast.2.refs_0_, f32[512,768]{1,0:T(8,128)} %get-tuple-element.124.refs_1_, f32[512,768]{1,0:T(8,128)} %collective-permute-done.29.refs_2_, bf16[512,768]{1,0:T(8,128)(2,1)S(1)} %copy-done.8, f32[768]{0:T(1024)S(1)} %copy-done.17, ...), custom_call_target="tpu_custom_call" | custom-call | flops 999999995904 | bytes 999999995904 | tf_op jit(solution)/shard_map/pallas_call | solution.py:892
  149.5 2.7 %collective-permute-done.30.refs_2_ = bf16[384,768]{1,0:T(8,128)(2,1)} collective-permute-done((bf16[384,768]{1,0:T(8,128)(2,1)}, bf16[384,768]{1,0:T(8,128)(2,1)}, u32[]{:S(2)}, u32[]{:S(2)}) %collective-permute-start.30) | collective-permute-done | bytes 589856 | tf_op jit(solution)/shard_map/ppermute | solution.py:29
  169.2 5.8 %collective-permute-done.33.refs_2_ = bf16[128,768]{1,0:T(8,128)(2,1)} collective-permute-done((bf16[128,768]{1,0:T(8,128)(2,1)}, bf16[128,768]{1,0:T(8,128)(2,1)}, u32[]{:S(2)}, u32[]{:S(2)}) %collective-permute-start.33) | collective-permute-done | bytes 196640 | tf_op jit(solution)/shard_map/ppermute | solution.py:29
  175.0 10.5 %collective-permute-done.34.refs_3_ = bf16[128,768]{1,0:T(8,128)(2,1)} collective-permute-done((bf16[128,768]{1,0:T(8,128)(2,1)}, bf16[128,768]{1,0:T(8,128)(2,1)}, u32[]{:S(2)}, u32[]{:S(2)}) %collective-permute-start.34) | collective-permute-done | bytes 196640 | tf_op jit(solution)/shard_map/ppermute | solution.py:29
  195.7 9.1 %collective-permute-done.37.refs_1_.refs_2_ = bf16[512,768]{1,0:T(8,128)(2,1)} collective-permute-done((bf16[512,768]{1,0:T(8,128)(2,1)}, bf16[512,768]{1,0:T(8,128)(2,1)}, u32[]{:S(2)}, u32[]{:S(2)}) %collective-permute-start.37) | collective-permute-done | bytes 786464 | tf_op jit(solution)/shard_map/ppermute | solution.py:29
  213.8 5.3 %collective-permute-done.43.refs_4_.refs_5_ = bf16[192,768]{1,0:T(8,128)(2,1)} collective-permute-done((bf16[192,768]{1,0:T(8,128)(2,1)}, bf16[192,768]{1,0:T(8,128)(2,1)}, u32[]{:S(2)}, u32[]{:S(2)}) %collective-permute-start.43) | collective-permute-done | bytes 294944 | tf_op jit(solution)/shard_map/ppermute | solution.py:29
  219.1 3.0 %collective-permute-done.42.refs_3_.refs_4_ = bf16[320,768]{1,0:T(8,128)(2,1)} collective-permute-done((bf16[320,768]{1,0:T(8,128)(2,1)}, bf16[320,768]{1,0:T(8,128)(2,1)}, u32[]{:S(2)}, u32[]{:S(2)}) %collective-permute-start.42) | collective-permute-done | bytes 491552 | tf_op jit(solution)/shard_map/ppermute | solution.py:29
  222.1 2.7 %shard_map.356 = (bf16[256,768]{1,0:T(8,128)(2,1)}, f32[1]{0:T(128)}, f32[2,384]{1,0:T(2,128)}, f32[768]{0:T(1024)}, f32[1536]{0:T(1024)}, /*index=5*/f32[768]{0...) custom-call(bf16[512,768]{1,0:T(8,128)(2,1)} %shard_map.352.refs_4_.refs_0_.refs_1_, ...), custom_call_target="tpu_custom_call" | custom-call | flops 999999995904 | bytes 999999995904 | tf_op jit(solution)/shard_map/pallas_call | solution.py:892
  224.8 4.3 %shard_map.357.refs_2_ = f32[768,1536]{1,0:T(8,128)} custom-call(s32[1]{0:T(128)} %bitcast.refs_0_, bf16[512,768]{1,0:T(8,128)(2,1)} %shard_map.352.refs_4_.refs_0_.refs_1_, bf16[512,768]{1,0:T(8,128)(2,1)} %collective-permute-done.37.refs_1_.refs_2_, bf16[512,768]{1,0:T(8,128)(2,1)} %collective-permute-done.38.refs_0_.refs_2_.refs_3_, ...), custom_call_target="tpu_custom_call" | custom-call | flops 999999995904 | bytes 999999995904 | tf_op jit(solution)/shard_map/pallas_call | solution.py:892
  235.8 2.5 collective-permute-start.50
  238.3 6.7 %shard_map.359.refs_6_ = f32[1536,768]{1,0:T(8,128)} custom-call(s32[1]{0:T(128)} %bitcast.2.refs_0_, bf16[128,1536]{1,0:T(8,128)(2,1)} %shard_map.340.refs_4_.refs_5_.refs_1_, bf16[128,1536]{1,0:T(8,128)(2,1)} %collective-permute-done.21.refs_6_.refs_2_, bf16[128,1536]{1,0:T(8,128)(2,1)} %collective-permute-done.22.refs_7_.refs_3_, ...), custom_call_target="tpu_custom_call" | custom-call | flops 999999995904 | bytes 999999995904 | tf_op jit(solution)/shard_map/pallas_call | solution.py:892
  245.0 4.6 %shard_map.360 = (f32[3,768,384]{2,1,0:T(8,128)}, f32[384,768]{1,0:T(8,128)}) custom-call(s32[1]{0:T(128)} %bitcast.refs_0_, bf16[384,768]{1,0:T(8,128)(2,1)} %shard_map.355.refs_6_.refs_1_, bf16[384,768]{1,0:T(8,128)(2,1)} %collective-permute-done.47.refs_1_.refs_2_, bf16[384,768]{1,0:T(8,128)(2,1)} %collective-permute-done.48.refs_0_.refs_3_, ...), custom_call_target="tpu_custom_call" | custom-call | flops 999999995904 | bytes 999999995904 | tf_op jit(solution)/shard_map/pallas_call | solution.py:892
  (168 shorter events, 87.0 us)
Async XLA Ops:
  51.5 15.9 %collective-permute-start = (f32[512,768]{1,0:T(8,128)}, f32[512,768]{1,0:T(8,128)}, u32[]{:S(2)}, u32[]{:S(2)}) collective-permute-start(f32[512,768]{1,0:T(8,128)} %get-tuple-element.87.refs_4_.refs_1_), channel_id=1, source_target_pairs={{0,1},{1,0},{2,3},{3,2},{4,5},{5,4},{6,7},{7,6},{8,9},{9,8},{10,11... | collective-permute-start | bytes 4718600 | tf_op jit(solution)/shard_map/ppermute | solution.py:24
  54.6 19.1 %collective-permute-start.4 = (bf16[64,768]{1,0:T(8,128)(2,1)}, bf16[64,768]{1,0:T(8,128)(2,1)}, u32[]{:S(2)}, u32[]{:S(2)}) collective-permute-start(bf16[64,768]{1,0:T(8,128)(2,1)} %shard_map.336.refs_10_.refs_0_), channel_id=1, source_target_pairs={{0,2},{2,0},{4,6},{6,4},{8,10},{10,8},{12,14},{14,12},{16,18},{18,... | collective-permute-start | bytes 294920 | tf_op jit(solution)/shard_map/ppermute | solution.py:29
  55.5 18.2 %collective-permute-start.5 = (bf16[64,768]{1,0:T(8,128)(2,1)}, bf16[64,768]{1,0:T(8,128)(2,1)}, u32[]{:S(2)}, u32[]{:S(2)}) collective-permute-start(bf16[64,768]{1,0:T(8,128)(2,1)} %shard_map.336.refs_10_.refs_0_), channel_id=1, source_target_pairs={{0,4},{2,6},{4,0},{6,2},{8,12},{10,14},{12,8},{14,10},{16,20},{18,... | collective-permute-start | bytes 294920 | tf_op jit(solution)/shard_map/ppermute | solution.py:29
  96.5 23.5 %collective-permute-start.21 = (bf16[128,1536]{1,0:T(8,128)(2,1)}, bf16[128,1536]{1,0:T(8,128)(2,1)}, u32[]{:S(2)}, u32[]{:S(2)}) collective-permute-start(bf16[128,1536]{1,0:T(8,128)(2,1)} %shard_map.340.refs_4_.refs_5_.refs_1_), channel_id=1, source_target_pairs={{0,2},{2,0},{4,6},{6,4},{8,10},{10,8},{12,14},{14,12},{16,18},{18,... | collective-permute-start | bytes 1179656 | tf_op jit(solution)/shard_map/ppermute | solution.py:29
  97.1 23.0 %collective-permute-start.22 = (bf16[128,1536]{1,0:T(8,128)(2,1)}, bf16[128,1536]{1,0:T(8,128)(2,1)}, u32[]{:S(2)}, u32[]{:S(2)}) collective-permute-start(bf16[128,1536]{1,0:T(8,128)(2,1)} %shard_map.340.refs_4_.refs_5_.refs_1_), channel_id=1, source_target_pairs={{0,4},{2,6},{4,0},{6,2},{8,12},{10,14},{12,8},{14,10},{16,20},{18,... | collective-permute-start | bytes 1179656 | tf_op jit(solution)/shard_map/ppermute | solution.py:29
  98.5 21.5 %collective-permute-start.23 = (bf16[128,1536]{1,0:T(8,128)(2,1)}, bf16[128,1536]{1,0:T(8,128)(2,1)}, u32[]{:S(2)}, u32[]{:S(2)}) collective-permute-start(bf16[128,1536]{1,0:T(8,128)(2,1)} %shard_map.340.refs_4_.refs_5_.refs_1_), channel_id=1, source_target_pairs={{0,6},{2,4},{4,2},{6,0},{8,14},{10,12},{12,10},{14,8},{16,22},{18,... | collective-permute-start | bytes 1179656 | tf_op jit(solution)/shard_map/ppermute | solution.py:29
  108.1 19.2 %collective-permute-start.18 = (bf16[384,768]{1,0:T(8,128)(2,1)}, bf16[384,768]{1,0:T(8,128)(2,1)}, u32[]{:S(2)}, u32[]{:S(2)}) collective-permute-start(bf16[384,768]{1,0:T(8,128)(2,1)} %get-tuple-element.103.refs_10_), channel_id=1, source_target_pairs={{0,2},{2,0},{4,6},{6,4},{8,10},{10,8},{12,14},{14,12},{16,18},{18,... | collective-permute-start | bytes 1769480 | tf_op jit(solution)/shard_map/ppermute | solution.py:29
  109.2 19.5 %collective-permute-start.19 = (bf16[384,768]{1,0:T(8,128)(2,1)}, bf16[384,768]{1,0:T(8,128)(2,1)}, u32[]{:S(2)}, u32[]{:S(2)}) collective-permute-start(bf16[384,768]{1,0:T(8,128)(2,1)} %get-tuple-element.105), channel_id=1, source_target_pairs={{0,4},{2,6},{4,0},{6,2},{8,12},{10,14},{12,8},{14,10},{16,20},{18,... | collective-permute-start | bytes 1769480 | tf_op jit(solution)/shard_map/ppermute | solution.py:29
  132.7 19.5 %collective-permute-start.30 = (bf16[384,768]{1,0:T(8,128)(2,1)}, bf16[384,768]{1,0:T(8,128)(2,1)}, u32[]{:S(2)}, u32[]{:S(2)}) collective-permute-start(bf16[384,768]{1,0:T(8,128)(2,1)} %get-tuple-element.115.refs_5_), channel_id=1, source_target_pairs={{0,2},{2,0},{4,6},{6,4},{8,10},{10,8},{12,14},{14,12},{16,18},{18,... | collective-permute-start | bytes 1769480 | tf_op jit(solution)/shard_map/ppermute | solution.py:29
  132.9 19.2 %collective-permute-start.31 = (bf16[384,768]{1,0:T(8,128)(2,1)}, bf16[384,768]{1,0:T(8,128)(2,1)}, u32[]{:S(2)}, u32[]{:S(2)}) collective-permute-start(bf16[384,768]{1,0:T(8,128)(2,1)} %get-tuple-element.132), channel_id=1, source_target_pairs={{0,4},{2,6},{4,0},{6,2},{8,12},{10,14},{12,8},{14,10},{16,20},{18,... | collective-permute-start | bytes 1769480 | tf_op jit(solution)/shard_map/ppermute | solution.py:29
  141.7 14.8 %collective-permute-start.26 = (bf16[96,768]{1,0:T(8,128)(2,1)}, bf16[96,768]{1,0:T(8,128)(2,1)}, u32[]{:S(2)}, u32[]{:S(2)}) collective-permute-start(bf16[96,768]{1,0:T(8,128)(2,1)} %get-tuple-element.121), channel_id=1, source_target_pairs={{0,8},{2,10},{4,12},{6,14},{8,0},{10,2},{12,4},{14,6},{16,24},{18,... | collective-permute-start | bytes 442376 | tf_op jit(solution)/shard_map/ppermute | solution.py:29
  159.5 15.5 %collective-permute-start.33 = (bf16[128,768]{1,0:T(8,128)(2,1)}, bf16[128,768]{1,0:T(8,128)(2,1)}, u32[]{:S(2)}, u32[]{:S(2)}) collective-permute-start(bf16[128,768]{1,0:T(8,128)(2,1)} %shard_map.350.refs_5_.refs_0_), channel_id=1, source_target_pairs={{0,16},{2,18},{4,20},{6,22},{8,24},{10,26},{12,28},{14,30},{16,0},... | collective-permute-start | bytes 589832 | tf_op jit(solution)/shard_map/ppermute | solution.py:29
  160.2 25.2 %collective-permute-start.34 = (bf16[128,768]{1,0:T(8,128)(2,1)}, bf16[128,768]{1,0:T(8,128)(2,1)}, u32[]{:S(2)}, u32[]{:S(2)}) collective-permute-start(bf16[128,768]{1,0:T(8,128)(2,1)} %shard_map.350.refs_5_.refs_0_), channel_id=1, source_target_pairs={{0,24},{2,26},{4,28},{6,30},{8,16},{10,18},{12,20},{14,22},{16,8},... | collective-permute-start | bytes 589832 | tf_op jit(solution)/shard_map/ppermute | solution.py:29
  165.7 24.1 %collective-permute-start.39 = (bf16[96,768]{1,0:T(8,128)(2,1)}, bf16[96,768]{1,0:T(8,128)(2,1)}, u32[]{:S(2)}, u32[]{:S(2)}) collective-permute-start(bf16[96,768]{1,0:T(8,128)(2,1)} %get-tuple-element.138), channel_id=1, source_target_pairs={{0,8},{2,10},{4,12},{6,14},{8,0},{10,2},{12,4},{14,6},{16,24},{18,... | collective-permute-start | bytes 442376 | tf_op jit(solution)/shard_map/ppermute | solution.py:29
  166.7 23.1 %collective-permute-start.40 = (bf16[96,768]{1,0:T(8,128)(2,1)}, bf16[96,768]{1,0:T(8,128)(2,1)}, u32[]{:S(2)}, u32[]{:S(2)}) collective-permute-start(bf16[96,768]{1,0:T(8,128)(2,1)} %get-tuple-element.139), channel_id=1, source_target_pairs={{0,16},{2,18},{4,20},{6,22},{8,24},{10,26},{12,28},{14,30},{16,0},... | collective-permute-start | bytes 442376 | tf_op jit(solution)/shard_map/ppermute | solution.py:29
  167.6 22.8 %collective-permute-start.41 = (bf16[96,768]{1,0:T(8,128)(2,1)}, bf16[96,768]{1,0:T(8,128)(2,1)}, u32[]{:S(2)}, u32[]{:S(2)}) collective-permute-start(bf16[96,768]{1,0:T(8,128)(2,1)} %get-tuple-element.140), channel_id=1, source_target_pairs={{0,24},{2,26},{4,28},{6,30},{8,16},{10,18},{12,20},{14,22},{16,8},... | collective-permute-start | bytes 442376 | tf_op jit(solution)/shard_map/ppermute | solution.py:29
  187.6 17.2 %collective-permute-start.37 = (bf16[512,768]{1,0:T(8,128)(2,1)}, bf16[512,768]{1,0:T(8,128)(2,1)}, u32[]{:S(2)}, u32[]{:S(2)}) collective-permute-start(bf16[512,768]{1,0:T(8,128)(2,1)} %shard_map.352.refs_4_.refs_0_.refs_1_), channel_id=1, source_target_pairs={{0,2},{2,0},{4,6},{6,4},{8,10},{10,8},{12,14},{14,12},{16,18},{18,... | collective-permute-start | bytes 2359304 | tf_op jit(solution)/shard_map/ppermute | solution.py:29
  189.2 16.3 %collective-permute-start.38 = (bf16[512,768]{1,0:T(8,128)(2,1)}, bf16[512,768]{1,0:T(8,128)(2,1)}, u32[]{:S(2)}, u32[]{:S(2)}) collective-permute-start(bf16[512,768]{1,0:T(8,128)(2,1)} %shard_map.352.refs_4_.refs_0_.refs_1_), channel_id=1, source_target_pairs={{0,4},{2,6},{4,0},{6,2},{8,12},{10,14},{12,8},{14,10},{16,20},{18,... | collective-permute-start | bytes 2359304 | tf_op jit(solution)/shard_map/ppermute | solution.py:29
  192.2 18.4 %collective-permute-start.44 = (bf16[96,768]{1,0:T(8,128)(2,1)}, bf16[96,768]{1,0:T(8,128)(2,1)}, u32[]{:S(2)}, u32[]{:S(2)}) collective-permute-start(bf16[96,768]{1,0:T(8,128)(2,1)} %shard_map.353.refs_2_.refs_0_), channel_id=1, source_target_pairs={{0,8},{2,10},{4,12},{6,14},{8,0},{10,2},{12,4},{14,6},{16,24},{18,... | collective-permute-start | bytes 442376 | tf_op jit(solution)/shard_map/ppermute | solution.py:29
  192.2 18.4 %collective-permute-start.45 = (bf16[96,768]{1,0:T(8,128)(2,1)}, bf16[96,768]{1,0:T(8,128)(2,1)}, u32[]{:S(2)}, u32[]{:S(2)}) collective-permute-start(bf16[96,768]{1,0:T(8,128)(2,1)} %shard_map.353.refs_2_.refs_0_), channel_id=1, source_target_pairs={{0,16},{2,18},{4,20},{6,22},{8,24},{10,26},{12,28},{14,30},{16,0},... | collective-permute-start | bytes 442376 | tf_op jit(solution)/shard_map/ppermute | solution.py:29
  194.1 16.6 %collective-permute-start.46 = (bf16[96,768]{1,0:T(8,128)(2,1)}, bf16[96,768]{1,0:T(8,128)(2,1)}, u32[]{:S(2)}, u32[]{:S(2)}) collective-permute-start(bf16[96,768]{1,0:T(8,128)(2,1)} %shard_map.353.refs_2_.refs_0_), channel_id=1, source_target_pairs={{0,24},{2,26},{4,28},{6,30},{8,16},{10,18},{12,20},{14,22},{16,8},... | collective-permute-start | bytes 442376 | tf_op jit(solution)/shard_map/ppermute | solution.py:29
  207.8 14.3 %collective-permute-start.42 = (bf16[320,768]{1,0:T(8,128)(2,1)}, bf16[320,768]{1,0:T(8,128)(2,1)}, u32[]{:S(2)}, u32[]{:S(2)}) collective-permute-start(bf16[320,768]{1,0:T(8,128)(2,1)} %get-tuple-element.141.refs_4_), channel_id=1, source_target_pairs={{0,2},{2,0},{4,6},{6,4},{8,10},{10,8},{12,14},{14,12},{16,18},{18,... | collective-permute-start | bytes 1474568 | tf_op jit(solution)/shard_map/ppermute | solution.py:29
  212.6 17.1 %collective-permute-start.47 = (bf16[384,768]{1,0:T(8,128)(2,1)}, bf16[384,768]{1,0:T(8,128)(2,1)}, u32[]{:S(2)}, u32[]{:S(2)}) collective-permute-start(bf16[384,768]{1,0:T(8,128)(2,1)} %shard_map.355.refs_6_.refs_1_), channel_id=1, source_target_pairs={{0,2},{2,0},{4,6},{6,4},{8,10},{10,8},{12,14},{14,12},{16,18},{18,... | collective-permute-start | bytes 1769480 | tf_op jit(solution)/shard_map/ppermute | solution.py:29
  212.9 16.8 %collective-permute-start.48 = (bf16[384,768]{1,0:T(8,128)(2,1)}, bf16[384,768]{1,0:T(8,128)(2,1)}, u32[]{:S(2)}, u32[]{:S(2)}) collective-permute-start(bf16[384,768]{1,0:T(8,128)(2,1)} %shard_map.355.refs_6_.refs_1_), channel_id=1, source_target_pairs={{0,4},{2,6},{4,0},{6,2},{8,12},{10,14},{12,8},{14,10},{16,20},{18,... | collective-permute-start | bytes 1769480 | tf_op jit(solution)/shard_map/ppermute | solution.py:29
  (58 other events, 504.5 us)

commit v3 on v2

--- a/solution.py
+++ b/solution.py
@@ -767,10 +767,13 @@
 def narrow_grad_kernel(half, index_ref, *refs):
     parts, (near_ref, far_ref, out_ref, grads) = refs[:-4], refs[-4:]
     rows, width = parts[0].shape[0], grads.shape[1]
-    for place in range(near_ref.shape[0] // half):
+    devices = near_ref.shape[0] // half
+    for place in range(devices):
+        plane, group, high = place % 4, place // 4 % (devices // GROUP), place * 4 // devices
+        source = (plane * Z_SIZE + high) * (devices // GROUP) + group
         for ref, which in ((near_ref, index_ref[0]), (far_ref, 1 - index_ref[0])):
             start = pl.multiple_of((2 * place + which) * half, half)
-            grads[pl.ds(start, half), :] = ref[place * half : (place + 1) * half, :]
+            grads[pl.ds(start, half), :] = ref[source * half : (source + 1) * half, :]
     for chunk in range(out_ref.shape[0] // width):
         lanes = slice(chunk * width, (chunk + 1) * width)
         total = t_dot(parts[0][:, lanes], grads[:rows, :])
@@ -876,7 +879,7 @@
         ref[...] = total[place]
 
 
-def call(kernel, inside, shapes, outside=(), scratch=(), index=(), small=(), after=(), limit=24):
+def call(kernel, inside, shapes, outside=(), scratch=(), index=(), small=(), after=(), limit=24, mark=False, busy=BUSY):
     vmem = pl.BlockSpec(memory_space=pltpu.VMEM)
     extra = [pltpu.VMEM(array.shape, array.dtype) for array in outside]
     extra += list(scratch)
@@ -886,8 +889,16 @@
     small = index + list(small)
     before = len(small) + len(inside) + len(outside)
 
+    if mark:
+        shapes = tuple(shapes) + (((8, 128), F32),)
+
     def body(*refs):
-        kernel(*refs[:before], *refs[before + len(after) :])
+        refs = refs[:before] + refs[before + len(after) :]
+        if mark:
+            last = before + len(shapes) - 1
+            refs[last][...] = jnp.zeros((8, 128), F32)
+            refs = refs[:last] + refs[last + 1 :]
+        kernel(*refs)
 
     return pl.pallas_call(
         body,
@@ -898,11 +909,11 @@
         out_specs=[vmem] * len(shapes),
         scratch_shapes=extra,
         compiler_params=pltpu.CompilerParams(vmem_limit_bytes=limit * 1024 * 1024),
-        cost_estimate=pl.CostEstimate(flops=BUSY, bytes_accessed=BUSY, transcendentals=0),
+        cost_estimate=pl.CostEstimate(flops=busy, bytes_accessed=busy, transcendentals=0),
     )(*small, *inside, *outside, *after)
 
 
-def move(arrays, sizes, plan, after=()):
+def move(arrays, sizes, plan, after=(), mark=False, busy=BUSY):
     width, kind = arrays[0].shape[1], arrays[0].dtype
 
     def body(*refs):
@@ -910,7 +921,7 @@
         for source, first, rows, target, start in plan:
             outs[target][start : start + rows, :] = ins[source][first : first + rows, :]
 
-    return call(body, arrays, tuple(((size, width), kind) for size in sizes), after=after)
+    return call(body, arrays, tuple(((size, width), kind) for size in sizes), after=after, mark=mark, busy=busy)
 
 
 GROUP = 16
@@ -961,42 +972,48 @@
     after = yield
     arrived = (dp_swap(first_sent, 1), dp_swap(second_sent, 2))
     half = (rows // 2, width)
-    first_sent, first_kept, second_sent, second_kept = call(
+    first_sent, first_kept, second_sent, second_kept, mark = call(
         fold_kernel,
         (first_kept, arrived[0], second_kept, arrived[1]),
         ((half, BF16), (half, F32), (half, BF16), (half, F32)),
         index=(place,),
         after=after,
-    )
-    after = yield first_kept
+        mark=True, busy=1,
+    )
+    after = yield mark
     arrived = (dp_swap(first_sent, 2), dp_swap(second_sent, 1))
     block = (rows // Z_SIZE, width)
-    own, *sent = call(
+    own, *sent, mark = call(
         cut_kernel,
         (first_kept, arrived[0], second_kept, arrived[1]),
         ((block, F32),) + ((block, BF16),) * (Z_SIZE - 1),
         index=(place,),
         after=after,
-    )
-    after = yield own
+        mark=True, busy=1,
+    )
+    after = yield mark
     arrived = [dp_swap(values, step * Z_STRIDE) for step, values in enumerate(sent, 1)]
     size = lax.axis_size("dp")
     more = 0 if extra is None else extra[0].shape[0]
     if size > GROUP:
-        (mine,) = call(add_kernel, (own, *arrived), ((own.shape, F32),), after=after)
+        mine, mark = call(
+            add_kernel, (own, *arrived), ((own.shape, F32),), after=after, mark=True, busy=1
+        )
         groups = [list(range(index, size, GROUP)) for index in range(GROUP)]
         mine = lax.psum(mine, "dp", axis_index_groups=groups).astype(BF16)
         if more:
             mine = jnp.concatenate([mine, *extra], axis=0)
     else:
-        (mine,) = call(
+        mine, mark = call(
             add_kernel,
             (own, *arrived) + (tuple(extra) if more else ()),
             (((block[0] + more, width), BF16),),
             after=after,
+            mark=True, busy=1,
         )
-    after = yield mine
-    pieces = [mine] + [dp_swap(mine, step * Z_STRIDE) for step in range(1, Z_SIZE)]
+    after = yield mark
+    high = dp_swap(mine, 2 * Z_STRIDE)
+    pieces = [mine, dp_swap(mine, Z_STRIDE), high, dp_swap(high, Z_STRIDE)]
     half = block[0] // 2
     plan, start = [], 0
     for first, count in ((0, half), (2 * half, more), (half, half)):
@@ -1004,17 +1021,18 @@
             if count:
                 plan.append((piece, first, count, 0, start))
             start += count
-    (joined,) = move(pieces, (start,), plan, after)
+    joined, mark = move(pieces, (start,), plan, after, mark=True, busy=1)
     along_x, along_y = dp_swap(joined, 1), dp_swap(joined, 2)
-    after = yield joined
+    after = yield mark
     share = Z_SIZE * half
-    first, second = move(
+    first, second, mark = move(
         (along_y, along_x),
         (start - share, share),
         ((0, 0, start - share, 0, 0), (1, start - share, share, 1, 0)),
         after,
-    )
-    after = yield first
+        mark=True, busy=1,
+    )
+    after = yield mark
     yield joined, along_x, along_y, dp_swap(first, 1), dp_swap(second, 2)
 
 
@@ -1120,7 +1138,7 @@
         locked_widening_matrix,
         locked_narrowing_matrix,
     )
-    normed, qkv, soft, mixed, part = call(
+    normed, qkv, soft, mixed, part, mark = call(
         text_mix_kernel,
         (
             sentence_layer_entry,
@@ -1140,9 +1158,10 @@
         ),
         after=(image_emb,),
         limit=60,
+        mark=True,
     )
     other = mp_other(part)
-    near_images = dp_gather(image_emb, steps[:0:-1], [part] * (len(steps) - 1))
+    near_images = dp_gather(image_emb, steps[:0:-1], [mark] * (len(steps) - 1))
     residual, normed2, slope, hidden_sums, resid_sum, branch = call(
         text_widen_kernel,
         (
@@ -1169,7 +1188,7 @@
     )
 
     near_images = dp_gather(near_images, steps[:1], (branch,))
-    sums_parts = dp_parts(hidden_sums, steps[-1])
+    sums_parts = dp_parts(hidden_sums, steps[0])
     images, unit, factor, logits, powers, row_sum, col_sum, row_loss = call(
         functools.partial(logits_kernel, gather_masks(steps[::-1])),
         (
@@ -1195,15 +1214,21 @@
         small=(matched_picture_ids, sharpening_log),
     )
     after = (unit,)
-    for step in steps[-2::-1]:
+    for step in steps[2:] + [None]:
         rows = sums_parts[0].shape[0]
-        (joined_sums,) = move(
+        joined_sums, mark = move(
             sums_parts,
             (4 * rows,),
             [(place, 0, rows, 0, place * rows) for place in range(4)],
             after,
+            mark=True,
         )
-        sums_parts, after = dp_parts(joined_sums, step), (joined_sums,)
+        after = (mark,)
+        if step is not None:
+            sums_parts = dp_parts(joined_sums, step)
+    sums_high = dp_swap(joined_sums, 2 * Z_STRIDE)
+    sums_parts = [joined_sums, dp_swap(joined_sums, Z_STRIDE), sums_high]
+    sums_parts.append(dp_swap(sums_high, Z_STRIDE))
     col_parts = dp_parts(col_sum, steps[0])
     for step in steps[1:]:
         (col_sum,) = call(sum_kernel, col_parts, ((col_sum.shape, F32),), after=after)
@@ -1233,12 +1258,13 @@
     )
 
     other = mp_other(part)
-    widen_dealt = call(
+    *widen_dealt, mark = call(
         widen_grad_kernel,
         (normed2, grad_pre),
         dealt,
         scratch=(pltpu.VMEM(square, BF16),) * 2,
         index=(place,),
+        mark=True,
     )
     grad_residual, grad_branch1, flat, part, mixer_stat = call(
         mixer_back_kernel,
@@ -1259,23 +1285,24 @@
             ((8, model_width), F32),
         ),
         outside=(qkv, soft, mixer_triple_matrix),
-        after=(widen_dealt[0],),
+        after=(mark,),
     )
     other = mp_other(part)
     extra = []
     widen_sum = scatter_steps(widen_dealt, place, extra)
     next(widen_sum)
-    mixer_dealt = call(
+    *mixer_dealt, mark = call(
         mixer_grad_kernel,
         (normed, flat, mixed, grad_branch1),
         dealt,
         scratch=(pltpu.VMEM(square, BF16),) * 2,
         index=(place,),
-        after=sums_parts,
+        after=sums_parts[1:3],
+        mark=True,
     )
     mixer_sum = scatter_steps(mixer_dealt, place)
     next(mixer_sum)
-    last = widen_sum.send((mixer_dealt[0],))
+    last = widen_sum.send((mark,))
     last = widen_sum.send((last,))
     extra_rows = captions // 2 + 16
     grad_input, mine = call(
@@ -1319,29 +1346,31 @@
         after=(last,),
     )
     error, grad_pair, grad_b_out, grad_b_up, grad_b_down = results[:5]
-    (grad_w_up,) = call(
+    grad_w_up, mark = call(
         unpack_widen_kernel,
         widen_pieces,
         ((widening_matrix.shape, F32),),
         index=(place,),
-        after=(near_grads,),
+        after=(results[0],),
         limit=56,
-    )
-    last = mixer_sum.send((grad_w_up,))
-    (grad_w_down,) = call(
+        mark=True,
+    )
+    last = mixer_sum.send((mark,))
+    grad_w_down, mark = call(
         functools.partial(narrow_grad_kernel, captions // 2),
         (*sums_parts, near_grads, mp_other(near_grads)),
         ((narrowing_matrix.shape, F32),),
         scratch=(pltpu.VMEM((all_pairs, model_width), BF16),),
         index=(core,),
         after=(last,),
+        mark=True,
     )
     grad_qkv, grad_w_out = call(
         unpack_mixer_kernel,
         mixer_sum.send(()),
         ((mixer_triple_matrix.shape, F32), (mixer_result_matrix.shape, F32)),
         index=(place,),
-        after=(grad_w_down,),
+        after=(mark,),
         limit=56,
     )
     return (

time: 245 us -> 226 us (0.922)
  the two profiles are of different devices: /device:TPU:16 before, /device:TPU:0 now
where the time goes in v3:
time: 226 us
  Pallas kernels  105 us (46%)
  starting transfers between devices  69.6 us (31%)
  waiting for transfers between devices  47.9 us (21%)
    pallas_call x26, Pallas kernels, call(): pl.pallas_call(body, out_shape=[jax.ShapeDtypeStruct(shape, kind) for sha...  69.7 us
    ppermute x46, starting transfers between devices, dp_swap(): lax.ppermute(values, 'dp', [(index, index ^ mask) for index in range(size)])  64.1 us
    ppermute x46, waiting for transfers between devices, dp_swap(): lax.ppermute(values, 'dp', [(index, index ^ mask) for index in range(size)])  47.9 us
    pallas_call x1, Pallas kernels, image_tower(): pl.pallas_call(image_kernel, out_shape=jax.ShapeDtypeStruct((images, widt...  35.2 us
    ppermute x6, starting transfers between devices, mp_other(): return lax.ppermute(values, 'mp', [(0, 1), (1, 0)])  5.54 us
  transfers between devices with their start and end apart: 52, of which 20 were waited for; matrix products, arithmetic and copies ran while one was open for 0% of the time, Pallas kernels for 27%

profile of v3, /device:TPU:0, one launch (start us, length us, event | category | flops | bytes accessed | tf_op | source)
XLA Modules:
  0.0 226.5 jit_solution(12684610479487544306)
XLA Ops:
  0.6 35.2 %shard_map.334.refs_7_.refs_0_ = bf16[16,768]{1,0:T(8,128)(2,1)} custom-call(s32[16]{0:T(128)} %flag_ref.1, bf16[145,16,768]{2,1,0:T(8,128)(2,1)} %bitcast.3, f32[2,768]{1,0:T(2,128)} %gain_ref.1, bf16[3,768,768]{2,1,0:T(8,128)(2,1)} %triple_hbm.1, bf16[768,768]{1,0:T(8,128)(2,1)} %result_hbm.1, bf16[768,3072]{1,0:T(8,128)(2,1)} %widen_hbm.1, ...), custom_call_target="tpu_custom_call" | custom-call | flops 999999995904 | bytes 999999995904 | tf_op jit(solution)/shard_map/pallas_call | solution.py:334
  35.9 5.1 %collective-permute-start.3 = (bf16[16,768]{1,0:T(8,128)(2,1)}, bf16[16,768]{1,0:T(8,128)(2,1)}, u32[]{:S(2)}, u32[]{:S(2)}) collective-permute-start(bf16[16,768]{1,0:T(8,128)(2,1)} %shard_map.334.refs_7_.refs_0_), channel_id=1, source_target_pairs={{0,24},{2,26},{4,28},{6,30},{8,16},{10,18},{12,20},{14,22},{16,8},... | collective-permute-start | bytes 73736 | tf_op jit(solution)/shard_map/ppermute | solution.py:29
  42.3 6.6 %shard_map.335 = (bf16[512,768]{1,0:T(8,128)(2,1)}, bf16[3,512,384]{2,1,0:T(8,128)(2,1)}, f32[4,3,256,128]{3,2,1,0:T(8,128)}, bf16[512,384]{1,0:T(8,128)(2,1)}, f32[512,768]{1,0:T(8,128)}, /*index=5*/f32[8,128]{1,0:T(8,128)}) custom-call(bf16[512,768]{1,0:T(8,128)(2,1)} %refs_3_.5, s32[512]{0:T(512)} %refs_4_.6, f32[768]{0:T(1024)} %refs_4_.7, f32[768]{0:T(1024)} %refs_3_.3, ...), custom_call_target="tpu_custom_call" | custom-call | flops 999999995904 | bytes 999999995904 | tf_op jit(solution)/shard_map/pallas_call | solution.py:903
  48.8 4.7 %collective-permute-start = (f32[512,768]{1,0:T(8,128)}, f32[512,768]{1,0:T(8,128)}, u32[]{:S(2)}, u32[]{:S(2)}) collective-permute-start(f32[512,768]{1,0:T(8,128)} %get-tuple-element.110.refs_1_), channel_id=1, source_target_pairs={{0,1},{1,0},{2,3},{3,2},{4,5},{5,4},{6,7},{7,6},{8,9},{9,8},{10,11... | collective-permute-start | bytes 4718600 | tf_op jit(solution)/shard_map/ppermute | solution.py:24
  55.9 3.7 %collective-permute-start.6 = (bf16[64,768]{1,0:T(8,128)(2,1)}, bf16[64,768]{1,0:T(8,128)(2,1)}, u32[]{:S(2)}, u32[]{:S(2)}) collective-permute-start(bf16[64,768]{1,0:T(8,128)(2,1)} %shard_map.336.refs_10_.refs_0_), channel_id=1, source_target_pairs={{0,6},{2,4},{4,2},{6,0},{8,14},{10,12},{12,10},{14,8},{16,22},{18,... | collective-permute-start | bytes 294920 | tf_op jit(solution)/shard_map/ppermute | solution.py:29
  59.6 4.7 %collective-permute-start.5 = (bf16[64,768]{1,0:T(8,128)(2,1)}, bf16[64,768]{1,0:T(8,128)(2,1)}, u32[]{:S(2)}, u32[]{:S(2)}) collective-permute-start(bf16[64,768]{1,0:T(8,128)(2,1)} %shard_map.336.refs_10_.refs_0_), channel_id=1, source_target_pairs={{0,4},{2,6},{4,0},{6,2},{8,12},{10,14},{12,8},{14,10},{16,20},{18,... | collective-permute-start | bytes 294920 | tf_op jit(solution)/shard_map/ppermute | solution.py:29
  64.4 6.2 %shard_map.337 = (f32[512,768]{1,0:T(8,128)S(1)}, bf16[512,768]{1,0:T(8,128)(2,1)S(1)}, f32[512,1536]{1,0:T(8,128)S(1)}, bf16[32,1536]{1,0:T(8,128)(2,1)}, f32[32,768]{1,0:T(8,128)S(1)}, /*index=5*/f32[32,768]{1,0:T(8,128)S(1)}) custom-call(bf16[512,768]{1,0:T(8,128)(2,1)S(1)} %copy-done.9, f32[512,768]{1,0:T(8,128)S(1)} %copy-done.8, ...), custom_call_target="tpu_custom_call" | custom-call | flops 999999995904 | bytes 999999995904 | tf_op jit(solution)/shard_map/pallas_call | solution.py:903
  93.1 5.4 %shard_map.342 = (f32[32,768]{1,0:T(8,128)S(1)}, bf16[32,768]{1,0:T(8,128)(2,1)S(1)}, bf16[512,1536]{1,0:T(8,128)(2,1)S(1)}, f32[512,768]{1,0:T(8,128)}, f32[8,768]{1,0:T(8,128)S(1)}) custom-call(s32[32]{0:T(128)S(1)} %copy-done.25, f32[1]{0:T(128)S(6)} %copy.38.refs_2_.refs_1_, f32[1,512]{1,0:T(1,128)S(1)} %shard_map.341.refs_2_, ...), custom_call_target="tpu_custom_call" | custom-call | flops 999999995904 | bytes 999999995904 | tf_op jit(solution)/shard_map/pallas_call | solution.py:903
  103.0 8.7 %shard_map.344 = (f32[512,768]{1,0:T(8,128)S(1)}, bf16[512,768]{1,0:T(8,128)(2,1)S(1)}, bf16[3,512,384]{2,1,0:T(8,128)(2,1)S(1)}, f32[512,768]{1,0:T(8,128)}, f32[8,768]{1,0:T(8,128)S(1)}) custom-call(f32[512,768]{1,0:T(8,128)} %get-tuple-element.132.refs_0_, f32[512,768]{1,0:T(8,128)} %collective-permute-done.20.refs_1_, ...), custom_call_target="tpu_custom_call" | custom-call | flops 999999995904 | bytes 999999995904 | tf_op jit(solution)/shard_map/pallas_call | solution.py:903
  111.9 3.0 %shard_map.345 = (bf16[384,768]{1,0:T(8,128)(2,1)}, bf16[384,768]{1,0:T(8,128)(2,1)S(1)}, bf16[384,768]{1,0:T(8,128)(2,1)}, bf16[384,768]{1,0:T(8,128)(2,1)S(1)}, f32[8,128]{1,0:T(8,128)S(1)}) custom-call(s32[1]{0:T(128)} %bitcast.refs_0_, bf16[512,768]{1,0:T(8,128)(2,1)S(1)} %copy-done.30, bf16[3,512,384]{2,1,0:T(8,128)(2,1)S(1)} %get-tuple-element.138.refs_2_, ...), custom_call_target="tpu_custom_call" | custom-call | flops 999999995904 | bytes 999999995904 | tf_op jit(solution)/shard_map/pallas_call | solution.py:903
  122.8 5.9 %collective-permute-done.23.refs_2_ = bf16[192,768]{1,0:T(8,128)(2,1)S(1)} collective-permute-done((bf16[192,768]{1,0:T(8,128)(2,1)S(1)}, bf16[192,768]{1,0:T(8,128)(2,1)S(1)}, u32[]{:S(2)}, u32[]{:S(2)}) %collective-permute-start.23) | collective-permute-done | bytes 294944 | tf_op jit(solution)/shard_map/ppermute | solution.py:29
  132.3 4.9 %collective-permute-start.26 = (bf16[96,768]{1,0:T(8,128)(2,1)}, bf16[96,768]{1,0:T(8,128)(2,1)}, u32[]{:S(2)}, u32[]{:S(2)}) collective-permute-start(bf16[96,768]{1,0:T(8,128)(2,1)} %get-tuple-element.150), channel_id=1, source_target_pairs={{0,16},{2,18},{4,20},{6,22},{8,24},{10,26},{12,28},{14,30},{16,0},... | collective-permute-start | bytes 442376 | tf_op jit(solution)/shard_map/ppermute | solution.py:29
  137.2 4.3 %shard_map.348 = (f32[512,768]{1,0:T(8,128)}, bf16[32,768]{1,0:T(8,128)(2,1)S(1)}) custom-call(s32[1]{0:T(128)} %bitcast.2.refs_0_, f32[512,768]{1,0:T(8,128)} %get-tuple-element.152.refs_1_, f32[512,768]{1,0:T(8,128)} %collective-permute-done.28.refs_2_, bf16[512,768]{1,0:T(8,128)(2,1)S(1)} %copy-done.10, f32[768]{0:T(1024)S(1)} %copy-done.22, ...), custom_call_target="tpu_custom_call" | custom-call | flops 999999995904 | bytes 999999995904 | tf_op jit(solution)/shard_map/pallas_call | solution.py:903
  147.0 3.1 %collective-permute-start.32 = (bf16[128,768]{1,0:T(8,128)(2,1)S(1)}, bf16[128,768]{1,0:T(8,128)(2,1)S(1)}, u32[]{:S(2)}, u32[]{:S(2)}) collective-permute-start(bf16[128,768]{1,0:T(8,128)(2,1)S(1)} %get-tuple-element.164.refs_0_), channel_id=1, source_target_pairs={{0,16},{2,18},{4,20},{6,22},{8,24},{10,26},{12,28},{14,30},{16,0},... | collective-permute-start | bytes 589832 | tf_op jit(solution)/shard_map/ppermute | solution.py:29
  152.2 4.8 %collective-permute-done.32.refs_2_ = bf16[128,768]{1,0:T(8,128)(2,1)S(1)} collective-permute-done((bf16[128,768]{1,0:T(8,128)(2,1)S(1)}, bf16[128,768]{1,0:T(8,128)(2,1)S(1)}, u32[]{:S(2)}, u32[]{:S(2)}) %collective-permute-start.32) | collective-permute-done | bytes 196640 | tf_op jit(solution)/shard_map/ppermute | solution.py:29
  159.2 3.5 %collective-permute-done.33.refs_3_ = bf16[128,768]{1,0:T(8,128)(2,1)S(1)} collective-permute-done((bf16[128,768]{1,0:T(8,128)(2,1)S(1)}, bf16[128,768]{1,0:T(8,128)(2,1)S(1)}, u32[]{:S(2)}, u32[]{:S(2)}) %collective-permute-start.33) | collective-permute-done | bytes 196640 | tf_op jit(solution)/shard_map/ppermute | solution.py:29
  165.6 3.4 %collective-permute-start.39 = (bf16[96,768]{1,0:T(8,128)(2,1)S(1)}, bf16[96,768]{1,0:T(8,128)(2,1)S(1)}, u32[]{:S(2)}, u32[]{:S(2)}) collective-permute-start(bf16[96,768]{1,0:T(8,128)(2,1)S(1)} %get-tuple-element.174), channel_id=1, source_target_pairs={{0,16},{2,18},{4,20},{6,22},{8,24},{10,26},{12,28},{14,30},{16,0},... | collective-permute-start | bytes 442376 | tf_op jit(solution)/shard_map/ppermute | solution.py:29
  170.6 7.9 %collective-permute-done.39.refs_2_ = bf16[96,768]{1,0:T(8,128)(2,1)S(1)} collective-permute-done((bf16[96,768]{1,0:T(8,128)(2,1)S(1)}, bf16[96,768]{1,0:T(8,128)(2,1)S(1)}, u32[]{:S(2)}, u32[]{:S(2)}) %collective-permute-start.39) | collective-permute-done | bytes 147488 | tf_op jit(solution)/shard_map/ppermute | solution.py:29
  182.1 3.2 %collective-permute-start.44 = (bf16[96,768]{1,0:T(8,128)(2,1)S(1)}, bf16[96,768]{1,0:T(8,128)(2,1)S(1)}, u32[]{:S(2)}, u32[]{:S(2)}) collective-permute-start(bf16[96,768]{1,0:T(8,128)(2,1)S(1)} %get-tuple-element.180.refs_0_), channel_id=1, source_target_pairs={{0,16},{2,18},{4,20},{6,22},{8,24},{10,26},{12,28},{14,30},{16,0},... | collective-permute-start | bytes 442376 | tf_op jit(solution)/shard_map/ppermute | solution.py:29
  193.2 3.7 %collective-permute-done.45.refs_3_ = bf16[96,768]{1,0:T(8,128)(2,1)S(1)} collective-permute-done((bf16[96,768]{1,0:T(8,128)(2,1)S(1)}, bf16[96,768]{1,0:T(8,128)(2,1)S(1)}, u32[]{:S(2)}, u32[]{:S(2)}) %collective-permute-start.45) | collective-permute-done | bytes 147488 | tf_op jit(solution)/shard_map/ppermute | solution.py:29
  200.9 5.0 %shard_map.357 = (f32[768,1536]{1,0:T(8,128)}, f32[8,128]{1,0:T(8,128)}) custom-call(s32[1]{0:T(128)} %bitcast.refs_0_, bf16[512,768]{1,0:T(8,128)(2,1)} %copy-done.11, bf16[512,768]{1,0:T(8,128)(2,1)} %copy-done.1, bf16[512,768]{1,0:T(8,128)(2,1)} %copy-done, bf16[320,768]{1,0:T(8,128)(2,1)} %copy-done.13, bf16[192,768]{1,0:T(8,128)(2,1)} %copy-done.14, ...), custom_call_target="tpu_custom_call" | custom-call | flops 999999995904 | bytes 999999995904 | tf_op jit(solution)/shard_map/pallas_call | solution.py:903
  205.9 3.2 %collective-permute-done.47.refs_0_.refs_3_ = bf16[384,768]{1,0:T(8,128)(2,1)} collective-permute-done((bf16[384,768]{1,0:T(8,128)(2,1)}, bf16[384,768]{1,0:T(8,128)(2,1)}, u32[]{:S(2)}, u32[]{:S(2)}) %collective-permute-start.47) | collective-permute-done | bytes 589856 | tf_op jit(solution)/shard_map/ppermute | solution.py:29
  214.6 6.7 %shard_map.359 = (f32[1536,768]{1,0:T(8,128)}, f32[8,128]{1,0:T(8,128)S(1)}) custom-call(s32[1]{0:T(128)} %bitcast.2.refs_0_, bf16[128,1536]{1,0:T(8,128)(2,1)} %get-tuple-element.141.refs_1_, bf16[128,1536]{1,0:T(8,128)(2,1)} %collective-permute-done.21.refs_5_.refs_2_, bf16[128,1536]{1,0:T(8,128)(2,1)} %collective-permute-done.22.refs_6_.refs_3_, ...), custom_call_target="tpu_custom_call" | custom-call | flops 999999995904 | bytes 999999995904 | tf_op jit(solution)/shard_map/pallas_call | solution.py:903
  221.9 4.6 %shard_map.360 = (f32[3,768,384]{2,1,0:T(8,128)}, f32[384,768]{1,0:T(8,128)}) custom-call(s32[1]{0:T(128)} %bitcast.refs_0_, bf16[384,768]{1,0:T(8,128)(2,1)} %get-tuple-element.185.refs_1_, bf16[384,768]{1,0:T(8,128)(2,1)} %collective-permute-done.46.refs_1_.refs_2_, bf16[384,768]{1,0:T(8,128)(2,1)} %collective-permute-done.47.refs_0_.refs_3_, ...), custom_call_target="tpu_custom_call" | custom-call | flops 999999995904 | bytes 999999995904 | tf_op jit(solution)/shard_map/pallas_call | solution.py:903
  (180 shorter events, 77.3 us)
Async XLA Ops:
  35.9 17.7 %collective-permute-start.3 = (bf16[16,768]{1,0:T(8,128)(2,1)}, bf16[16,768]{1,0:T(8,128)(2,1)}, u32[]{:S(2)}, u32[]{:S(2)}) collective-permute-start(bf16[16,768]{1,0:T(8,128)(2,1)} %shard_map.334.refs_7_.refs_0_), channel_id=1, source_target_pairs={{0,24},{2,26},{4,28},{6,30},{8,16},{10,18},{12,20},{14,22},{16,8},... | collective-permute-start | bytes 73736 | tf_op jit(solution)/shard_map/ppermute | solution.py:29
  41.0 12.6 %collective-permute-start.2 = (bf16[16,768]{1,0:T(8,128)(2,1)}, bf16[16,768]{1,0:T(8,128)(2,1)}, u32[]{:S(2)}, u32[]{:S(2)}) collective-permute-start(bf16[16,768]{1,0:T(8,128)(2,1)} %shard_map.334.refs_7_.refs_0_), channel_id=1, source_target_pairs={{0,16},{2,18},{4,20},{6,22},{8,24},{10,26},{12,28},{14,30},{16,0},... | collective-permute-start | bytes 73736 | tf_op jit(solution)/shard_map/ppermute | solution.py:29
  41.8 11.7 %collective-permute-start.1 = (bf16[16,768]{1,0:T(8,128)(2,1)}, bf16[16,768]{1,0:T(8,128)(2,1)}, u32[]{:S(2)}, u32[]{:S(2)}) collective-permute-start(bf16[16,768]{1,0:T(8,128)(2,1)} %shard_map.334.refs_7_.refs_0_), channel_id=1, source_target_pairs={{0,8},{2,10},{4,12},{6,14},{8,0},{10,2},{12,4},{14,6},{16,24},{18,... | collective-permute-start | bytes 73736 | tf_op jit(solution)/shard_map/ppermute | solution.py:29
  48.8 15.4 %collective-permute-start = (f32[512,768]{1,0:T(8,128)}, f32[512,768]{1,0:T(8,128)}, u32[]{:S(2)}, u32[]{:S(2)}) collective-permute-start(f32[512,768]{1,0:T(8,128)} %get-tuple-element.110.refs_1_), channel_id=1, source_target_pairs={{0,1},{1,0},{2,3},{3,2},{4,5},{5,4},{6,7},{7,6},{8,9},{9,8},{10,11... | collective-permute-start | bytes 4718600 | tf_op jit(solution)/shard_map/ppermute | solution.py:24
  55.9 14.7 %collective-permute-start.6 = (bf16[64,768]{1,0:T(8,128)(2,1)}, bf16[64,768]{1,0:T(8,128)(2,1)}, u32[]{:S(2)}, u32[]{:S(2)}) collective-permute-start(bf16[64,768]{1,0:T(8,128)(2,1)} %shard_map.336.refs_10_.refs_0_), channel_id=1, source_target_pairs={{0,6},{2,4},{4,2},{6,0},{8,14},{10,12},{12,10},{14,8},{16,22},{18,... | collective-permute-start | bytes 294920 | tf_op jit(solution)/shard_map/ppermute | solution.py:29
  59.6 11.0 %collective-permute-start.5 = (bf16[64,768]{1,0:T(8,128)(2,1)}, bf16[64,768]{1,0:T(8,128)(2,1)}, u32[]{:S(2)}, u32[]{:S(2)}) collective-permute-start(bf16[64,768]{1,0:T(8,128)(2,1)} %shard_map.336.refs_10_.refs_0_), channel_id=1, source_target_pairs={{0,4},{2,6},{4,0},{6,2},{8,12},{10,14},{12,8},{14,10},{16,20},{18,... | collective-permute-start | bytes 294920 | tf_op jit(solution)/shard_map/ppermute | solution.py:29
  91.4 20.4 %collective-permute-start.22 = (bf16[128,1536]{1,0:T(8,128)(2,1)}, bf16[128,1536]{1,0:T(8,128)(2,1)}, u32[]{:S(2)}, u32[]{:S(2)}) collective-permute-start(bf16[128,1536]{1,0:T(8,128)(2,1)} %get-tuple-element.141.refs_1_), channel_id=1, source_target_pairs={{0,16},{2,18},{4,20},{6,22},{8,24},{10,26},{12,28},{14,30},{16,0},... | collective-permute-start | bytes 1179656 | tf_op jit(solution)/shard_map/ppermute | solution.py:29
  91.4 20.4 %collective-permute-start.21 = (bf16[128,1536]{1,0:T(8,128)(2,1)}, bf16[128,1536]{1,0:T(8,128)(2,1)}, u32[]{:S(2)}, u32[]{:S(2)}) collective-permute-start(bf16[128,1536]{1,0:T(8,128)(2,1)} %get-tuple-element.141.refs_1_), channel_id=1, source_target_pairs={{0,8},{2,10},{4,12},{6,14},{8,0},{10,2},{12,4},{14,6},{16,24},{18,... | collective-permute-start | bytes 1179656 | tf_op jit(solution)/shard_map/ppermute | solution.py:29
  101.1 16.0 %collective-permute-start.18 = (bf16[384,768]{1,0:T(8,128)(2,1)}, bf16[384,768]{1,0:T(8,128)(2,1)}, u32[]{:S(2)}, u32[]{:S(2)}) collective-permute-start(bf16[384,768]{1,0:T(8,128)(2,1)} %get-tuple-element.128), channel_id=1, source_target_pairs={{0,2},{2,0},{4,6},{6,4},{8,10},{10,8},{12,14},{14,12},{16,18},{18,... | collective-permute-start | bytes 1769480 | tf_op jit(solution)/shard_map/ppermute | solution.py:29
  101.4 15.7 %collective-permute-start.19 = (bf16[384,768]{1,0:T(8,128)(2,1)}, bf16[384,768]{1,0:T(8,128)(2,1)}, u32[]{:S(2)}, u32[]{:S(2)}) collective-permute-start(bf16[384,768]{1,0:T(8,128)(2,1)} %get-tuple-element.130), channel_id=1, source_target_pairs={{0,4},{2,6},{4,0},{6,2},{8,12},{10,14},{12,8},{14,10},{16,20},{18,... | collective-permute-start | bytes 1769480 | tf_op jit(solution)/shard_map/ppermute | solution.py:29
  111.8 25.4 %collective-permute-start.28 = (f32[512,768]{1,0:T(8,128)}, f32[512,768]{1,0:T(8,128)}, u32[]{:S(2)}, u32[]{:S(2)}) collective-permute-start(f32[512,768]{1,0:T(8,128)} %get-tuple-element.152.refs_1_), channel_id=1, source_target_pairs={{0,1},{1,0},{2,3},{3,2},{4,5},{5,4},{6,7},{7,6},{8,9},{9,8},{10,11... | collective-permute-start | bytes 4718600 | tf_op jit(solution)/shard_map/ppermute | solution.py:24
  120.8 20.6 %collective-permute-start.29 = (bf16[384,768]{1,0:T(8,128)(2,1)}, bf16[384,768]{1,0:T(8,128)(2,1)}, u32[]{:S(2)}, u32[]{:S(2)}) collective-permute-start(bf16[384,768]{1,0:T(8,128)(2,1)} %get-tuple-element.160), channel_id=1, source_target_pairs={{0,2},{2,0},{4,6},{6,4},{8,10},{10,8},{12,14},{14,12},{16,18},{18,... | collective-permute-start | bytes 1769480 | tf_op jit(solution)/shard_map/ppermute | solution.py:29
  122.3 19.1 %collective-permute-start.30 = (bf16[384,768]{1,0:T(8,128)(2,1)}, bf16[384,768]{1,0:T(8,128)(2,1)}, u32[]{:S(2)}, u32[]{:S(2)}) collective-permute-start(bf16[384,768]{1,0:T(8,128)(2,1)} %get-tuple-element.162), channel_id=1, source_target_pairs={{0,4},{2,6},{4,0},{6,2},{8,12},{10,14},{12,8},{14,10},{16,20},{18,... | collective-permute-start | bytes 1769480 | tf_op jit(solution)/shard_map/ppermute | solution.py:29
  131.1 11.8 %collective-permute-start.25 = (bf16[96,768]{1,0:T(8,128)(2,1)}, bf16[96,768]{1,0:T(8,128)(2,1)}, u32[]{:S(2)}, u32[]{:S(2)}) collective-permute-start(bf16[96,768]{1,0:T(8,128)(2,1)} %get-tuple-element.149), channel_id=1, source_target_pairs={{0,8},{2,10},{4,12},{6,14},{8,0},{10,2},{12,4},{14,6},{16,24},{18,... | collective-permute-start | bytes 442376 | tf_op jit(solution)/shard_map/ppermute | solution.py:29
  132.3 13.6 %collective-permute-start.26 = (bf16[96,768]{1,0:T(8,128)(2,1)}, bf16[96,768]{1,0:T(8,128)(2,1)}, u32[]{:S(2)}, u32[]{:S(2)}) collective-permute-start(bf16[96,768]{1,0:T(8,128)(2,1)} %get-tuple-element.150), channel_id=1, source_target_pairs={{0,16},{2,18},{4,20},{6,22},{8,24},{10,26},{12,28},{14,30},{16,0},... | collective-permute-start | bytes 442376 | tf_op jit(solution)/shard_map/ppermute | solution.py:29
  162.8 17.1 %collective-permute-start.37 = (bf16[512,768]{1,0:T(8,128)(2,1)S(1)}, bf16[512,768]{1,0:T(8,128)(2,1)S(1)}, u32[]{:S(2)}, u32[]{:S(2)}) collective-permute-start(bf16[512,768]{1,0:T(8,128)(2,1)S(1)} %get-tuple-element.171.refs_0_.refs_1_), channel_id=1, source_target_pairs={{0,4},{2,6},{4,0},{6,2},{8,12},{10,14},{12,8},{14,10},{16,20},{18,... | collective-permute-start | bytes 2359304 | tf_op jit(solution)/shard_map/ppermute | solution.py:29
  163.6 17.6 %collective-permute-start.36 = (bf16[512,768]{1,0:T(8,128)(2,1)S(1)}, bf16[512,768]{1,0:T(8,128)(2,1)S(1)}, u32[]{:S(2)}, u32[]{:S(2)}) collective-permute-start(bf16[512,768]{1,0:T(8,128)(2,1)S(1)} %get-tuple-element.171.refs_0_.refs_1_), channel_id=1, source_target_pairs={{0,2},{2,0},{4,6},{6,4},{8,10},{10,8},{12,14},{14,12},{16,18},{18,... | collective-permute-start | bytes 2359304 | tf_op jit(solution)/shard_map/ppermute | solution.py:29
  165.6 12.9 %collective-permute-start.39 = (bf16[96,768]{1,0:T(8,128)(2,1)S(1)}, bf16[96,768]{1,0:T(8,128)(2,1)S(1)}, u32[]{:S(2)}, u32[]{:S(2)}) collective-permute-start(bf16[96,768]{1,0:T(8,128)(2,1)S(1)} %get-tuple-element.174), channel_id=1, source_target_pairs={{0,16},{2,18},{4,20},{6,22},{8,24},{10,26},{12,28},{14,30},{16,0},... | collective-permute-start | bytes 442376 | tf_op jit(solution)/shard_map/ppermute | solution.py:29
  181.2 18.6 %collective-permute-start.41 = (bf16[320,768]{1,0:T(8,128)(2,1)S(1)}, bf16[320,768]{1,0:T(8,128)(2,1)S(1)}, u32[]{:S(2)}, u32[]{:S(2)}) collective-permute-start(bf16[320,768]{1,0:T(8,128)(2,1)S(1)} %get-tuple-element.178), channel_id=1, source_target_pairs={{0,2},{2,0},{4,6},{6,4},{8,10},{10,8},{12,14},{14,12},{16,18},{18,... | collective-permute-start | bytes 1474568 | tf_op jit(solution)/shard_map/ppermute | solution.py:29
  185.3 14.5 %collective-permute-start.42 = (bf16[192,768]{1,0:T(8,128)(2,1)S(1)}, bf16[192,768]{1,0:T(8,128)(2,1)S(1)}, u32[]{:S(2)}, u32[]{:S(2)}) collective-permute-start(bf16[192,768]{1,0:T(8,128)(2,1)S(1)} %get-tuple-element.179), channel_id=1, source_target_pairs={{0,4},{2,6},{4,0},{6,2},{8,12},{10,14},{12,8},{14,10},{16,20},{18,... | collective-permute-start | bytes 884744 | tf_op jit(solution)/shard_map/ppermute | solution.py:29
  191.0 23.6 %collective-permute-start.50 = (bf16[128,1536]{1,0:T(8,128)(2,1)}, bf16[128,1536]{1,0:T(8,128)(2,1)}, u32[]{:S(2)}, u32[]{:S(2)}) collective-permute-start(bf16[128,1536]{1,0:T(8,128)(2,1)} %collective-permute-done.22.refs_6_.refs_3_), channel_id=1, source_target_pairs={{0,8},{2,10},{4,12},{6,14},{8,0},{10,2},{12,4},{14,6},{16,24},{18,... | collective-permute-start | bytes 1179656 | tf_op jit(solution)/shard_map/ppermute | solution.py:29
  197.8 11.3 %collective-permute-start.47 = (bf16[384,768]{1,0:T(8,128)(2,1)}, bf16[384,768]{1,0:T(8,128)(2,1)}, u32[]{:S(2)}, u32[]{:S(2)}) collective-permute-start(bf16[384,768]{1,0:T(8,128)(2,1)} %get-tuple-element.185.refs_1_), channel_id=1, source_target_pairs={{0,4},{2,6},{4,0},{6,2},{8,12},{10,14},{12,8},{14,10},{16,20},{18,... | collective-permute-start | bytes 1769480 | tf_op jit(solution)/shard_map/ppermute | solution.py:29
  198.7 10.8 %collective-permute-start.46 = (bf16[384,768]{1,0:T(8,128)(2,1)}, bf16[384,768]{1,0:T(8,128)(2,1)}, u32[]{:S(2)}, u32[]{:S(2)}) collective-permute-start(bf16[384,768]{1,0:T(8,128)(2,1)} %get-tuple-element.185.refs_1_), channel_id=1, source_target_pairs={{0,2},{2,0},{4,6},{6,4},{8,10},{10,8},{12,14},{14,12},{16,18},{18,... | collective-permute-start | bytes 1769480 | tf_op jit(solution)/shard_map/ppermute | solution.py:29
  200.8 13.7 %collective-permute-start.51 = (bf16[256,768]{1,0:T(8,128)(2,1)}, bf16[256,768]{1,0:T(8,128)(2,1)}, u32[]{:S(2)}, u32[]{:S(2)}) collective-permute-start(bf16[256,768]{1,0:T(8,128)(2,1)} %get-tuple-element.189.refs_5_), channel_id=1, source_target_pairs={{0,1},{1,0},{2,3},{3,2},{4,5},{5,4},{6,7},{7,6},{8,9},{9,8},{10,11... | collective-permute-start | bytes 1179656 | tf_op jit(solution)/shard_map/ppermute | solution.py:24
  (64 other events, 508.9 us)

commit v4 on v3

--- a/solution.py
+++ b/solution.py
@@ -828,36 +828,36 @@
     return values[0]
 
 
-def collect_kernel(
-    scale,
-    rows,
-    joined_ref,
-    along_x_ref,
-    along_y_ref,
-    first_far_ref,
-    second_far_ref,
-    loss_ref,
-    near_ref,
-    error_ref,
-    pair_ref,
-    result_ref,
-    widen_ref,
-    narrow_ref,
-    gain1_ref,
-    shift1_ref,
-    gain2_ref,
-    shift2_ref,
-    temperature_ref,
-):
+def collect_kernel(scale, rows, *refs):
+    gathered, loss_ref, near_ref = refs[:8], refs[8], refs[9]
+    (
+        error_ref,
+        pair_ref,
+        result_ref,
+        widen_ref,
+        narrow_ref,
+        gain1_ref,
+        shift1_ref,
+        gain2_ref,
+        shift2_ref,
+        temperature_ref,
+    ) = refs[10:]
     half = rows - 16
-    first = second_far_ref.shape[0]
-    count = (first_far_ref.shape[0] - first) // rows
+    size = gathered[7].shape[0] // Z_SIZE
+    more = gathered[1].shape[0] - 2 * size
     totals = []
-    for piece, ref in enumerate((joined_ref, along_x_ref, along_y_ref, first_far_ref)):
-        for place in range(count):
-            row = first + place * rows
-            near_ref[pl.ds((piece * count + place) * half, half), :] = ref[row : row + half, :]
-            totals.append(ref[row + half : row + rows, :].astype(F32))
+    for piece in range(4):
+        for step in range(Z_SIZE):
+            if piece == 3:
+                ref, first = gathered[6], Z_SIZE * size + step * more
+            elif step < Z_SIZE - 1:
+                ref, first = gathered[2 * piece], 3 * size + step * more
+            else:
+                ref, first = gathered[2 * piece + 1], 2 * size
+            for row in range(first, first + more, rows):
+                place = len(totals)
+                near_ref[place * half : (place + 1) * half, :] = ref[row : row + half, :]
+                totals.append(ref[row + half : row + rows, :].astype(F32))
     total = tree_sum(totals)
     scalars = total[3:4] + total[15:16]
     error_ref[...] = ((scalars[:, 1:2] + loss_ref[3:4, 2:3]) * scale).reshape(1)
@@ -1013,27 +1013,41 @@
         )
     after = yield mark
     high = dp_swap(mine, 2 * Z_STRIDE)
-    pieces = [mine, dp_swap(mine, Z_STRIDE), high, dp_swap(high, Z_STRIDE)]
+    early = (mine, dp_swap(mine, Z_STRIDE), high)
+    late = dp_swap(high, Z_STRIDE)
     half = block[0] // 2
     plan, start = [], 0
     for first, count in ((0, half), (2 * half, more), (half, half)):
-        for piece in range(Z_SIZE):
+        for piece in range(len(early)):
             if count:
                 plan.append((piece, first, count, 0, start))
             start += count
-    joined, mark = move(pieces, (start,), plan, after, mark=True, busy=1)
+    joined, mark = move(early, (start,), plan, after, mark=True, busy=1)
     along_x, along_y = dp_swap(joined, 1), dp_swap(joined, 2)
+    late_x, late_y = dp_swap(late, 1), dp_swap(late, 2)
     after = yield mark
-    share = Z_SIZE * half
+    plan = [
+        (0, 0, 3 * half, 0, 0),
+        (1, 0, half, 0, 3 * half),
+        (2, 3 * (half + more), 3 * half, 1, 0),
+        (3, half, half, 1, 3 * half),
+    ]
+    if more:
+        plan += [
+            (0, 3 * half, 3 * more, 0, 4 * half),
+            (1, 2 * half, more, 0, 4 * half + 3 * more),
+        ]
     first, second, mark = move(
-        (along_y, along_x),
-        (start - share, share),
-        ((0, 0, start - share, 0, 0), (1, start - share, share, 1, 0)),
+        (along_y, late_y, along_x, late_x),
+        (4 * (half + more), 4 * half),
+        plan,
         after,
-        mark=True, busy=1,
+        mark=True,
+        busy=1,
     )
     after = yield mark
-    yield joined, along_x, along_y, dp_swap(first, 1), dp_swap(second, 2)
+    far = (dp_swap(first, 1), dp_swap(second, 2))
+    yield (joined, late, along_x, late_x, along_y, late_y, *far)
 
 
 def block_home(index, block, outer, inner):
@@ -1043,18 +1057,18 @@
 
 
 def relative_blocks(refs, tensor):
-    joined, along_x, along_y, first_far, second_far = refs
-    size = second_far.shape[0]
-    start = joined.shape[0] - size if tensor else 0
-    if tensor:
-        pieces = ((joined, start), (along_x, start), (along_y, start), (second_far, 0))
-    else:
-        pieces = ((joined, 0), (along_y, 0), (along_x, 0), (first_far, 0))
-    rows = size // Z_SIZE
-    for piece, (ref, start) in enumerate(pieces):
+    rows = refs[7].shape[0] // Z_SIZE
+    more = refs[1].shape[0] - 2 * rows
+    for piece, early in enumerate((0, 2, 4) if tensor else (0, 4, 2)):
         for step in range(Z_SIZE):
-            first = start + step * rows
+            if step < Z_SIZE - 1:
+                ref, first = refs[early], tensor * 3 * (rows + more) + step * rows
+            else:
+                ref, first = refs[early + 1], tensor * rows
             yield piece * Z_SIZE + step, rows, ref[first : first + rows, :]
+    for step in range(Z_SIZE):
+        values = refs[6 + tensor][step * rows : (step + 1) * rows, :]
+        yield 3 * Z_SIZE + step, rows, values
 
 
 def unpack_widen_kernel(index_ref, *refs):

time: 226 us -> 223 us (0.987)
  Pallas kernels: 105 us -> 101 us
    ppermute x6, starting transfers between devices: 5.54 us -> 0.85 us  [mp_other(): return lax.ppermute(values, 'mp', [(0, 1), (1, 0)])]
    pallas_call x1, Pallas kernels: 35.2 us -> 30.9 us  [image_tower(): pl.pallas_call(image_kernel, out_shape=jax.ShapeDtypeStruct((images, widt...]
    ppermute x46 -> x50, starting transfers between devices: 64.1 us -> 67.9 us  [dp_swap(): lax.ppermute(values, 'dp', [(index, index ^ mask) for index in range(size)])]
    ppermute x46 -> x50, waiting for transfers between devices: 47.9 us -> 49.3 us  [dp_swap(): lax.ppermute(values, 'dp', [(index, index ^ mask) for index in range(size)])]
  transfers between devices with their start and end apart: 52 -> 56, of which waited for: 20 -> 18; matrix products, arithmetic and copies ran while one was open for 0% -> 0% of each run, Pallas kernels for 27% -> 28%
where the time goes in v4:
time: 223 us
  Pallas kernels  101 us (45%)
  starting transfers between devices  68.7 us (31%)
  waiting for transfers between devices  49.3 us (22%)
    pallas_call x26, Pallas kernels, call(): pl.pallas_call(body, out_shape=[jax.ShapeDtypeStruct(shape, kind) for sha...  69.7 us
    ppermute x50, starting transfers between devices, dp_swap(): lax.ppermute(values, 'dp', [(index, index ^ mask) for index in range(size)])  67.9 us
    ppermute x50, waiting for transfers between devices, dp_swap(): lax.ppermute(values, 'dp', [(index, index ^ mask) for index in range(size)])  49.3 us
    pallas_call x1, Pallas kernels, image_tower(): pl.pallas_call(image_kernel, out_shape=jax.ShapeDtypeStruct((images, widt...  30.9 us
  transfers between devices with their start and end apart: 56, of which 18 were waited for; matrix products, arithmetic and copies ran while one was open for 0% of the time, Pallas kernels for 28%

profile of v4, /device:TPU:0, one launch (start us, length us, event | category | flops | bytes accessed | tf_op | source)
XLA Modules:
  0.0 222.7 jit_solution(5503818797182699945)
XLA Ops:
  0.6 30.9 %shard_map.334.refs_7_.refs_0_ = bf16[16,768]{1,0:T(8,128)(2,1)} custom-call(s32[16]{0:T(128)} %flag_ref.1, bf16[145,16,768]{2,1,0:T(8,128)(2,1)} %bitcast.3, f32[2,768]{1,0:T(2,128)} %gain_ref.1, bf16[3,768,768]{2,1,0:T(8,128)(2,1)} %triple_hbm.1, bf16[768,768]{1,0:T(8,128)(2,1)} %result_hbm.1, bf16[768,3072]{1,0:T(8,128)(2,1)} %widen_hbm.1, ...), custom_call_target="tpu_custom_call" | custom-call | flops 999999995904 | bytes 999999995904 | tf_op jit(solution)/shard_map/pallas_call | solution.py:334
  31.5 11.2 %collective-permute-start.3 = (bf16[16,768]{1,0:T(8,128)(2,1)}, bf16[16,768]{1,0:T(8,128)(2,1)}, u32[]{:S(2)}, u32[]{:S(2)}) collective-permute-start(bf16[16,768]{1,0:T(8,128)(2,1)} %shard_map.334.refs_7_.refs_0_), channel_id=1, source_target_pairs={{0,24},{2,26},{4,28},{6,30},{8,16},{10,18},{12,20},{14,22},{16,8},... | collective-permute-start | bytes 73736 | tf_op jit(solution)/shard_map/ppermute | solution.py:29
  42.7 3.9 %collective-permute-start.2 = (bf16[16,768]{1,0:T(8,128)(2,1)}, bf16[16,768]{1,0:T(8,128)(2,1)}, u32[]{:S(2)}, u32[]{:S(2)}) collective-permute-start(bf16[16,768]{1,0:T(8,128)(2,1)} %shard_map.334.refs_7_.refs_0_), channel_id=1, source_target_pairs={{0,16},{2,18},{4,20},{6,22},{8,24},{10,26},{12,28},{14,30},{16,0},... | collective-permute-start | bytes 73736 | tf_op jit(solution)/shard_map/ppermute | solution.py:29
  47.1 6.6 %shard_map.335 = (bf16[512,768]{1,0:T(8,128)(2,1)}, bf16[3,512,384]{2,1,0:T(8,128)(2,1)}, f32[4,3,256,128]{3,2,1,0:T(8,128)}, bf16[512,384]{1,0:T(8,128)(2,1)}, f32[512,768]{1,0:T(8,128)}, /*index=5*/f32[8,128]{1,0:T(8,128)}) custom-call(bf16[512,768]{1,0:T(8,128)(2,1)} %refs_3_.5, s32[512]{0:T(512)} %refs_4_.6, f32[768]{0:T(1024)} %refs_4_.7, f32[768]{0:T(1024)} %refs_3_.3, ...), custom_call_target="tpu_custom_call" | custom-call | flops 999999995904 | bytes 999999995904 | tf_op jit(solution)/shard_map/pallas_call | solution.py:903
  56.0 2.7 %collective-permute-start.6 = (bf16[64,768]{1,0:T(8,128)(2,1)}, bf16[64,768]{1,0:T(8,128)(2,1)}, u32[]{:S(2)}, u32[]{:S(2)}) collective-permute-start(bf16[64,768]{1,0:T(8,128)(2,1)} %shard_map.336.refs_10_.refs_0_), channel_id=1, source_target_pairs={{0,6},{2,4},{4,2},{6,0},{8,14},{10,12},{12,10},{14,8},{16,22},{18,... | collective-permute-start | bytes 294920 | tf_op jit(solution)/shard_map/ppermute | solution.py:29
  60.2 6.2 %shard_map.337 = (f32[512,768]{1,0:T(8,128)S(1)}, bf16[512,768]{1,0:T(8,128)(2,1)S(1)}, f32[512,1536]{1,0:T(8,128)S(1)}, bf16[32,1536]{1,0:T(8,128)(2,1)}, f32[32,768]{1,0:T(8,128)S(1)}, /*index=5*/f32[32,768]{1,0:T(8,128)S(1)}) custom-call(bf16[512,768]{1,0:T(8,128)(2,1)S(1)} %copy-done.11, f32[512,768]{1,0:T(8,128)S(1)} %copy-done.10, ...), custom_call_target="tpu_custom_call" | custom-call | flops 999999995904 | bytes 999999995904 | tf_op jit(solution)/shard_map/pallas_call | solution.py:903
  82.9 3.7 %collective-permute-start.17 = (f32[1,512]{1,0:T(1,128)S(1)}, f32[1,512]{1,0:T(1,128)S(1)}, u32[]{:S(2)}, u32[]{:S(2)}) collective-permute-start(f32[1,512]{1,0:T(1,128)S(1)} %shard_map.341.refs_2_), channel_id=1, source_target_pairs={{0,24},{2,26},{4,28},{6,30},{8,16},{10,18},{12,20},{14,22},{16,8},... | collective-permute-start | bytes 6152 | tf_op jit(solution)/shard_map/ppermute | solution.py:29
  93.5 5.4 %shard_map.342 = (f32[32,768]{1,0:T(8,128)S(1)}, bf16[32,768]{1,0:T(8,128)(2,1)S(1)}, bf16[512,1536]{1,0:T(8,128)(2,1)S(1)}, f32[512,768]{1,0:T(8,128)}, f32[8,768]{1,0:T(8,128)S(1)}) custom-call(s32[32]{0:T(128)S(1)} %copy-done.28, f32[1]{0:T(128)S(6)} %copy.38.refs_2_.refs_1_, f32[1,512]{1,0:T(1,128)S(1)} %shard_map.341.refs_2_, ...), custom_call_target="tpu_custom_call" | custom-call | flops 999999995904 | bytes 999999995904 | tf_op jit(solution)/shard_map/pallas_call | solution.py:903
  99.0 2.5 %shard_map.343 = (bf16[384,768]{1,0:T(8,128)(2,1)}, bf16[384,768]{1,0:T(8,128)(2,1)S(1)}, bf16[384,768]{1,0:T(8,128)(2,1)}, bf16[384,768]{1,0:T(8,128)(2,1)S(1)}, f32[8,128]{1,0:T(8,128)S(1)}) custom-call(s32[1]{0:T(128)} %bitcast.refs_0_, bf16[512,768]{1,0:T(8,128)(2,1)S(1)} %get-tuple-element.112.refs_1_, bf16[512,1536]{1,0:T(8,128)(2,1)S(1)} %get-tuple-element.126.refs_2_), custom_call_target="tpu_custom_call" | custom-call | flops 999999995904 | bytes 999999995904 | tf_op jit(solution)/shard_map/pallas_call | solution.py:903
  104.7 8.7 %shard_map.344 = (f32[512,768]{1,0:T(8,128)S(1)}, bf16[512,768]{1,0:T(8,128)(2,1)S(1)}, bf16[3,512,384]{2,1,0:T(8,128)(2,1)S(1)}, f32[512,768]{1,0:T(8,128)}, f32[8,768]{1,0:T(8,128)S(1)}) custom-call(f32[512,768]{1,0:T(8,128)} %get-tuple-element.132.refs_0_, f32[512,768]{1,0:T(8,128)} %collective-permute-done.20.refs_1_, ...), custom_call_target="tpu_custom_call" | custom-call | flops 999999995904 | bytes 999999995904 | tf_op jit(solution)/shard_map/pallas_call | solution.py:903
  113.5 3.0 %shard_map.345 = (bf16[384,768]{1,0:T(8,128)(2,1)}, bf16[384,768]{1,0:T(8,128)(2,1)S(1)}, bf16[384,768]{1,0:T(8,128)(2,1)}, bf16[384,768]{1,0:T(8,128)(2,1)S(1)}, f32[8,128]{1,0:T(8,128)S(1)}) custom-call(s32[1]{0:T(128)} %bitcast.refs_0_, bf16[512,768]{1,0:T(8,128)(2,1)S(1)} %copy-done.33, bf16[3,512,384]{2,1,0:T(8,128)(2,1)S(1)} %get-tuple-element.138.refs_2_, ...), custom_call_target="tpu_custom_call" | custom-call | flops 999999995904 | bytes 999999995904 | tf_op jit(solution)/shard_map/pallas_call | solution.py:903
  124.5 5.9 %collective-permute-done.23.refs_2_ = bf16[192,768]{1,0:T(8,128)(2,1)S(1)} collective-permute-done((bf16[192,768]{1,0:T(8,128)(2,1)S(1)}, bf16[192,768]{1,0:T(8,128)(2,1)S(1)}, u32[]{:S(2)}, u32[]{:S(2)}) %collective-permute-start.23) | collective-permute-done | bytes 294944 | tf_op jit(solution)/shard_map/ppermute | solution.py:29
  132.7 4.4 %collective-permute-start.27 = (bf16[96,768]{1,0:T(8,128)(2,1)}, bf16[96,768]{1,0:T(8,128)(2,1)}, u32[]{:S(2)}, u32[]{:S(2)}) collective-permute-start(bf16[96,768]{1,0:T(8,128)(2,1)} %get-tuple-element.151), channel_id=1, source_target_pairs={{0,24},{2,26},{4,28},{6,30},{8,16},{10,18},{12,20},{14,22},{16,8},... | collective-permute-start | bytes 442376 | tf_op jit(solution)/shard_map/ppermute | solution.py:29
  137.1 4.2 %shard_map.348 = (f32[512,768]{1,0:T(8,128)}, bf16[32,768]{1,0:T(8,128)(2,1)S(1)}) custom-call(s32[1]{0:T(128)} %bitcast.2.refs_0_, f32[512,768]{1,0:T(8,128)} %get-tuple-element.152.refs_1_, f32[512,768]{1,0:T(8,128)} %collective-permute-done.28.refs_2_, bf16[512,768]{1,0:T(8,128)(2,1)S(1)} %copy-done.12, f32[768]{0:T(1024)S(1)} %copy-done.25, ...), custom_call_target="tpu_custom_call" | custom-call | flops 999999995904 | bytes 999999995904 | tf_op jit(solution)/shard_map/pallas_call | solution.py:903
  147.2 4.1 %collective-permute-done.33.refs_2_ = bf16[192,768]{1,0:T(8,128)(2,1)S(1)} collective-permute-done((bf16[192,768]{1,0:T(8,128)(2,1)S(1)}, bf16[192,768]{1,0:T(8,128)(2,1)S(1)}, u32[]{:S(2)}, u32[]{:S(2)}) %collective-permute-start.33) | collective-permute-done | bytes 294944 | tf_op jit(solution)/shard_map/ppermute | solution.py:29
  151.7 4.3 %collective-permute-done.32.refs_2_ = bf16[128,768]{1,0:T(8,128)(2,1)S(1)} collective-permute-done((bf16[128,768]{1,0:T(8,128)(2,1)S(1)}, bf16[128,768]{1,0:T(8,128)(2,1)S(1)}, u32[]{:S(2)}, u32[]{:S(2)}) %collective-permute-start.32) | collective-permute-done | bytes 196640 | tf_op jit(solution)/shard_map/ppermute | solution.py:29
  160.8 6.4 %collective-permute-done.35.refs_1_.refs_2_ = bf16[128,768]{1,0:T(8,128)(2,1)S(1)} collective-permute-done((bf16[128,768]{1,0:T(8,128)(2,1)S(1)}, bf16[128,768]{1,0:T(8,128)(2,1)S(1)}, u32[]{:S(2)}, u32[]{:S(2)}) %collective-permute-start.35) | collective-permute-done | bytes 196640 | tf_op jit(solution)/shard_map/ppermute | solution.py:29
  169.8 8.6 %collective-permute-done.42.refs_3_ = bf16[96,768]{1,0:T(8,128)(2,1)S(1)} collective-permute-done((bf16[96,768]{1,0:T(8,128)(2,1)S(1)}, bf16[96,768]{1,0:T(8,128)(2,1)S(1)}, u32[]{:S(2)}, u32[]{:S(2)}) %collective-permute-start.42) | collective-permute-done | bytes 147488 | tf_op jit(solution)/shard_map/ppermute | solution.py:29
  179.2 2.6 %collective-permute-start.46 = (bf16[96,768]{1,0:T(8,128)(2,1)S(1)}, bf16[96,768]{1,0:T(8,128)(2,1)S(1)}, u32[]{:S(2)}, u32[]{:S(2)}) collective-permute-start(bf16[96,768]{1,0:T(8,128)(2,1)S(1)} %get-tuple-element.180.refs_0_), channel_id=1, source_target_pairs={{0,16},{2,18},{4,20},{6,22},{8,24},{10,26},{12,28},{14,30},{16,0},... | collective-permute-start | bytes 442376 | tf_op jit(solution)/shard_map/ppermute | solution.py:29
  181.8 4.9 %collective-permute-done.46.refs_2_ = bf16[96,768]{1,0:T(8,128)(2,1)S(1)} collective-permute-done((bf16[96,768]{1,0:T(8,128)(2,1)S(1)}, bf16[96,768]{1,0:T(8,128)(2,1)S(1)}, u32[]{:S(2)}, u32[]{:S(2)}) %collective-permute-start.46) | collective-permute-done | bytes 147488 | tf_op jit(solution)/shard_map/ppermute | solution.py:29
  189.6 3.4 %collective-permute-done.47.refs_2_ = bf16[96,768]{1,0:T(8,128)(2,1)} collective-permute-done((bf16[96,768]{1,0:T(8,128)(2,1)S(1)}, bf16[96,768]{1,0:T(8,128)(2,1)}, u32[]{:S(2)}, u32[]{:S(2)}) %collective-permute-start.47) | collective-permute-done | bytes 147488 | tf_op jit(solution)/shard_map/ppermute | solution.py:29
  199.9 5.1 %shard_map.357 = (f32[768,1536]{1,0:T(8,128)}, f32[8,128]{1,0:T(8,128)}) custom-call(s32[1]{0:T(128)} %bitcast.refs_0_, bf16[384,768]{1,0:T(8,128)(2,1)} %copy-done.14, bf16[128,768]{1,0:T(8,128)(2,1)} %copy-done.17, bf16[384,768]{1,0:T(8,128)(2,1)} %copy-done.1, bf16[128,768]{1,0:T(8,128)(2,1)} %copy-done.3, bf16[384,768]{1,0:T(8,128)(2,1)} %copy-done, ...), custom_call_target="tpu_custom_call" | custom-call | flops 999999995904 | bytes 999999995904 | tf_op jit(solution)/shard_map/pallas_call | solution.py:903
  210.7 6.7 %shard_map.359 = (f32[1536,768]{1,0:T(8,128)}, f32[8,128]{1,0:T(8,128)S(1)}) custom-call(s32[1]{0:T(128)} %bitcast.2.refs_0_, bf16[128,1536]{1,0:T(8,128)(2,1)} %get-tuple-element.141.refs_1_, bf16[128,1536]{1,0:T(8,128)(2,1)} %collective-permute-done.21.refs_5_.refs_2_, bf16[128,1536]{1,0:T(8,128)(2,1)} %collective-permute-done.22.refs_6_.refs_3_, ...), custom_call_target="tpu_custom_call" | custom-call | flops 999999995904 | bytes 999999995904 | tf_op jit(solution)/shard_map/pallas_call | solution.py:903
  218.1 4.7 %shard_map.360 = (f32[3,768,384]{2,1,0:T(8,128)}, f32[384,768]{1,0:T(8,128)}) custom-call(s32[1]{0:T(128)} %bitcast.refs_0_, bf16[288,768]{1,0:T(8,128)(2,1)} %get-tuple-element.185.refs_1_, bf16[96,768]{1,0:T(8,128)(2,1)} %collective-permute-done.47.refs_2_, bf16[288,768]{1,0:T(8,128)(2,1)} %collective-permute-done.48.refs_2_.refs_3_, ...), custom_call_target="tpu_custom_call" | custom-call | flops 999999995904 | bytes 999999995904 | tf_op jit(solution)/shard_map/pallas_call | solution.py:903
  (194 shorter events, 70.7 us)
Async XLA Ops:
  31.5 22.2 %collective-permute-start.3 = (bf16[16,768]{1,0:T(8,128)(2,1)}, bf16[16,768]{1,0:T(8,128)(2,1)}, u32[]{:S(2)}, u32[]{:S(2)}) collective-permute-start(bf16[16,768]{1,0:T(8,128)(2,1)} %shard_map.334.refs_7_.refs_0_), channel_id=1, source_target_pairs={{0,24},{2,26},{4,28},{6,30},{8,16},{10,18},{12,20},{14,22},{16,8},... | collective-permute-start | bytes 73736 | tf_op jit(solution)/shard_map/ppermute | solution.py:29
  42.7 11.0 %collective-permute-start.2 = (bf16[16,768]{1,0:T(8,128)(2,1)}, bf16[16,768]{1,0:T(8,128)(2,1)}, u32[]{:S(2)}, u32[]{:S(2)}) collective-permute-start(bf16[16,768]{1,0:T(8,128)(2,1)} %shard_map.334.refs_7_.refs_0_), channel_id=1, source_target_pairs={{0,16},{2,18},{4,20},{6,22},{8,24},{10,26},{12,28},{14,30},{16,0},... | collective-permute-start | bytes 73736 | tf_op jit(solution)/shard_map/ppermute | solution.py:29
  56.0 10.3 %collective-permute-start.6 = (bf16[64,768]{1,0:T(8,128)(2,1)}, bf16[64,768]{1,0:T(8,128)(2,1)}, u32[]{:S(2)}, u32[]{:S(2)}) collective-permute-start(bf16[64,768]{1,0:T(8,128)(2,1)} %shard_map.336.refs_10_.refs_0_), channel_id=1, source_target_pairs={{0,6},{2,4},{4,2},{6,0},{8,14},{10,12},{12,10},{14,8},{16,22},{18,... | collective-permute-start | bytes 294920 | tf_op jit(solution)/shard_map/ppermute | solution.py:29
  87.3 26.2 %collective-permute-start.22 = (bf16[128,1536]{1,0:T(8,128)(2,1)}, bf16[128,1536]{1,0:T(8,128)(2,1)}, u32[]{:S(2)}, u32[]{:S(2)}) collective-permute-start(bf16[128,1536]{1,0:T(8,128)(2,1)} %get-tuple-element.141.refs_1_), channel_id=1, source_target_pairs={{0,16},{2,18},{4,20},{6,22},{8,24},{10,26},{12,28},{14,30},{16,0},... | collective-permute-start | bytes 1179656 | tf_op jit(solution)/shard_map/ppermute | solution.py:29
  89.6 23.9 %collective-permute-start.21 = (bf16[128,1536]{1,0:T(8,128)(2,1)}, bf16[128,1536]{1,0:T(8,128)(2,1)}, u32[]{:S(2)}, u32[]{:S(2)}) collective-permute-start(bf16[128,1536]{1,0:T(8,128)(2,1)} %get-tuple-element.141.refs_1_), channel_id=1, source_target_pairs={{0,8},{2,10},{4,12},{6,14},{8,0},{10,2},{12,4},{14,6},{16,24},{18,... | collective-permute-start | bytes 1179656 | tf_op jit(solution)/shard_map/ppermute | solution.py:29
  101.5 16.0 %collective-permute-start.18 = (bf16[384,768]{1,0:T(8,128)(2,1)}, bf16[384,768]{1,0:T(8,128)(2,1)}, u32[]{:S(2)}, u32[]{:S(2)}) collective-permute-start(bf16[384,768]{1,0:T(8,128)(2,1)} %get-tuple-element.128), channel_id=1, source_target_pairs={{0,2},{2,0},{4,6},{6,4},{8,10},{10,8},{12,14},{14,12},{16,18},{18,... | collective-permute-start | bytes 1769480 | tf_op jit(solution)/shard_map/ppermute | solution.py:29
  103.1 15.7 %collective-permute-start.19 = (bf16[384,768]{1,0:T(8,128)(2,1)}, bf16[384,768]{1,0:T(8,128)(2,1)}, u32[]{:S(2)}, u32[]{:S(2)}) collective-permute-start(bf16[384,768]{1,0:T(8,128)(2,1)} %get-tuple-element.130), channel_id=1, source_target_pairs={{0,4},{2,6},{4,0},{6,2},{8,12},{10,14},{12,8},{14,10},{16,20},{18,... | collective-permute-start | bytes 1769480 | tf_op jit(solution)/shard_map/ppermute | solution.py:29
  113.4 19.3 %collective-permute-start.28 = (f32[512,768]{1,0:T(8,128)}, f32[512,768]{1,0:T(8,128)}, u32[]{:S(2)}, u32[]{:S(2)}) collective-permute-start(f32[512,768]{1,0:T(8,128)} %get-tuple-element.152.refs_1_), channel_id=1, source_target_pairs={{0,1},{1,0},{2,3},{3,2},{4,5},{5,4},{6,7},{7,6},{8,9},{9,8},{10,11... | collective-permute-start | bytes 4718600 | tf_op jit(solution)/shard_map/ppermute | solution.py:24
  120.4 10.0 %collective-permute-start.23 = (bf16[192,768]{1,0:T(8,128)(2,1)S(1)}, bf16[192,768]{1,0:T(8,128)(2,1)S(1)}, u32[]{:S(2)}, u32[]{:S(2)}) collective-permute-start(bf16[192,768]{1,0:T(8,128)(2,1)S(1)} %get-tuple-element.144), channel_id=1, source_target_pairs={{0,4},{2,6},{4,0},{6,2},{8,12},{10,14},{12,8},{14,10},{16,20},{18,... | collective-permute-start | bytes 884744 | tf_op jit(solution)/shard_map/ppermute | solution.py:29
  122.0 9.9 %collective-permute-start.24 = (bf16[192,768]{1,0:T(8,128)(2,1)S(1)}, bf16[192,768]{1,0:T(8,128)(2,1)S(1)}, u32[]{:S(2)}, u32[]{:S(2)}) collective-permute-start(bf16[192,768]{1,0:T(8,128)(2,1)S(1)} %get-tuple-element.146), channel_id=1, source_target_pairs={{0,2},{2,0},{4,6},{6,4},{8,10},{10,8},{12,14},{14,12},{16,18},{18,... | collective-permute-start | bytes 884744 | tf_op jit(solution)/shard_map/ppermute | solution.py:29
  122.2 20.4 %collective-permute-start.29 = (bf16[384,768]{1,0:T(8,128)(2,1)}, bf16[384,768]{1,0:T(8,128)(2,1)}, u32[]{:S(2)}, u32[]{:S(2)}) collective-permute-start(bf16[384,768]{1,0:T(8,128)(2,1)} %get-tuple-element.160), channel_id=1, source_target_pairs={{0,2},{2,0},{4,6},{6,4},{8,10},{10,8},{12,14},{14,12},{16,18},{18,... | collective-permute-start | bytes 1769480 | tf_op jit(solution)/shard_map/ppermute | solution.py:29
  124.0 18.7 %collective-permute-start.30 = (bf16[384,768]{1,0:T(8,128)(2,1)}, bf16[384,768]{1,0:T(8,128)(2,1)}, u32[]{:S(2)}, u32[]{:S(2)}) collective-permute-start(bf16[384,768]{1,0:T(8,128)(2,1)} %get-tuple-element.162), channel_id=1, source_target_pairs={{0,4},{2,6},{4,0},{6,2},{8,12},{10,14},{12,8},{14,10},{16,20},{18,... | collective-permute-start | bytes 1769480 | tf_op jit(solution)/shard_map/ppermute | solution.py:29
  132.7 12.6 %collective-permute-start.25 = (bf16[96,768]{1,0:T(8,128)(2,1)}, bf16[96,768]{1,0:T(8,128)(2,1)}, u32[]{:S(2)}, u32[]{:S(2)}) collective-permute-start(bf16[96,768]{1,0:T(8,128)(2,1)} %get-tuple-element.149), channel_id=1, source_target_pairs={{0,8},{2,10},{4,12},{6,14},{8,0},{10,2},{12,4},{14,6},{16,24},{18,... | collective-permute-start | bytes 442376 | tf_op jit(solution)/shard_map/ppermute | solution.py:29
  132.7 12.6 %collective-permute-start.26 = (bf16[96,768]{1,0:T(8,128)(2,1)}, bf16[96,768]{1,0:T(8,128)(2,1)}, u32[]{:S(2)}, u32[]{:S(2)}) collective-permute-start(bf16[96,768]{1,0:T(8,128)(2,1)} %get-tuple-element.150), channel_id=1, source_target_pairs={{0,16},{2,18},{4,20},{6,22},{8,24},{10,26},{12,28},{14,30},{16,0},... | collective-permute-start | bytes 442376 | tf_op jit(solution)/shard_map/ppermute | solution.py:29
  132.7 12.6 %collective-permute-start.27 = (bf16[96,768]{1,0:T(8,128)(2,1)}, bf16[96,768]{1,0:T(8,128)(2,1)}, u32[]{:S(2)}, u32[]{:S(2)}) collective-permute-start(bf16[96,768]{1,0:T(8,128)(2,1)} %get-tuple-element.151), channel_id=1, source_target_pairs={{0,24},{2,26},{4,28},{6,30},{8,16},{10,18},{12,20},{14,22},{16,8},... | collective-permute-start | bytes 442376 | tf_op jit(solution)/shard_map/ppermute | solution.py:29
  156.0 22.5 %collective-permute-start.38 = (bf16[384,768]{1,0:T(8,128)(2,1)S(1)}, bf16[384,768]{1,0:T(8,128)(2,1)S(1)}, u32[]{:S(2)}, u32[]{:S(2)}) collective-permute-start(bf16[384,768]{1,0:T(8,128)(2,1)S(1)} %get-tuple-element.171.refs_0_.refs_1_), channel_id=1, source_target_pairs={{0,4},{2,6},{4,0},{6,2},{8,12},{10,14},{12,8},{14,10},{16,20},{18,... | collective-permute-start | bytes 1769480 | tf_op jit(solution)/shard_map/ppermute | solution.py:29
  157.2 21.4 %collective-permute-start.36 = (bf16[384,768]{1,0:T(8,128)(2,1)S(1)}, bf16[384,768]{1,0:T(8,128)(2,1)S(1)}, u32[]{:S(2)}, u32[]{:S(2)}) collective-permute-start(bf16[384,768]{1,0:T(8,128)(2,1)S(1)} %get-tuple-element.171.refs_0_.refs_1_), channel_id=1, source_target_pairs={{0,2},{2,0},{4,6},{6,4},{8,10},{10,8},{12,14},{14,12},{16,18},{18,... | collective-permute-start | bytes 1769480 | tf_op jit(solution)/shard_map/ppermute | solution.py:29
  158.5 10.3 %collective-permute-start.40 = (bf16[96,768]{1,0:T(8,128)(2,1)S(1)}, bf16[96,768]{1,0:T(8,128)(2,1)S(1)}, u32[]{:S(2)}, u32[]{:S(2)}) collective-permute-start(bf16[96,768]{1,0:T(8,128)(2,1)S(1)} %get-tuple-element.173), channel_id=1, source_target_pairs={{0,8},{2,10},{4,12},{6,14},{8,0},{10,2},{12,4},{14,6},{16,24},{18,... | collective-permute-start | bytes 442376 | tf_op jit(solution)/shard_map/ppermute | solution.py:29
  167.2 11.3 %collective-permute-start.39 = (bf16[128,768]{1,0:T(8,128)(2,1)S(1)}, bf16[128,768]{1,0:T(8,128)(2,1)S(1)}, u32[]{:S(2)}, u32[]{:S(2)}) collective-permute-start(bf16[128,768]{1,0:T(8,128)(2,1)S(1)} %collective-permute-done.35.refs_1_.refs_2_), channel_id=1, source_target_pairs={{0,4},{2,6},{4,0},{6,2},{8,12},{10,14},{12,8},{14,10},{16,20},{18,... | collective-permute-start | bytes 589832 | tf_op jit(solution)/shard_map/ppermute | solution.py:29
  178.7 18.5 %collective-permute-start.43 = (bf16[320,768]{1,0:T(8,128)(2,1)S(1)}, bf16[320,768]{1,0:T(8,128)(2,1)S(1)}, u32[]{:S(2)}, u32[]{:S(2)}) collective-permute-start(bf16[320,768]{1,0:T(8,128)(2,1)S(1)} %get-tuple-element.178), channel_id=1, source_target_pairs={{0,2},{2,0},{4,6},{6,4},{8,10},{10,8},{12,14},{14,12},{16,18},{18,... | collective-permute-start | bytes 1474568 | tf_op jit(solution)/shard_map/ppermute | solution.py:29
  181.8 14.5 %collective-permute-start.44 = (bf16[192,768]{1,0:T(8,128)(2,1)S(1)}, bf16[192,768]{1,0:T(8,128)(2,1)S(1)}, u32[]{:S(2)}, u32[]{:S(2)}) collective-permute-start(bf16[192,768]{1,0:T(8,128)(2,1)S(1)} %get-tuple-element.179), channel_id=1, source_target_pairs={{0,4},{2,6},{4,0},{6,2},{8,12},{10,14},{12,8},{14,10},{16,20},{18,... | collective-permute-start | bytes 884744 | tf_op jit(solution)/shard_map/ppermute | solution.py:29
  188.7 22.0 %collective-permute-start.54 = (bf16[128,1536]{1,0:T(8,128)(2,1)}, bf16[128,1536]{1,0:T(8,128)(2,1)}, u32[]{:S(2)}, u32[]{:S(2)}) collective-permute-start(bf16[128,1536]{1,0:T(8,128)(2,1)} %collective-permute-done.22.refs_6_.refs_3_), channel_id=1, source_target_pairs={{0,8},{2,10},{4,12},{6,14},{8,0},{10,2},{12,4},{14,6},{16,24},{18,... | collective-permute-start | bytes 1179656 | tf_op jit(solution)/shard_map/ppermute | solution.py:29
  194.5 10.5 %collective-permute-start.49 = (bf16[96,768]{1,0:T(8,128)(2,1)}, bf16[96,768]{1,0:T(8,128)(2,1)}, u32[]{:S(2)}, u32[]{:S(2)}) collective-permute-start(bf16[96,768]{1,0:T(8,128)(2,1)} %collective-permute-done.47.refs_2_), channel_id=1, source_target_pairs={{0,2},{2,0},{4,6},{6,4},{8,10},{10,8},{12,14},{14,12},{16,18},{18,... | collective-permute-start | bytes 442376 | tf_op jit(solution)/shard_map/ppermute | solution.py:29
  199.8 10.9 %collective-permute-start.55 = (bf16[256,768]{1,0:T(8,128)(2,1)}, bf16[256,768]{1,0:T(8,128)(2,1)}, u32[]{:S(2)}, u32[]{:S(2)}) collective-permute-start(bf16[256,768]{1,0:T(8,128)(2,1)} %get-tuple-element.189.refs_5_), channel_id=1, source_target_pairs={{0,1},{1,0},{2,3},{3,2},{4,5},{5,4},{6,7},{7,6},{8,9},{9,8},{10,11... | collective-permute-start | bytes 1179656 | tf_op jit(solution)/shard_map/ppermute | solution.py:24
  (71 other events, 613.0 us)

commit v5 on v4

--- a/solution.py
+++ b/solution.py
@@ -1227,7 +1227,11 @@
         index=(place, core),
         small=(matched_picture_ids, sharpening_log),
     )
-    after = (unit,)
+    col_parts = dp_parts(col_sum, steps[0])
+    for step in steps[1:]:
+        (col_sum,) = call(sum_kernel, col_parts, ((col_sum.shape, F32),))
+        col_parts = dp_parts(col_sum, step)
+    after = (col_sum,)
     for step in steps[2:] + [None]:
         rows = sums_parts[0].shape[0]
         joined_sums, mark = move(
@@ -1243,10 +1247,6 @@
     sums_high = dp_swap(joined_sums, 2 * Z_STRIDE)
     sums_parts = [joined_sums, dp_swap(joined_sums, Z_STRIDE), sums_high]
     sums_parts.append(dp_swap(sums_high, Z_STRIDE))
-    col_parts = dp_parts(col_sum, steps[0])
-    for step in steps[1:]:
-        (col_sum,) = call(sum_kernel, col_parts, ((col_sum.shape, F32),), after=after)
-        col_parts = dp_parts(col_sum, step)
     grad_caption, grad_caption_low, grad_pre, part, loss_stat = call(
         loss_grad_kernel,
         (
@@ -1268,6 +1268,7 @@
             ((8, model_width), F32),
         ),
         outside=(narrowing_matrix, slope, widening_matrix),
+        after=after,
         small=(matched_picture_ids, sharpening_log),
     )
 

time: 223 us -> 222 us (level)
  waiting for transfers between devices: 49.3 us -> 43.7 us
  starting transfers between devices: 68.7 us -> 72.5 us
    ppermute x50, waiting for transfers between devices: 49.3 us -> 42.8 us  [dp_swap(): lax.ppermute(values, 'dp', [(index, index ^ mask) for index in range(size)])]
    ppermute x50, starting transfers between devices: 67.9 us -> 71.6 us  [dp_swap(): lax.ppermute(values, 'dp', [(index, index ^ mask) for index in range(size)])]
  transfers between devices with their start and end apart: 56 -> 56, of which waited for: 18 -> 17; matrix products, arithmetic and copies ran while one was open for 0% -> 0% of each run, Pallas kernels for 28% -> 28%
where the time goes in v5:
time: 222 us; the launch traced here: 220 us
  Pallas kernels  99.6 us (45%)
  starting transfers between devices  72.5 us (33%)
  waiting for transfers between devices  43.7 us (20%)
    ppermute x50, starting transfers between devices, dp_swap(): lax.ppermute(values, 'dp', [(index, index ^ mask) for index in range(size)])  71.6 us
    pallas_call x26, Pallas kernels, call(): pl.pallas_call(body, out_shape=[jax.ShapeDtypeStruct(shape, kind) for sha...  69.2 us
    ppermute x50, waiting for transfers between devices, dp_swap(): lax.ppermute(values, 'dp', [(index, index ^ mask) for index in range(size)])  42.8 us
    pallas_call x1, Pallas kernels, image_tower(): pl.pallas_call(image_kernel, out_shape=jax.ShapeDtypeStruct((images, widt...  30.3 us
  transfers between devices with their start and end apart: 56, of which 17 were waited for; matrix products, arithmetic and copies ran while one was open for 0% of the time, Pallas kernels for 28%

profile of v5, /device:TPU:0, one launch (start us, length us, event | category | flops | bytes accessed | tf_op | source)
XLA Modules:
  0.0 219.9 jit_solution(14347025442467456749)
XLA Ops:
  0.6 30.3 %shard_map.334.refs_7_.refs_0_ = bf16[16,768]{1,0:T(8,128)(2,1)} custom-call(s32[16]{0:T(128)} %flag_ref.1, bf16[145,16,768]{2,1,0:T(8,128)(2,1)} %bitcast.3, f32[2,768]{1,0:T(2,128)} %gain_ref.1, bf16[3,768,768]{2,1,0:T(8,128)(2,1)} %triple_hbm.1, bf16[768,768]{1,0:T(8,128)(2,1)} %result_hbm.1, bf16[768,3072]{1,0:T(8,128)(2,1)} %widen_hbm.1, ...), custom_call_target="tpu_custom_call" | custom-call | flops 999999995904 | bytes 999999995904 | tf_op jit(solution)/shard_map/pallas_call | solution.py:334
  31.0 16.0 %collective-permute-start.3 = (bf16[16,768]{1,0:T(8,128)(2,1)}, bf16[16,768]{1,0:T(8,128)(2,1)}, u32[]{:S(2)}, u32[]{:S(2)}) collective-permute-start(bf16[16,768]{1,0:T(8,128)(2,1)} %shard_map.334.refs_7_.refs_0_), channel_id=1, source_target_pairs={{0,24},{2,26},{4,28},{6,30},{8,16},{10,18},{12,20},{14,22},{16,8},... | collective-permute-start | bytes 73736 | tf_op jit(solution)/shard_map/ppermute | solution.py:29
  47.7 6.6 %shard_map.335 = (bf16[512,768]{1,0:T(8,128)(2,1)}, bf16[3,512,384]{2,1,0:T(8,128)(2,1)}, f32[4,3,256,128]{3,2,1,0:T(8,128)}, bf16[512,384]{1,0:T(8,128)(2,1)}, f32[512,768]{1,0:T(8,128)}, /*index=5*/f32[8,128]{1,0:T(8,128)}) custom-call(bf16[512,768]{1,0:T(8,128)(2,1)} %refs_3_.5, s32[512]{0:T(512)} %refs_4_.6, f32[768]{0:T(1024)} %refs_4_.7, f32[768]{0:T(1024)} %refs_3_.3, ...), custom_call_target="tpu_custom_call" | custom-call | flops 999999995904 | bytes 999999995904 | tf_op jit(solution)/shard_map/pallas_call | solution.py:903
  60.2 6.2 %shard_map.337 = (f32[512,768]{1,0:T(8,128)S(1)}, bf16[512,768]{1,0:T(8,128)(2,1)S(1)}, f32[512,1536]{1,0:T(8,128)S(1)}, bf16[32,1536]{1,0:T(8,128)(2,1)}, f32[32,768]{1,0:T(8,128)S(1)}, /*index=5*/f32[32,768]{1,0:T(8,128)S(1)}) custom-call(bf16[512,768]{1,0:T(8,128)(2,1)S(1)} %copy-done.11, f32[512,768]{1,0:T(8,128)S(1)} %copy-done.10, ...), custom_call_target="tpu_custom_call" | custom-call | flops 999999995904 | bytes 999999995904 | tf_op jit(solution)/shard_map/pallas_call | solution.py:903
  79.2 3.7 %collective-permute-start.14 = (f32[1,512]{1,0:T(1,128)}, f32[1,512]{1,0:T(1,128)}, u32[]{:S(2)}, u32[]{:S(2)}) collective-permute-start(f32[1,512]{1,0:T(1,128)} %shard_map.340.refs_4_.refs_2_), channel_id=1, source_target_pairs={{0,24},{2,26},{4,28},{6,30},{8,16},{10,18},{12,20},{14,22},{16,8},... | collective-permute-start | bytes 6152 | tf_op jit(solution)/shard_map/ppermute | solution.py:29
  85.6 2.3 %collective-permute-start.22 = (bf16[128,1536]{1,0:T(8,128)(2,1)}, bf16[128,1536]{1,0:T(8,128)(2,1)}, u32[]{:S(2)}, u32[]{:S(2)}) collective-permute-start(bf16[128,1536]{1,0:T(8,128)(2,1)} %get-tuple-element.141.refs_1_), channel_id=1, source_target_pairs={{0,16},{2,18},{4,20},{6,22},{8,24},{10,26},{12,28},{14,30},{16,0},... | collective-permute-start | bytes 1179656 | tf_op jit(solution)/shard_map/ppermute | solution.py:29
  89.9 5.5 %shard_map.342 = (f32[32,768]{1,0:T(8,128)S(1)}, bf16[32,768]{1,0:T(8,128)(2,1)S(1)}, bf16[512,1536]{1,0:T(8,128)(2,1)S(1)}, f32[512,768]{1,0:T(8,128)}, f32[8,768]{1,0:T(8,128)S(1)}) custom-call(s32[32]{0:T(128)S(1)} %copy-done.28, f32[1]{0:T(128)S(6)} %copy.38.refs_2_.refs_1_, f32[1,512]{1,0:T(1,128)} %shard_map.340.refs_4_.refs_2_, ...), custom_call_target="tpu_custom_call" | custom-call | flops 999999995904 | bytes 999999995904 | tf_op jit(solution)/shard_map/pallas_call | solution.py:903
  95.6 2.5 %shard_map.343 = (bf16[384,768]{1,0:T(8,128)(2,1)}, bf16[384,768]{1,0:T(8,128)(2,1)S(1)}, bf16[384,768]{1,0:T(8,128)(2,1)}, bf16[384,768]{1,0:T(8,128)(2,1)S(1)}, f32[8,128]{1,0:T(8,128)S(1)}) custom-call(s32[1]{0:T(128)} %bitcast.refs_0_, bf16[512,768]{1,0:T(8,128)(2,1)S(1)} %get-tuple-element.112.refs_1_, bf16[512,1536]{1,0:T(8,128)(2,1)S(1)} %get-tuple-element.126.refs_2_), custom_call_target="tpu_custom_call" | custom-call | flops 999999995904 | bytes 999999995904 | tf_op jit(solution)/shard_map/pallas_call | solution.py:903
  100.7 8.7 %shard_map.344 = (f32[512,768]{1,0:T(8,128)S(1)}, bf16[512,768]{1,0:T(8,128)(2,1)S(1)}, bf16[3,512,384]{2,1,0:T(8,128)(2,1)S(1)}, f32[512,768]{1,0:T(8,128)}, f32[8,768]{1,0:T(8,128)S(1)}) custom-call(f32[512,768]{1,0:T(8,128)} %get-tuple-element.132.refs_0_, f32[512,768]{1,0:T(8,128)} %collective-permute-done.20.refs_1_, ...), custom_call_target="tpu_custom_call" | custom-call | flops 999999995904 | bytes 999999995904 | tf_op jit(solution)/shard_map/pallas_call | solution.py:903
  109.6 3.0 %shard_map.345 = (bf16[384,768]{1,0:T(8,128)(2,1)}, bf16[384,768]{1,0:T(8,128)(2,1)S(1)}, bf16[384,768]{1,0:T(8,128)(2,1)}, bf16[384,768]{1,0:T(8,128)(2,1)S(1)}, f32[8,128]{1,0:T(8,128)S(1)}) custom-call(s32[1]{0:T(128)} %bitcast.refs_0_, bf16[512,768]{1,0:T(8,128)(2,1)S(1)} %copy-done.33, bf16[3,512,384]{2,1,0:T(8,128)(2,1)S(1)} %get-tuple-element.138.refs_2_, ...), custom_call_target="tpu_custom_call" | custom-call | flops 999999995904 | bytes 999999995904 | tf_op jit(solution)/shard_map/pallas_call | solution.py:903
  120.3 5.9 %collective-permute-done.23.refs_2_ = bf16[192,768]{1,0:T(8,128)(2,1)S(1)} collective-permute-done((bf16[192,768]{1,0:T(8,128)(2,1)S(1)}, bf16[192,768]{1,0:T(8,128)(2,1)S(1)}, u32[]{:S(2)}, u32[]{:S(2)}) %collective-permute-start.23) | collective-permute-done | bytes 294944 | tf_op jit(solution)/shard_map/ppermute | solution.py:29
  130.4 2.8 %collective-permute-start.27 = (bf16[96,768]{1,0:T(8,128)(2,1)}, bf16[96,768]{1,0:T(8,128)(2,1)}, u32[]{:S(2)}, u32[]{:S(2)}) collective-permute-start(bf16[96,768]{1,0:T(8,128)(2,1)} %get-tuple-element.151), channel_id=1, source_target_pairs={{0,24},{2,26},{4,28},{6,30},{8,16},{10,18},{12,20},{14,22},{16,8},... | collective-permute-start | bytes 442376 | tf_op jit(solution)/shard_map/ppermute | solution.py:29
  133.2 4.2 %shard_map.348 = (f32[512,768]{1,0:T(8,128)}, bf16[32,768]{1,0:T(8,128)(2,1)S(1)}) custom-call(s32[1]{0:T(128)} %bitcast.2.refs_0_, f32[512,768]{1,0:T(8,128)} %get-tuple-element.152.refs_1_, f32[512,768]{1,0:T(8,128)} %collective-permute-done.28.refs_2_, bf16[512,768]{1,0:T(8,128)(2,1)S(1)} %copy-done.12, f32[768]{0:T(1024)S(1)} %copy-done.25, ...), custom_call_target="tpu_custom_call" | custom-call | flops 999999995904 | bytes 999999995904 | tf_op jit(solution)/shard_map/pallas_call | solution.py:903
  144.6 2.7 %collective-permute-done.33.refs_2_ = bf16[192,768]{1,0:T(8,128)(2,1)S(1)} collective-permute-done((bf16[192,768]{1,0:T(8,128)(2,1)S(1)}, bf16[192,768]{1,0:T(8,128)(2,1)S(1)}, u32[]{:S(2)}, u32[]{:S(2)}) %collective-permute-start.33) | collective-permute-done | bytes 294944 | tf_op jit(solution)/shard_map/ppermute | solution.py:29
  148.1 4.3 %collective-permute-done.32.refs_2_ = bf16[128,768]{1,0:T(8,128)(2,1)S(1)} collective-permute-done((bf16[128,768]{1,0:T(8,128)(2,1)S(1)}, bf16[128,768]{1,0:T(8,128)(2,1)S(1)}, u32[]{:S(2)}, u32[]{:S(2)}) %collective-permute-start.32) | collective-permute-done | bytes 196640 | tf_op jit(solution)/shard_map/ppermute | solution.py:29
  157.4 6.9 %collective-permute-done.35.refs_1_.refs_2_ = bf16[128,768]{1,0:T(8,128)(2,1)S(1)} collective-permute-done((bf16[128,768]{1,0:T(8,128)(2,1)S(1)}, bf16[128,768]{1,0:T(8,128)(2,1)S(1)}, u32[]{:S(2)}, u32[]{:S(2)}) %collective-permute-start.35) | collective-permute-done | bytes 196640 | tf_op jit(solution)/shard_map/ppermute | solution.py:29
  168.8 5.3 %collective-permute-done.42.refs_3_ = bf16[96,768]{1,0:T(8,128)(2,1)S(1)} collective-permute-done((bf16[96,768]{1,0:T(8,128)(2,1)S(1)}, bf16[96,768]{1,0:T(8,128)(2,1)S(1)}, u32[]{:S(2)}, u32[]{:S(2)}) %collective-permute-start.42) | collective-permute-done | bytes 147488 | tf_op jit(solution)/shard_map/ppermute | solution.py:29
  175.7 2.1 collective-permute-start.44
  177.9 4.4 %collective-permute-done.46.refs_2_ = bf16[96,768]{1,0:T(8,128)(2,1)S(1)} collective-permute-done((bf16[96,768]{1,0:T(8,128)(2,1)S(1)}, bf16[96,768]{1,0:T(8,128)(2,1)S(1)}, u32[]{:S(2)}, u32[]{:S(2)}) %collective-permute-start.46) | collective-permute-done | bytes 147488 | tf_op jit(solution)/shard_map/ppermute | solution.py:29
  184.4 4.8 %collective-permute-done.47.refs_2_ = bf16[96,768]{1,0:T(8,128)(2,1)} collective-permute-done((bf16[96,768]{1,0:T(8,128)(2,1)S(1)}, bf16[96,768]{1,0:T(8,128)(2,1)}, u32[]{:S(2)}, u32[]{:S(2)}) %collective-permute-start.47) | collective-permute-done | bytes 147488 | tf_op jit(solution)/shard_map/ppermute | solution.py:29
  196.4 5.1 %shard_map.357 = (f32[768,1536]{1,0:T(8,128)}, f32[8,128]{1,0:T(8,128)}) custom-call(s32[1]{0:T(128)} %bitcast.refs_0_, bf16[384,768]{1,0:T(8,128)(2,1)} %copy-done.14, bf16[128,768]{1,0:T(8,128)(2,1)} %copy-done.17, bf16[384,768]{1,0:T(8,128)(2,1)} %copy-done.1, bf16[128,768]{1,0:T(8,128)(2,1)} %copy-done.3, bf16[384,768]{1,0:T(8,128)(2,1)} %copy-done, ...), custom_call_target="tpu_custom_call" | custom-call | flops 999999995904 | bytes 999999995904 | tf_op jit(solution)/shard_map/pallas_call | solution.py:903
  203.8 2.1 shard_map.358
  207.9 6.7 %shard_map.359 = (f32[1536,768]{1,0:T(8,128)}, f32[8,128]{1,0:T(8,128)S(1)}) custom-call(s32[1]{0:T(128)} %bitcast.2.refs_0_, bf16[128,1536]{1,0:T(8,128)(2,1)} %get-tuple-element.141.refs_1_, bf16[128,1536]{1,0:T(8,128)(2,1)} %collective-permute-done.21.refs_5_.refs_2_, bf16[128,1536]{1,0:T(8,128)(2,1)} %collective-permute-done.22.refs_6_.refs_3_, ...), custom_call_target="tpu_custom_call" | custom-call | flops 999999995904 | bytes 999999995904 | tf_op jit(solution)/shard_map/pallas_call | solution.py:903
  215.2 4.7 %shard_map.360 = (f32[3,768,384]{2,1,0:T(8,128)}, f32[384,768]{1,0:T(8,128)}) custom-call(s32[1]{0:T(128)} %bitcast.refs_0_, bf16[288,768]{1,0:T(8,128)(2,1)} %get-tuple-element.185.refs_1_, bf16[96,768]{1,0:T(8,128)(2,1)} %collective-permute-done.47.refs_2_, bf16[288,768]{1,0:T(8,128)(2,1)} %collective-permute-done.48.refs_2_.refs_3_, ...), custom_call_target="tpu_custom_call" | custom-call | flops 999999995904 | bytes 999999995904 | tf_op jit(solution)/shard_map/pallas_call | solution.py:903
  (190 shorter events, 71.0 us)
Async XLA Ops:
  31.0 23.3 %collective-permute-start.3 = (bf16[16,768]{1,0:T(8,128)(2,1)}, bf16[16,768]{1,0:T(8,128)(2,1)}, u32[]{:S(2)}, u32[]{:S(2)}) collective-permute-start(bf16[16,768]{1,0:T(8,128)(2,1)} %shard_map.334.refs_7_.refs_0_), channel_id=1, source_target_pairs={{0,24},{2,26},{4,28},{6,30},{8,16},{10,18},{12,20},{14,22},{16,8},... | collective-permute-start | bytes 73736 | tf_op jit(solution)/shard_map/ppermute | solution.py:29
  79.2 10.7 %collective-permute-start.14 = (f32[1,512]{1,0:T(1,128)}, f32[1,512]{1,0:T(1,128)}, u32[]{:S(2)}, u32[]{:S(2)}) collective-permute-start(f32[1,512]{1,0:T(1,128)} %shard_map.340.refs_4_.refs_2_), channel_id=1, source_target_pairs={{0,24},{2,26},{4,28},{6,30},{8,16},{10,18},{12,20},{14,22},{16,8},... | collective-permute-start | bytes 6152 | tf_op jit(solution)/shard_map/ppermute | solution.py:29
  85.6 23.9 %collective-permute-start.22 = (bf16[128,1536]{1,0:T(8,128)(2,1)}, bf16[128,1536]{1,0:T(8,128)(2,1)}, u32[]{:S(2)}, u32[]{:S(2)}) collective-permute-start(bf16[128,1536]{1,0:T(8,128)(2,1)} %get-tuple-element.141.refs_1_), channel_id=1, source_target_pairs={{0,16},{2,18},{4,20},{6,22},{8,24},{10,26},{12,28},{14,30},{16,0},... | collective-permute-start | bytes 1179656 | tf_op jit(solution)/shard_map/ppermute | solution.py:29
  87.9 21.7 %collective-permute-start.21 = (bf16[128,1536]{1,0:T(8,128)(2,1)}, bf16[128,1536]{1,0:T(8,128)(2,1)}, u32[]{:S(2)}, u32[]{:S(2)}) collective-permute-start(bf16[128,1536]{1,0:T(8,128)(2,1)} %get-tuple-element.141.refs_1_), channel_id=1, source_target_pairs={{0,8},{2,10},{4,12},{6,14},{8,0},{10,2},{12,4},{14,6},{16,24},{18,... | collective-permute-start | bytes 1179656 | tf_op jit(solution)/shard_map/ppermute | solution.py:29
  98.1 16.0 %collective-permute-start.18 = (bf16[384,768]{1,0:T(8,128)(2,1)}, bf16[384,768]{1,0:T(8,128)(2,1)}, u32[]{:S(2)}, u32[]{:S(2)}) collective-permute-start(bf16[384,768]{1,0:T(8,128)(2,1)} %get-tuple-element.128), channel_id=1, source_target_pairs={{0,2},{2,0},{4,6},{6,4},{8,10},{10,8},{12,14},{14,12},{16,18},{18,... | collective-permute-start | bytes 1769480 | tf_op jit(solution)/shard_map/ppermute | solution.py:29
  98.6 16.0 %collective-permute-start.19 = (bf16[384,768]{1,0:T(8,128)(2,1)}, bf16[384,768]{1,0:T(8,128)(2,1)}, u32[]{:S(2)}, u32[]{:S(2)}) collective-permute-start(bf16[384,768]{1,0:T(8,128)(2,1)} %get-tuple-element.130), channel_id=1, source_target_pairs={{0,4},{2,6},{4,0},{6,2},{8,12},{10,14},{12,8},{14,10},{16,20},{18,... | collective-permute-start | bytes 1769480 | tf_op jit(solution)/shard_map/ppermute | solution.py:29
  109.4 20.9 %collective-permute-start.28 = (f32[512,768]{1,0:T(8,128)}, f32[512,768]{1,0:T(8,128)}, u32[]{:S(2)}, u32[]{:S(2)}) collective-permute-start(f32[512,768]{1,0:T(8,128)} %get-tuple-element.152.refs_1_), channel_id=1, source_target_pairs={{0,1},{1,0},{2,3},{3,2},{4,5},{5,4},{6,7},{7,6},{8,9},{9,8},{10,11... | collective-permute-start | bytes 4718600 | tf_op jit(solution)/shard_map/ppermute | solution.py:24
  116.2 10.0 %collective-permute-start.23 = (bf16[192,768]{1,0:T(8,128)(2,1)S(1)}, bf16[192,768]{1,0:T(8,128)(2,1)S(1)}, u32[]{:S(2)}, u32[]{:S(2)}) collective-permute-start(bf16[192,768]{1,0:T(8,128)(2,1)S(1)} %get-tuple-element.144), channel_id=1, source_target_pairs={{0,4},{2,6},{4,0},{6,2},{8,12},{10,14},{12,8},{14,10},{16,20},{18,... | collective-permute-start | bytes 884744 | tf_op jit(solution)/shard_map/ppermute | solution.py:29
  118.0 9.9 %collective-permute-start.24 = (bf16[192,768]{1,0:T(8,128)(2,1)S(1)}, bf16[192,768]{1,0:T(8,128)(2,1)S(1)}, u32[]{:S(2)}, u32[]{:S(2)}) collective-permute-start(bf16[192,768]{1,0:T(8,128)(2,1)S(1)} %get-tuple-element.146), channel_id=1, source_target_pairs={{0,2},{2,0},{4,6},{6,4},{8,10},{10,8},{12,14},{14,12},{16,18},{18,... | collective-permute-start | bytes 884744 | tf_op jit(solution)/shard_map/ppermute | solution.py:29
  118.3 20.4 %collective-permute-start.29 = (bf16[384,768]{1,0:T(8,128)(2,1)}, bf16[384,768]{1,0:T(8,128)(2,1)}, u32[]{:S(2)}, u32[]{:S(2)}) collective-permute-start(bf16[384,768]{1,0:T(8,128)(2,1)} %get-tuple-element.160), channel_id=1, source_target_pairs={{0,2},{2,0},{4,6},{6,4},{8,10},{10,8},{12,14},{14,12},{16,18},{18,... | collective-permute-start | bytes 1769480 | tf_op jit(solution)/shard_map/ppermute | solution.py:29
  120.0 18.7 %collective-permute-start.30 = (bf16[384,768]{1,0:T(8,128)(2,1)}, bf16[384,768]{1,0:T(8,128)(2,1)}, u32[]{:S(2)}, u32[]{:S(2)}) collective-permute-start(bf16[384,768]{1,0:T(8,128)(2,1)} %get-tuple-element.162), channel_id=1, source_target_pairs={{0,4},{2,6},{4,0},{6,2},{8,12},{10,14},{12,8},{14,10},{16,20},{18,... | collective-permute-start | bytes 1769480 | tf_op jit(solution)/shard_map/ppermute | solution.py:29
  128.8 13.1 %collective-permute-start.25 = (bf16[96,768]{1,0:T(8,128)(2,1)}, bf16[96,768]{1,0:T(8,128)(2,1)}, u32[]{:S(2)}, u32[]{:S(2)}) collective-permute-start(bf16[96,768]{1,0:T(8,128)(2,1)} %get-tuple-element.149), channel_id=1, source_target_pairs={{0,8},{2,10},{4,12},{6,14},{8,0},{10,2},{12,4},{14,6},{16,24},{18,... | collective-permute-start | bytes 442376 | tf_op jit(solution)/shard_map/ppermute | solution.py:29
  128.9 13.0 %collective-permute-start.26 = (bf16[96,768]{1,0:T(8,128)(2,1)}, bf16[96,768]{1,0:T(8,128)(2,1)}, u32[]{:S(2)}, u32[]{:S(2)}) collective-permute-start(bf16[96,768]{1,0:T(8,128)(2,1)} %get-tuple-element.150), channel_id=1, source_target_pairs={{0,16},{2,18},{4,20},{6,22},{8,24},{10,26},{12,28},{14,30},{16,0},... | collective-permute-start | bytes 442376 | tf_op jit(solution)/shard_map/ppermute | solution.py:29
  130.4 11.5 %collective-permute-start.27 = (bf16[96,768]{1,0:T(8,128)(2,1)}, bf16[96,768]{1,0:T(8,128)(2,1)}, u32[]{:S(2)}, u32[]{:S(2)}) collective-permute-start(bf16[96,768]{1,0:T(8,128)(2,1)} %get-tuple-element.151), channel_id=1, source_target_pairs={{0,24},{2,26},{4,28},{6,30},{8,16},{10,18},{12,20},{14,22},{16,8},... | collective-permute-start | bytes 442376 | tf_op jit(solution)/shard_map/ppermute | solution.py:29
  152.4 21.8 %collective-permute-start.38 = (bf16[384,768]{1,0:T(8,128)(2,1)S(1)}, bf16[384,768]{1,0:T(8,128)(2,1)S(1)}, u32[]{:S(2)}, u32[]{:S(2)}) collective-permute-start(bf16[384,768]{1,0:T(8,128)(2,1)S(1)} %get-tuple-element.171.refs_0_.refs_1_), channel_id=1, source_target_pairs={{0,4},{2,6},{4,0},{6,2},{8,12},{10,14},{12,8},{14,10},{16,20},{18,... | collective-permute-start | bytes 1769480 | tf_op jit(solution)/shard_map/ppermute | solution.py:29
  153.6 20.6 %collective-permute-start.36 = (bf16[384,768]{1,0:T(8,128)(2,1)S(1)}, bf16[384,768]{1,0:T(8,128)(2,1)S(1)}, u32[]{:S(2)}, u32[]{:S(2)}) collective-permute-start(bf16[384,768]{1,0:T(8,128)(2,1)S(1)} %get-tuple-element.171.refs_0_.refs_1_), channel_id=1, source_target_pairs={{0,2},{2,0},{4,6},{6,4},{8,10},{10,8},{12,14},{14,12},{16,18},{18,... | collective-permute-start | bytes 1769480 | tf_op jit(solution)/shard_map/ppermute | solution.py:29
  154.7 11.1 %collective-permute-start.40 = (bf16[96,768]{1,0:T(8,128)(2,1)S(1)}, bf16[96,768]{1,0:T(8,128)(2,1)S(1)}, u32[]{:S(2)}, u32[]{:S(2)}) collective-permute-start(bf16[96,768]{1,0:T(8,128)(2,1)S(1)} %get-tuple-element.173), channel_id=1, source_target_pairs={{0,8},{2,10},{4,12},{6,14},{8,0},{10,2},{12,4},{14,6},{16,24},{18,... | collective-permute-start | bytes 442376 | tf_op jit(solution)/shard_map/ppermute | solution.py:29
  156.8 10.3 %collective-permute-start.41 = (bf16[96,768]{1,0:T(8,128)(2,1)S(1)}, bf16[96,768]{1,0:T(8,128)(2,1)S(1)}, u32[]{:S(2)}, u32[]{:S(2)}) collective-permute-start(bf16[96,768]{1,0:T(8,128)(2,1)S(1)} %get-tuple-element.174), channel_id=1, source_target_pairs={{0,16},{2,18},{4,20},{6,22},{8,24},{10,26},{12,28},{14,30},{16,0},... | collective-permute-start | bytes 442376 | tf_op jit(solution)/shard_map/ppermute | solution.py:29
  164.2 9.9 %collective-permute-start.39 = (bf16[128,768]{1,0:T(8,128)(2,1)S(1)}, bf16[128,768]{1,0:T(8,128)(2,1)S(1)}, u32[]{:S(2)}, u32[]{:S(2)}) collective-permute-start(bf16[128,768]{1,0:T(8,128)(2,1)S(1)} %collective-permute-done.35.refs_1_.refs_2_), channel_id=1, source_target_pairs={{0,4},{2,6},{4,0},{6,2},{8,12},{10,14},{12,8},{14,10},{16,20},{18,... | collective-permute-start | bytes 589832 | tf_op jit(solution)/shard_map/ppermute | solution.py:29
  174.3 20.2 %collective-permute-start.43 = (bf16[320,768]{1,0:T(8,128)(2,1)S(1)}, bf16[320,768]{1,0:T(8,128)(2,1)S(1)}, u32[]{:S(2)}, u32[]{:S(2)}) collective-permute-start(bf16[320,768]{1,0:T(8,128)(2,1)S(1)} %get-tuple-element.178), channel_id=1, source_target_pairs={{0,2},{2,0},{4,6},{6,4},{8,10},{10,8},{12,14},{14,12},{16,18},{18,... | collective-permute-start | bytes 1474568 | tf_op jit(solution)/shard_map/ppermute | solution.py:29
  175.7 17.5 %collective-permute-start.44 = (bf16[192,768]{1,0:T(8,128)(2,1)S(1)}, bf16[192,768]{1,0:T(8,128)(2,1)S(1)}, u32[]{:S(2)}, u32[]{:S(2)}) collective-permute-start(bf16[192,768]{1,0:T(8,128)(2,1)S(1)} %get-tuple-element.179), channel_id=1, source_target_pairs={{0,4},{2,6},{4,0},{6,2},{8,12},{10,14},{12,8},{14,10},{16,20},{18,... | collective-permute-start | bytes 884744 | tf_op jit(solution)/shard_map/ppermute | solution.py:29
  184.3 23.6 %collective-permute-start.54 = (bf16[128,1536]{1,0:T(8,128)(2,1)}, bf16[128,1536]{1,0:T(8,128)(2,1)}, u32[]{:S(2)}, u32[]{:S(2)}) collective-permute-start(bf16[128,1536]{1,0:T(8,128)(2,1)} %collective-permute-done.22.refs_6_.refs_3_), channel_id=1, source_target_pairs={{0,8},{2,10},{4,12},{6,14},{8,0},{10,2},{12,4},{14,6},{16,24},{18,... | collective-permute-start | bytes 1179656 | tf_op jit(solution)/shard_map/ppermute | solution.py:29
  191.7 9.8 %collective-permute-start.49 = (bf16[96,768]{1,0:T(8,128)(2,1)}, bf16[96,768]{1,0:T(8,128)(2,1)}, u32[]{:S(2)}, u32[]{:S(2)}) collective-permute-start(bf16[96,768]{1,0:T(8,128)(2,1)} %collective-permute-done.47.refs_2_), channel_id=1, source_target_pairs={{0,2},{2,0},{4,6},{6,4},{8,10},{10,8},{12,14},{14,12},{16,18},{18,... | collective-permute-start | bytes 442376 | tf_op jit(solution)/shard_map/ppermute | solution.py:29
  196.3 11.6 %collective-permute-start.55 = (bf16[256,768]{1,0:T(8,128)(2,1)}, bf16[256,768]{1,0:T(8,128)(2,1)}, u32[]{:S(2)}, u32[]{:S(2)}) collective-permute-start(bf16[256,768]{1,0:T(8,128)(2,1)} %get-tuple-element.189.refs_5_), channel_id=1, source_target_pairs={{0,1},{1,0},{2,3},{3,2},{4,5},{5,4},{6,7},{7,6},{8,9},{9,8},{10,11... | collective-permute-start | bytes 1179656 | tf_op jit(solution)/shard_map/ppermute | solution.py:24
  (69 other events, 562.8 us)

commit v6 on v5

--- a/solution.py
+++ b/solution.py
@@ -765,7 +765,7 @@
 
 
 def narrow_grad_kernel(half, index_ref, *refs):
-    parts, (near_ref, far_ref, out_ref, grads) = refs[:-4], refs[-4:]
+    parts, (near_ref, far_ref, out_ref, grads, sums) = refs[:-5], refs[-5:]
     rows, width = parts[0].shape[0], grads.shape[1]
     devices = near_ref.shape[0] // half
     for place in range(devices):
@@ -774,14 +774,11 @@
         for ref, which in ((near_ref, index_ref[0]), (far_ref, 1 - index_ref[0])):
             start = pl.multiple_of((2 * place + which) * half, half)
             grads[pl.ds(start, half), :] = ref[source * half : (source + 1) * half, :]
+    for place, part in enumerate(parts):
+        sums[place * rows : (place + 1) * rows, :] = part[...]
     for chunk in range(out_ref.shape[0] // width):
         lanes = slice(chunk * width, (chunk + 1) * width)
-        total = t_dot(parts[0][:, lanes], grads[:rows, :])
-        for place in range(1, len(parts)):
-            total = total + t_dot(
-                parts[place][:, lanes], grads[place * rows : (place + 1) * rows, :]
-            )
-        out_ref[lanes, :] = total
+        out_ref[lanes, :] = t_dot(sums[:, lanes], grads[...])
 
 
 def entry_grad_kernel(
@@ -1375,7 +1372,10 @@
         functools.partial(narrow_grad_kernel, captions // 2),
         (*sums_parts, near_grads, mp_other(near_grads)),
         ((narrowing_matrix.shape, F32),),
-        scratch=(pltpu.VMEM((all_pairs, model_width), BF16),),
+        scratch=(
+            pltpu.VMEM((all_pairs, model_width), BF16),
+            pltpu.VMEM((all_pairs, hidden), BF16),
+        ),
         index=(core,),
         after=(last,),
         mark=True,

time: 222 us -> 223 us (level); the launches traced: 220 us -> 225 us
  waiting for transfers between devices: 43.7 us -> 48.9 us
  starting transfers between devices: 72.5 us -> 69.5 us
  Pallas kernels: 99.6 us -> 102 us
    ppermute x50, starting transfers between devices: 71.6 us -> 65.8 us  [dp_swap(): lax.ppermute(values, 'dp', [(index, index ^ mask) for index in range(size)])]
    ppermute x50, waiting for transfers between devices: 42.8 us -> 48 us  [dp_swap(): lax.ppermute(values, 'dp', [(index, index ^ mask) for index in range(size)])]
    pallas_call x1, Pallas kernels: 30.3 us -> 34.7 us  [image_tower(): pl.pallas_call(image_kernel, out_shape=jax.ShapeDtypeStruct((images, widt...]
    ppermute x6, starting transfers between devices: 0.85 us -> 3.67 us  [mp_other(): return lax.ppermute(values, 'mp', [(0, 1), (1, 0)])]
  transfers between devices with their start and end apart: 56 -> 56, of which waited for: 17 -> 20; matrix products, arithmetic and copies ran while one was open for 0% -> 0% of each run, Pallas kernels for 28% -> 27%
where the time goes in v6:
time: 223 us; the launch traced here: 225 us
  Pallas kernels  102 us (46%)
  starting transfers between devices  69.5 us (31%)
  waiting for transfers between devices  48.9 us (22%)
    pallas_call x26, Pallas kernels, call(): pl.pallas_call(body, out_shape=[jax.ShapeDtypeStruct(shape, kind) for sha...  67.7 us
    ppermute x50, starting transfers between devices, dp_swap(): lax.ppermute(values, 'dp', [(index, index ^ mask) for index in range(size)])  65.8 us
    ppermute x50, waiting for transfers between devices, dp_swap(): lax.ppermute(values, 'dp', [(index, index ^ mask) for index in range(size)])  48 us
    pallas_call x1, Pallas kernels, image_tower(): pl.pallas_call(image_kernel, out_shape=jax.ShapeDtypeStruct((images, widt...  34.7 us
  transfers between devices with their start and end apart: 56, of which 20 were waited for; matrix products, arithmetic and copies ran while one was open for 0% of the time, Pallas kernels for 27%

profile of v6, /device:TPU:0, one launch (start us, length us, event | category | flops | bytes accessed | tf_op | source)
XLA Modules:
  0.0 225.0 jit_solution(10693594537545009310)
XLA Ops:
  0.6 34.7 %shard_map.334.refs_7_.refs_0_ = bf16[16,768]{1,0:T(8,128)(2,1)} custom-call(s32[16]{0:T(128)} %flag_ref.1, bf16[145,16,768]{2,1,0:T(8,128)(2,1)} %bitcast.3, f32[2,768]{1,0:T(2,128)} %gain_ref.1, bf16[3,768,768]{2,1,0:T(8,128)(2,1)} %triple_hbm.1, bf16[768,768]{1,0:T(8,128)(2,1)} %result_hbm.1, bf16[768,3072]{1,0:T(8,128)(2,1)} %widen_hbm.1, ...), custom_call_target="tpu_custom_call" | custom-call | flops 999999995904 | bytes 999999995904 | tf_op jit(solution)/shard_map/pallas_call | solution.py:334
  35.4 7.4 %collective-permute-start.3 = (bf16[16,768]{1,0:T(8,128)(2,1)}, bf16[16,768]{1,0:T(8,128)(2,1)}, u32[]{:S(2)}, u32[]{:S(2)}) collective-permute-start(bf16[16,768]{1,0:T(8,128)(2,1)} %shard_map.334.refs_7_.refs_0_), channel_id=1, source_target_pairs={{0,24},{2,26},{4,28},{6,30},{8,16},{10,18},{12,20},{14,22},{16,8},... | collective-permute-start | bytes 73736 | tf_op jit(solution)/shard_map/ppermute | solution.py:29
  43.4 6.6 %shard_map.335 = (bf16[512,768]{1,0:T(8,128)(2,1)}, bf16[3,512,384]{2,1,0:T(8,128)(2,1)}, f32[4,3,256,128]{3,2,1,0:T(8,128)}, bf16[512,384]{1,0:T(8,128)(2,1)}, f32[512,768]{1,0:T(8,128)}, /*index=5*/f32[8,128]{1,0:T(8,128)}) custom-call(bf16[512,768]{1,0:T(8,128)(2,1)} %refs_3_.5, s32[512]{0:T(512)} %refs_4_.6, f32[768]{0:T(1024)} %refs_4_.7, f32[768]{0:T(1024)} %refs_3_.3, ...), custom_call_target="tpu_custom_call" | custom-call | flops 999999995904 | bytes 999999995904 | tf_op jit(solution)/shard_map/pallas_call | solution.py:900
  49.9 2.7 %collective-permute-start = (f32[512,768]{1,0:T(8,128)}, f32[512,768]{1,0:T(8,128)}, u32[]{:S(2)}, u32[]{:S(2)}) collective-permute-start(f32[512,768]{1,0:T(8,128)} %get-tuple-element.110.refs_1_), channel_id=1, source_target_pairs={{0,1},{1,0},{2,3},{3,2},{4,5},{5,4},{6,7},{7,6},{8,9},{9,8},{10,11... | collective-permute-start | bytes 4718600 | tf_op jit(solution)/shard_map/ppermute | solution.py:24
  54.9 3.4 %collective-permute-start.6 = (bf16[64,768]{1,0:T(8,128)(2,1)}, bf16[64,768]{1,0:T(8,128)(2,1)}, u32[]{:S(2)}, u32[]{:S(2)}) collective-permute-start(bf16[64,768]{1,0:T(8,128)(2,1)} %shard_map.336.refs_10_.refs_0_), channel_id=1, source_target_pairs={{0,6},{2,4},{4,2},{6,0},{8,14},{10,12},{12,10},{14,8},{16,22},{18,... | collective-permute-start | bytes 294920 | tf_op jit(solution)/shard_map/ppermute | solution.py:29
  58.3 6.8 %collective-permute-start.5 = (bf16[64,768]{1,0:T(8,128)(2,1)}, bf16[64,768]{1,0:T(8,128)(2,1)}, u32[]{:S(2)}, u32[]{:S(2)}) collective-permute-start(bf16[64,768]{1,0:T(8,128)(2,1)} %shard_map.336.refs_10_.refs_0_), channel_id=1, source_target_pairs={{0,4},{2,6},{4,0},{6,2},{8,12},{10,14},{12,8},{14,10},{16,20},{18,... | collective-permute-start | bytes 294920 | tf_op jit(solution)/shard_map/ppermute | solution.py:29
  65.2 6.2 %shard_map.337 = (f32[512,768]{1,0:T(8,128)S(1)}, bf16[512,768]{1,0:T(8,128)(2,1)S(1)}, f32[512,1536]{1,0:T(8,128)S(1)}, bf16[32,1536]{1,0:T(8,128)(2,1)}, f32[32,768]{1,0:T(8,128)S(1)}, /*index=5*/f32[32,768]{1,0:T(8,128)S(1)}) custom-call(bf16[512,768]{1,0:T(8,128)(2,1)S(1)} %copy-done.11, f32[512,768]{1,0:T(8,128)S(1)} %copy-done.10, ...), custom_call_target="tpu_custom_call" | custom-call | flops 999999995904 | bytes 999999995904 | tf_op jit(solution)/shard_map/pallas_call | solution.py:900
  84.3 3.7 %collective-permute-start.14 = (f32[1,512]{1,0:T(1,128)}, f32[1,512]{1,0:T(1,128)}, u32[]{:S(2)}, u32[]{:S(2)}) collective-permute-start(f32[1,512]{1,0:T(1,128)} %shard_map.340.refs_4_.refs_2_), channel_id=1, source_target_pairs={{0,24},{2,26},{4,28},{6,30},{8,16},{10,18},{12,20},{14,22},{16,8},... | collective-permute-start | bytes 6152 | tf_op jit(solution)/shard_map/ppermute | solution.py:29
  95.0 5.5 %shard_map.342 = (f32[32,768]{1,0:T(8,128)S(1)}, bf16[32,768]{1,0:T(8,128)(2,1)S(1)}, bf16[512,1536]{1,0:T(8,128)(2,1)S(1)}, f32[512,768]{1,0:T(8,128)}, f32[8,768]{1,0:T(8,128)S(1)}) custom-call(s32[32]{0:T(128)S(1)} %copy-done.28, f32[1]{0:T(128)S(6)} %copy.38.refs_2_.refs_1_, f32[1,512]{1,0:T(1,128)} %shard_map.340.refs_4_.refs_2_, ...), custom_call_target="tpu_custom_call" | custom-call | flops 999999995904 | bytes 999999995904 | tf_op jit(solution)/shard_map/pallas_call | solution.py:900
  100.7 2.5 %shard_map.343 = (bf16[384,768]{1,0:T(8,128)(2,1)}, bf16[384,768]{1,0:T(8,128)(2,1)S(1)}, bf16[384,768]{1,0:T(8,128)(2,1)}, bf16[384,768]{1,0:T(8,128)(2,1)S(1)}, f32[8,128]{1,0:T(8,128)S(1)}) custom-call(s32[1]{0:T(128)} %bitcast.refs_0_, bf16[512,768]{1,0:T(8,128)(2,1)S(1)} %get-tuple-element.112.refs_1_, bf16[512,1536]{1,0:T(8,128)(2,1)S(1)} %get-tuple-element.126.refs_2_), custom_call_target="tpu_custom_call" | custom-call | flops 999999995904 | bytes 999999995904 | tf_op jit(solution)/shard_map/pallas_call | solution.py:900
  105.3 8.7 %shard_map.344 = (f32[512,768]{1,0:T(8,128)S(1)}, bf16[512,768]{1,0:T(8,128)(2,1)S(1)}, bf16[3,512,384]{2,1,0:T(8,128)(2,1)S(1)}, f32[512,768]{1,0:T(8,128)}, f32[8,768]{1,0:T(8,128)S(1)}) custom-call(f32[512,768]{1,0:T(8,128)} %get-tuple-element.132.refs_0_, f32[512,768]{1,0:T(8,128)} %collective-permute-done.20.refs_1_, ...), custom_call_target="tpu_custom_call" | custom-call | flops 999999995904 | bytes 999999995904 | tf_op jit(solution)/shard_map/pallas_call | solution.py:900
  114.3 3.0 %shard_map.345 = (bf16[384,768]{1,0:T(8,128)(2,1)}, bf16[384,768]{1,0:T(8,128)(2,1)S(1)}, bf16[384,768]{1,0:T(8,128)(2,1)}, bf16[384,768]{1,0:T(8,128)(2,1)S(1)}, f32[8,128]{1,0:T(8,128)S(1)}) custom-call(s32[1]{0:T(128)} %bitcast.refs_0_, bf16[512,768]{1,0:T(8,128)(2,1)S(1)} %copy-done.33, bf16[3,512,384]{2,1,0:T(8,128)(2,1)S(1)} %get-tuple-element.138.refs_2_, ...), custom_call_target="tpu_custom_call" | custom-call | flops 999999995904 | bytes 999999995904 | tf_op jit(solution)/shard_map/pallas_call | solution.py:900
  126.6 5.9 %collective-permute-done.23.refs_2_ = bf16[192,768]{1,0:T(8,128)(2,1)S(1)} collective-permute-done((bf16[192,768]{1,0:T(8,128)(2,1)S(1)}, bf16[192,768]{1,0:T(8,128)(2,1)S(1)}, u32[]{:S(2)}, u32[]{:S(2)}) %collective-permute-start.23) | collective-permute-done | bytes 294944 | tf_op jit(solution)/shard_map/ppermute | solution.py:29
  135.2 2.8 %collective-permute-start.27 = (bf16[96,768]{1,0:T(8,128)(2,1)}, bf16[96,768]{1,0:T(8,128)(2,1)}, u32[]{:S(2)}, u32[]{:S(2)}) collective-permute-start(bf16[96,768]{1,0:T(8,128)(2,1)} %get-tuple-element.151), channel_id=1, source_target_pairs={{0,24},{2,26},{4,28},{6,30},{8,16},{10,18},{12,20},{14,22},{16,8},... | collective-permute-start | bytes 442376 | tf_op jit(solution)/shard_map/ppermute | solution.py:29
  138.0 4.2 %shard_map.348 = (f32[512,768]{1,0:T(8,128)}, bf16[32,768]{1,0:T(8,128)(2,1)S(1)}) custom-call(s32[1]{0:T(128)} %bitcast.2.refs_0_, f32[512,768]{1,0:T(8,128)} %get-tuple-element.152.refs_1_, f32[512,768]{1,0:T(8,128)} %collective-permute-done.28.refs_2_, bf16[512,768]{1,0:T(8,128)(2,1)S(1)} %copy-done.12, f32[768]{0:T(1024)S(1)} %copy-done.25, ...), custom_call_target="tpu_custom_call" | custom-call | flops 999999995904 | bytes 999999995904 | tf_op jit(solution)/shard_map/pallas_call | solution.py:900
  150.3 2.6 %collective-permute-done.33.refs_2_ = bf16[192,768]{1,0:T(8,128)(2,1)S(1)} collective-permute-done((bf16[192,768]{1,0:T(8,128)(2,1)S(1)}, bf16[192,768]{1,0:T(8,128)(2,1)S(1)}, u32[]{:S(2)}, u32[]{:S(2)}) %collective-permute-start.33) | collective-permute-done | bytes 294944 | tf_op jit(solution)/shard_map/ppermute | solution.py:29
  153.8 4.3 %collective-permute-done.32.refs_2_ = bf16[128,768]{1,0:T(8,128)(2,1)S(1)} collective-permute-done((bf16[128,768]{1,0:T(8,128)(2,1)S(1)}, bf16[128,768]{1,0:T(8,128)(2,1)S(1)}, u32[]{:S(2)}, u32[]{:S(2)}) %collective-permute-start.32) | collective-permute-done | bytes 196640 | tf_op jit(solution)/shard_map/ppermute | solution.py:29
  162.9 7.2 %collective-permute-done.35.refs_1_.refs_2_ = bf16[128,768]{1,0:T(8,128)(2,1)S(1)} collective-permute-done((bf16[128,768]{1,0:T(8,128)(2,1)S(1)}, bf16[128,768]{1,0:T(8,128)(2,1)S(1)}, u32[]{:S(2)}, u32[]{:S(2)}) %collective-permute-start.35) | collective-permute-done | bytes 196640 | tf_op jit(solution)/shard_map/ppermute | solution.py:29
  174.2 6.8 %collective-permute-done.42.refs_3_ = bf16[96,768]{1,0:T(8,128)(2,1)S(1)} collective-permute-done((bf16[96,768]{1,0:T(8,128)(2,1)S(1)}, bf16[96,768]{1,0:T(8,128)(2,1)S(1)}, u32[]{:S(2)}, u32[]{:S(2)}) %collective-permute-start.42) | collective-permute-done | bytes 147488 | tf_op jit(solution)/shard_map/ppermute | solution.py:29
  182.3 5.4 %collective-permute-done.46.refs_2_ = bf16[96,768]{1,0:T(8,128)(2,1)S(1)} collective-permute-done((bf16[96,768]{1,0:T(8,128)(2,1)S(1)}, bf16[96,768]{1,0:T(8,128)(2,1)S(1)}, u32[]{:S(2)}, u32[]{:S(2)}) %collective-permute-start.46) | collective-permute-done | bytes 147488 | tf_op jit(solution)/shard_map/ppermute | solution.py:29
  189.8 4.8 %collective-permute-done.47.refs_2_ = bf16[96,768]{1,0:T(8,128)(2,1)} collective-permute-done((bf16[96,768]{1,0:T(8,128)(2,1)S(1)}, bf16[96,768]{1,0:T(8,128)(2,1)}, u32[]{:S(2)}, u32[]{:S(2)}) %collective-permute-start.47) | collective-permute-done | bytes 147488 | tf_op jit(solution)/shard_map/ppermute | solution.py:29
  202.1 5.1 %shard_map.357 = (f32[768,1536]{1,0:T(8,128)}, f32[8,128]{1,0:T(8,128)}) custom-call(s32[1]{0:T(128)} %bitcast.refs_0_, bf16[384,768]{1,0:T(8,128)(2,1)} %copy-done.14, bf16[128,768]{1,0:T(8,128)(2,1)} %copy-done.17, bf16[384,768]{1,0:T(8,128)(2,1)} %copy-done.1, bf16[128,768]{1,0:T(8,128)(2,1)} %copy-done.3, bf16[384,768]{1,0:T(8,128)(2,1)} %copy-done, ...), custom_call_target="tpu_custom_call" | custom-call | flops 999999995904 | bytes 999999995904 | tf_op jit(solution)/shard_map/pallas_call | solution.py:900
  213.8 5.2 %shard_map.359 = (f32[1536,768]{1,0:T(8,128)}, f32[8,128]{1,0:T(8,128)S(1)}) custom-call(s32[1]{0:T(128)} %bitcast.2.refs_0_, bf16[128,1536]{1,0:T(8,128)(2,1)} %get-tuple-element.141.refs_1_, bf16[128,1536]{1,0:T(8,128)(2,1)} %collective-permute-done.21.refs_5_.refs_2_, bf16[128,1536]{1,0:T(8,128)(2,1)} %collective-permute-done.22.refs_6_.refs_3_, ...), custom_call_target="tpu_custom_call" | custom-call | flops 999999995904 | bytes 999999995904 | tf_op jit(solution)/shard_map/pallas_call | solution.py:900
  220.3 4.7 %shard_map.360 = (f32[3,768,384]{2,1,0:T(8,128)}, f32[384,768]{1,0:T(8,128)}) custom-call(s32[1]{0:T(128)} %bitcast.refs_0_, bf16[288,768]{1,0:T(8,128)(2,1)} %get-tuple-element.185.refs_1_, bf16[96,768]{1,0:T(8,128)(2,1)} %collective-permute-done.47.refs_2_, bf16[288,768]{1,0:T(8,128)(2,1)} %collective-permute-done.48.refs_2_.refs_3_, ...), custom_call_target="tpu_custom_call" | custom-call | flops 999999995904 | bytes 999999995904 | tf_op jit(solution)/shard_map/pallas_call | solution.py:900
  (190 shorter events, 72.8 us)
Async XLA Ops:
  35.4 17.2 %collective-permute-start.3 = (bf16[16,768]{1,0:T(8,128)(2,1)}, bf16[16,768]{1,0:T(8,128)(2,1)}, u32[]{:S(2)}, u32[]{:S(2)}) collective-permute-start(bf16[16,768]{1,0:T(8,128)(2,1)} %shard_map.334.refs_7_.refs_0_), channel_id=1, source_target_pairs={{0,24},{2,26},{4,28},{6,30},{8,16},{10,18},{12,20},{14,22},{16,8},... | collective-permute-start | bytes 73736 | tf_op jit(solution)/shard_map/ppermute | solution.py:29
  49.9 15.2 %collective-permute-start = (f32[512,768]{1,0:T(8,128)}, f32[512,768]{1,0:T(8,128)}, u32[]{:S(2)}, u32[]{:S(2)}) collective-permute-start(f32[512,768]{1,0:T(8,128)} %get-tuple-element.110.refs_1_), channel_id=1, source_target_pairs={{0,1},{1,0},{2,3},{3,2},{4,5},{5,4},{6,7},{7,6},{8,9},{9,8},{10,11... | collective-permute-start | bytes 4718600 | tf_op jit(solution)/shard_map/ppermute | solution.py:24
  54.9 16.5 %collective-permute-start.6 = (bf16[64,768]{1,0:T(8,128)(2,1)}, bf16[64,768]{1,0:T(8,128)(2,1)}, u32[]{:S(2)}, u32[]{:S(2)}) collective-permute-start(bf16[64,768]{1,0:T(8,128)(2,1)} %shard_map.336.refs_10_.refs_0_), channel_id=1, source_target_pairs={{0,6},{2,4},{4,2},{6,0},{8,14},{10,12},{12,10},{14,8},{16,22},{18,... | collective-permute-start | bytes 294920 | tf_op jit(solution)/shard_map/ppermute | solution.py:29
  58.3 13.1 %collective-permute-start.5 = (bf16[64,768]{1,0:T(8,128)(2,1)}, bf16[64,768]{1,0:T(8,128)(2,1)}, u32[]{:S(2)}, u32[]{:S(2)}) collective-permute-start(bf16[64,768]{1,0:T(8,128)(2,1)} %shard_map.336.refs_10_.refs_0_), channel_id=1, source_target_pairs={{0,4},{2,6},{4,0},{6,2},{8,12},{10,14},{12,8},{14,10},{16,20},{18,... | collective-permute-start | bytes 294920 | tf_op jit(solution)/shard_map/ppermute | solution.py:29
  84.3 10.7 %collective-permute-start.14 = (f32[1,512]{1,0:T(1,128)}, f32[1,512]{1,0:T(1,128)}, u32[]{:S(2)}, u32[]{:S(2)}) collective-permute-start(f32[1,512]{1,0:T(1,128)} %shard_map.340.refs_4_.refs_2_), channel_id=1, source_target_pairs={{0,24},{2,26},{4,28},{6,30},{8,16},{10,18},{12,20},{14,22},{16,8},... | collective-permute-start | bytes 6152 | tf_op jit(solution)/shard_map/ppermute | solution.py:29
  90.7 23.6 %collective-permute-start.22 = (bf16[128,1536]{1,0:T(8,128)(2,1)}, bf16[128,1536]{1,0:T(8,128)(2,1)}, u32[]{:S(2)}, u32[]{:S(2)}) collective-permute-start(bf16[128,1536]{1,0:T(8,128)(2,1)} %get-tuple-element.141.refs_1_), channel_id=1, source_target_pairs={{0,16},{2,18},{4,20},{6,22},{8,24},{10,26},{12,28},{14,30},{16,0},... | collective-permute-start | bytes 1179656 | tf_op jit(solution)/shard_map/ppermute | solution.py:29
  93.0 21.2 %collective-permute-start.21 = (bf16[128,1536]{1,0:T(8,128)(2,1)}, bf16[128,1536]{1,0:T(8,128)(2,1)}, u32[]{:S(2)}, u32[]{:S(2)}) collective-permute-start(bf16[128,1536]{1,0:T(8,128)(2,1)} %get-tuple-element.141.refs_1_), channel_id=1, source_target_pairs={{0,8},{2,10},{4,12},{6,14},{8,0},{10,2},{12,4},{14,6},{16,24},{18,... | collective-permute-start | bytes 1179656 | tf_op jit(solution)/shard_map/ppermute | solution.py:29
  103.3 16.2 %collective-permute-start.18 = (bf16[384,768]{1,0:T(8,128)(2,1)}, bf16[384,768]{1,0:T(8,128)(2,1)}, u32[]{:S(2)}, u32[]{:S(2)}) collective-permute-start(bf16[384,768]{1,0:T(8,128)(2,1)} %get-tuple-element.128), channel_id=1, source_target_pairs={{0,2},{2,0},{4,6},{6,4},{8,10},{10,8},{12,14},{14,12},{16,18},{18,... | collective-permute-start | bytes 1769480 | tf_op jit(solution)/shard_map/ppermute | solution.py:29
  105.2 15.7 %collective-permute-start.19 = (bf16[384,768]{1,0:T(8,128)(2,1)}, bf16[384,768]{1,0:T(8,128)(2,1)}, u32[]{:S(2)}, u32[]{:S(2)}) collective-permute-start(bf16[384,768]{1,0:T(8,128)(2,1)} %get-tuple-element.130), channel_id=1, source_target_pairs={{0,4},{2,6},{4,0},{6,2},{8,12},{10,14},{12,8},{14,10},{16,20},{18,... | collective-permute-start | bytes 1769480 | tf_op jit(solution)/shard_map/ppermute | solution.py:29
  114.0 21.2 %collective-permute-start.28 = (f32[512,768]{1,0:T(8,128)}, f32[512,768]{1,0:T(8,128)}, u32[]{:S(2)}, u32[]{:S(2)}) collective-permute-start(f32[512,768]{1,0:T(8,128)} %get-tuple-element.152.refs_1_), channel_id=1, source_target_pairs={{0,1},{1,0},{2,3},{3,2},{4,5},{5,4},{6,7},{7,6},{8,9},{9,8},{10,11... | collective-permute-start | bytes 4718600 | tf_op jit(solution)/shard_map/ppermute | solution.py:24
  123.2 20.7 %collective-permute-start.29 = (bf16[384,768]{1,0:T(8,128)(2,1)}, bf16[384,768]{1,0:T(8,128)(2,1)}, u32[]{:S(2)}, u32[]{:S(2)}) collective-permute-start(bf16[384,768]{1,0:T(8,128)(2,1)} %get-tuple-element.160), channel_id=1, source_target_pairs={{0,2},{2,0},{4,6},{6,4},{8,10},{10,8},{12,14},{14,12},{16,18},{18,... | collective-permute-start | bytes 1769480 | tf_op jit(solution)/shard_map/ppermute | solution.py:29
  124.9 19.0 %collective-permute-start.30 = (bf16[384,768]{1,0:T(8,128)(2,1)}, bf16[384,768]{1,0:T(8,128)(2,1)}, u32[]{:S(2)}, u32[]{:S(2)}) collective-permute-start(bf16[384,768]{1,0:T(8,128)(2,1)} %get-tuple-element.162), channel_id=1, source_target_pairs={{0,4},{2,6},{4,0},{6,2},{8,12},{10,14},{12,8},{14,10},{16,20},{18,... | collective-permute-start | bytes 1769480 | tf_op jit(solution)/shard_map/ppermute | solution.py:29
  133.6 13.9 %collective-permute-start.25 = (bf16[96,768]{1,0:T(8,128)(2,1)}, bf16[96,768]{1,0:T(8,128)(2,1)}, u32[]{:S(2)}, u32[]{:S(2)}) collective-permute-start(bf16[96,768]{1,0:T(8,128)(2,1)} %get-tuple-element.149), channel_id=1, source_target_pairs={{0,8},{2,10},{4,12},{6,14},{8,0},{10,2},{12,4},{14,6},{16,24},{18,... | collective-permute-start | bytes 442376 | tf_op jit(solution)/shard_map/ppermute | solution.py:29
  133.7 13.8 %collective-permute-start.26 = (bf16[96,768]{1,0:T(8,128)(2,1)}, bf16[96,768]{1,0:T(8,128)(2,1)}, u32[]{:S(2)}, u32[]{:S(2)}) collective-permute-start(bf16[96,768]{1,0:T(8,128)(2,1)} %get-tuple-element.150), channel_id=1, source_target_pairs={{0,16},{2,18},{4,20},{6,22},{8,24},{10,26},{12,28},{14,30},{16,0},... | collective-permute-start | bytes 442376 | tf_op jit(solution)/shard_map/ppermute | solution.py:29
  135.2 12.3 %collective-permute-start.27 = (bf16[96,768]{1,0:T(8,128)(2,1)}, bf16[96,768]{1,0:T(8,128)(2,1)}, u32[]{:S(2)}, u32[]{:S(2)}) collective-permute-start(bf16[96,768]{1,0:T(8,128)(2,1)} %get-tuple-element.151), channel_id=1, source_target_pairs={{0,24},{2,26},{4,28},{6,30},{8,16},{10,18},{12,20},{14,22},{16,8},... | collective-permute-start | bytes 442376 | tf_op jit(solution)/shard_map/ppermute | solution.py:29
  158.1 23.0 %collective-permute-start.38 = (bf16[384,768]{1,0:T(8,128)(2,1)S(1)}, bf16[384,768]{1,0:T(8,128)(2,1)S(1)}, u32[]{:S(2)}, u32[]{:S(2)}) collective-permute-start(bf16[384,768]{1,0:T(8,128)(2,1)S(1)} %get-tuple-element.171.refs_0_.refs_1_), channel_id=1, source_target_pairs={{0,4},{2,6},{4,0},{6,2},{8,12},{10,14},{12,8},{14,10},{16,20},{18,... | collective-permute-start | bytes 1769480 | tf_op jit(solution)/shard_map/ppermute | solution.py:29
  159.1 22.1 %collective-permute-start.36 = (bf16[384,768]{1,0:T(8,128)(2,1)S(1)}, bf16[384,768]{1,0:T(8,128)(2,1)S(1)}, u32[]{:S(2)}, u32[]{:S(2)}) collective-permute-start(bf16[384,768]{1,0:T(8,128)(2,1)S(1)} %get-tuple-element.171.refs_0_.refs_1_), channel_id=1, source_target_pairs={{0,2},{2,0},{4,6},{6,4},{8,10},{10,8},{12,14},{14,12},{16,18},{18,... | collective-permute-start | bytes 1769480 | tf_op jit(solution)/shard_map/ppermute | solution.py:29
  160.2 11.4 %collective-permute-start.40 = (bf16[96,768]{1,0:T(8,128)(2,1)S(1)}, bf16[96,768]{1,0:T(8,128)(2,1)S(1)}, u32[]{:S(2)}, u32[]{:S(2)}) collective-permute-start(bf16[96,768]{1,0:T(8,128)(2,1)S(1)} %get-tuple-element.173), channel_id=1, source_target_pairs={{0,8},{2,10},{4,12},{6,14},{8,0},{10,2},{12,4},{14,6},{16,24},{18,... | collective-permute-start | bytes 442376 | tf_op jit(solution)/shard_map/ppermute | solution.py:29
  162.3 10.6 %collective-permute-start.41 = (bf16[96,768]{1,0:T(8,128)(2,1)S(1)}, bf16[96,768]{1,0:T(8,128)(2,1)S(1)}, u32[]{:S(2)}, u32[]{:S(2)}) collective-permute-start(bf16[96,768]{1,0:T(8,128)(2,1)S(1)} %get-tuple-element.174), channel_id=1, source_target_pairs={{0,16},{2,18},{4,20},{6,22},{8,24},{10,26},{12,28},{14,30},{16,0},... | collective-permute-start | bytes 442376 | tf_op jit(solution)/shard_map/ppermute | solution.py:29
  170.1 11.0 %collective-permute-start.39 = (bf16[128,768]{1,0:T(8,128)(2,1)S(1)}, bf16[128,768]{1,0:T(8,128)(2,1)S(1)}, u32[]{:S(2)}, u32[]{:S(2)}) collective-permute-start(bf16[128,768]{1,0:T(8,128)(2,1)S(1)} %collective-permute-done.35.refs_1_.refs_2_), channel_id=1, source_target_pairs={{0,4},{2,6},{4,0},{6,2},{8,12},{10,14},{12,8},{14,10},{16,20},{18,... | collective-permute-start | bytes 589832 | tf_op jit(solution)/shard_map/ppermute | solution.py:29
  181.2 18.6 %collective-permute-start.43 = (bf16[320,768]{1,0:T(8,128)(2,1)S(1)}, bf16[320,768]{1,0:T(8,128)(2,1)S(1)}, u32[]{:S(2)}, u32[]{:S(2)}) collective-permute-start(bf16[320,768]{1,0:T(8,128)(2,1)S(1)} %get-tuple-element.178), channel_id=1, source_target_pairs={{0,2},{2,0},{4,6},{6,4},{8,10},{10,8},{12,14},{14,12},{16,18},{18,... | collective-permute-start | bytes 1474568 | tf_op jit(solution)/shard_map/ppermute | solution.py:29
  181.4 17.7 %collective-permute-start.44 = (bf16[192,768]{1,0:T(8,128)(2,1)S(1)}, bf16[192,768]{1,0:T(8,128)(2,1)S(1)}, u32[]{:S(2)}, u32[]{:S(2)}) collective-permute-start(bf16[192,768]{1,0:T(8,128)(2,1)S(1)} %get-tuple-element.179), channel_id=1, source_target_pairs={{0,4},{2,6},{4,0},{6,2},{8,12},{10,14},{12,8},{14,10},{16,20},{18,... | collective-permute-start | bytes 884744 | tf_op jit(solution)/shard_map/ppermute | solution.py:29
  189.8 24.0 %collective-permute-start.54 = (bf16[128,1536]{1,0:T(8,128)(2,1)}, bf16[128,1536]{1,0:T(8,128)(2,1)}, u32[]{:S(2)}, u32[]{:S(2)}) collective-permute-start(bf16[128,1536]{1,0:T(8,128)(2,1)} %collective-permute-done.22.refs_6_.refs_3_), channel_id=1, source_target_pairs={{0,8},{2,10},{4,12},{6,14},{8,0},{10,2},{12,4},{14,6},{16,24},{18,... | collective-permute-start | bytes 1179656 | tf_op jit(solution)/shard_map/ppermute | solution.py:29
  202.0 11.7 %collective-permute-start.55 = (bf16[256,768]{1,0:T(8,128)(2,1)}, bf16[256,768]{1,0:T(8,128)(2,1)}, u32[]{:S(2)}, u32[]{:S(2)}) collective-permute-start(bf16[256,768]{1,0:T(8,128)(2,1)} %get-tuple-element.189.refs_5_), channel_id=1, source_target_pairs={{0,1},{1,0},{2,3},{3,2},{4,5},{5,4},{6,7},{7,6},{8,9},{9,8},{10,11... | collective-permute-start | bytes 1179656 | tf_op jit(solution)/shard_map/ppermute | solution.py:24
  (69 other events, 628.6 us)
